TPU v7x, 32 devices: a whole 2x2x4 slice. The times are simulated.
32 devices in a mesh: qx: 4 (over y, core), qy: 8 (over z, x).
Axes of the slice: x: 2, y: 2, z: 4, core: 2. Of those that a mesh axis runs over, the one named last changes fastest.
Arguments:
- positions: float32 [16, 32, 2, 256], replicated, may hold values from 0 to 32, as said below
- samples: bfloat16 [16, 32, 256, 256], P('qx', 'qy'), may hold values from -6 to 6
- leaf_basis: bfloat16 [16, 32, 256, 256], P('qx', 'qy'), may hold values from -0.375 to 0.375
- transfer_one: bfloat16 [16, 32, 256, 256], P('qx', 'qy'), may hold values from -0.25 to 0.25
- transfer_two: bfloat16 [8, 16, 256, 256], P('qx', 'qy'), may hold values from -0.25 to 0.25
- couplings: bfloat16 [3, 20, 256, 256], replicated, may hold values from -0.078125 to 0.078125
- near_lists: int32 [16, 32, 9], P('qx', 'qy'), may hold values from -1 to 511, as said below
- far_zero: int32 [16, 32, 27], P('qx', 'qy'), may hold values from -1 to 511, as said below
- far_one: int32 [8, 16, 27], P('qx', 'qy'), may hold values from -1 to 127, as said below
- far_two: int32 [4, 8, 27], P('qx', 'qy'), may hold values from -1 to 31, as said below
Outputs:
- product: bfloat16 [16, 32, 256, 256], P('qx', 'qy')
Inputs may be any that keep to these rules, and one draw needn't show every extreme that they name: Site p of leaf (i, j) lies at positions[i, j, 0, p] between i and i + 1 and positions[i, j, 1, p] between j and j + 1. `near_lists`: every entry of the list of leaf (i, j) is -1 or the id r * 32 + c of a leaf (r, c) with abs(r - i) <= 1 and abs(c - j) <= 1; the leaf's own id is always in its list, and no id stands twice. `far_zero`: every entry of the list of leaf (i, j) is -1 or the id r * 32 + c of a leaf (r, c) with max(abs(r - i), abs(c - j)) >= 2 whose parent (r // 2, c // 2) is within one step of (i // 2, j // 2) along each coordinate; no id stands twice. `far_one`: every entry of the list of level-1 cell (i, j) is -1 or the id r * 16 + c of a level-1 cell (r, c) with max(abs(r - i), abs(c - j)) >= 2 and (r // 2, c // 2) within one step of (i // 2, j // 2) along each coordinate; no id stands twice. `far_two`: every entry of the list of level-2 cell (i, j) is -1 or the id r * 8 + c of a level-2 cell (r, c) with max(abs(r - i), abs(c - j)) >= 2 and (r // 2, c // 2) within one step of (i // 2, j // 2) along each coordinate; no id stands twice.
All inputs are finite; a program needn't handle non-finite values.
Results may differ from a plain program's by a relative error of at most 0.0085.
Values may be sent and summed in bfloat16 or wider, within the bound.
No kernel may reach another device: no remote copies, remote signals or barrier semaphores. Data moves between devices by JAX's collectives and lax.ppermute only.
A program may use at most 256 MiB of HBM per device.

v0:
```python
import jax
import jax.numpy as jnp
import numpy as np
from jax import lax
from jax.sharding import PartitionSpec as P

root_three = 1.7320508075688772
length_scale = 1.0


def padded(block, sides, width):
    for axis, dim in sides:
        count = lax.axis_size(axis)
        forward = [(i, i + 1) for i in range(count - 1)]
        backward = [(target, source) for source, target in forward]
        low = lax.ppermute(
            lax.slice_in_dim(block, block.shape[dim] - width, None, axis=dim), axis, forward
        )
        high = lax.ppermute(lax.slice_in_dim(block, 0, width, axis=dim), axis, backward)
        block = jnp.concatenate([low, block, high], axis=dim)
    return block


def passed_along(x, axis, by):
    peers = lax.axis_size(axis)
    pairs = [(i, i + by) for i in range(peers) if 0 <= i + by < peers]
    return lax.ppermute(x, axis, pairs)


def offset_plan():
    slot_of = np.zeros((49,), np.int32)
    flip_of = np.zeros((49,), np.int32)
    active = np.zeros((49,), np.int32)
    upper_half = []
    for number in range(49):
        row_step = number // 7 - 3
        col_step = number % 7 - 3
        if max(abs(row_step), abs(col_step)) >= 2 and (
            row_step > 0 or (row_step == 0 and col_step > 0)
        ):
            upper_half.append(number)
    for number in range(49):
        row_step = number // 7 - 3
        col_step = number % 7 - 3
        if max(abs(row_step), abs(col_step)) >= 2:
            active[number] = 1
            if number in upper_half:
                slot_of[number] = upper_half.index(number)
            else:
                slot_of[number] = upper_half.index((3 - row_step) * 7 + 3 - col_step)
                flip_of[number] = 1
    return (slot_of, flip_of, active)


def coupling_table(level_couplings):
    slot_of, flip_of, active = offset_plan()
    pieces = []
    for number in range(49):
        matrix = level_couplings[int(slot_of[number])]
        if flip_of[number] == 1:
            matrix = matrix.T
        if active[number] == 0:
            matrix = jnp.zeros_like(matrix)
        pieces.append(matrix)
    return jnp.stack(pieces)


def matern_tiles(targets, sources, allowed):
    gap_rows = targets[:, 0][:, :, None] - sources[:, 0][:, None, :]
    gap_cols = targets[:, 1][:, :, None] - sources[:, 1][:, None, :]
    distance = jnp.sqrt(gap_rows * gap_rows + gap_cols * gap_cols)
    scaled = root_three * distance / length_scale
    variance = float(sources.shape[2]) ** (-0.5)
    kernel_value = (1.0 + scaled) * jnp.exp(-scaled) * variance
    return jnp.where(allowed[:, None, None], kernel_value, 0.0).astype(jnp.bfloat16)


def children_sum(transfer, coef):
    child_terms = jnp.einsum("xyrs,xyrc->xysc", transfer, coef, preferred_element_type=jnp.float32)
    grid_rows, grid_cols = (coef.shape[0], coef.shape[1])
    shaped = child_terms.reshape(
        grid_rows // 2, 2, grid_cols // 2, 2, transfer.shape[3], coef.shape[3]
    )
    return shaped.sum(axis=(1, 3))


def descend(transfer, parent):
    grid_rows, grid_cols = (parent.shape[0], parent.shape[1])
    shaped = transfer.reshape(grid_rows, 2, grid_cols, 2, transfer.shape[2], transfer.shape[3])
    spread = jnp.einsum("xaybrs,xysc->xaybrc", shaped, parent, preferred_element_type=jnp.float32)
    return spread.reshape(2 * grid_rows, 2 * grid_cols, transfer.shape[2], parent.shape[3])


def far_block(extended, lists, couple_table, first_row, first_col, ext_row, ext_col, grid_cols):
    block_rows, block_cols, slot_count = lists.shape
    ext_cols = extended.shape[1]
    flattened = extended.reshape(-1, extended.shape[2], extended.shape[3])
    source_ids = lists.reshape(block_rows * block_cols, slot_count)
    usable = source_ids >= 0
    clipped = jnp.maximum(source_ids, 0)
    source_row = clipped // grid_cols
    source_col = clipped % grid_cols
    cell_ids = jnp.arange(block_rows * block_cols, dtype=jnp.int32)
    target_row = first_row + (cell_ids // block_cols)[:, None]
    target_col = first_col + (cell_ids % block_cols)[:, None]
    offset_kind = jnp.clip((source_row - target_row + 3) * 7 + source_col - target_col + 3, 0, 48)
    located = jnp.clip(
        (source_row - ext_row) * ext_cols + source_col - ext_col, 0, flattened.shape[0] - 1
    )

    def one_cell(packed):
        places, kind_here, allowed = packed
        matrices = jnp.where(
            allowed[:, None, None], couple_table[kind_here], jnp.zeros((), couple_table.dtype)
        )
        return jnp.einsum(
            "jrs,jsc->rc", matrices, flattened[places], preferred_element_type=jnp.float32
        )

    result = lax.map(one_cell, (located, offset_kind, usable))
    return result.reshape(block_rows, block_cols, flattened.shape[1], flattened.shape[2])


def near_prepare(ext_samples, lists, positions, first_row, first_col, grid_cols):
    side_rows, side_cols, slot_count = lists.shape
    ext_cols = ext_samples.shape[1]
    flattened = ext_samples.reshape(-1, ext_samples.shape[2], ext_samples.shape[3])
    source_ids = lists.reshape(-1, slot_count)
    usable = source_ids >= 0
    clipped = jnp.maximum(source_ids, 0)
    located = (
        (clipped // grid_cols - first_row + 1) * ext_cols + clipped % grid_cols - first_col + 1
    )
    located = jnp.clip(located, 0, flattened.shape[0] - 1)
    site_count = positions.shape[3]
    sources = positions.reshape(-1, 2, site_count)[clipped]
    targets = lax.dynamic_slice(
        positions, (first_row, first_col, 0, 0), (side_rows, side_cols, 2, site_count)
    )
    return (flattened, located, usable, sources, targets.reshape(-1, 2, site_count))


def near_padded(flattened, located, usable, sources, targets):

    def one_leaf(packed):
        target, source_rows, places, allowed = packed
        kernel_tiles = matern_tiles(target[None], source_rows, allowed)
        return jnp.einsum(
            "jpq,jqc->pc", kernel_tiles, flattened[places], preferred_element_type=jnp.float32
        )

    return lax.map(one_leaf, (targets, sources, located, usable))


def per_device(
    positions,
    samples,
    leaf_basis,
    transfer_one,
    transfer_two,
    couplings,
    near_lists,
    far_zero,
    far_one,
    far_two,
):
    row_index = lax.axis_index("qx")
    col_index = lax.axis_index("qy")
    col_count = lax.axis_size("qy")
    leaf_side = samples.shape[0]
    half_side = leaf_side // 2
    leaf_cols = leaf_side * col_count
    first_row = row_index * leaf_side
    first_col = col_index * leaf_side
    ext_samples = padded(samples, (("qx", 0), ("qy", 1)), 1)
    coef_zero = jnp.einsum(
        "xypr,xypc->xyrc", leaf_basis, samples, preferred_element_type=jnp.float32
    ).astype(jnp.bfloat16)
    ext_zero = padded(coef_zero, (("qx", 0), ("qy", 1)), 2)
    coef_one = children_sum(transfer_one, coef_zero).astype(jnp.bfloat16)
    ext_one = padded(coef_one, (("qx", 0), ("qy", 1)), 2)
    coef_two = children_sum(transfer_two, coef_one).astype(jnp.bfloat16)
    center = coef_two[0, 0]
    column_list = []
    for offset in range(-3, 4):
        if offset == 0:
            column_list.append(center)
        else:
            column_list.append(passed_along(center, "qx", -offset))
    stacked = jnp.stack(column_list)
    row_list = []
    for offset in range(-3, 4):
        if offset == 0:
            row_list.append(stacked)
        else:
            row_list.append(passed_along(stacked, "qy", -offset))
    block_two = jnp.stack(row_list, axis=1)
    field_two = far_block(
        block_two,
        far_two,
        coupling_table(couplings[2]),
        row_index,
        col_index,
        row_index - 3,
        col_index - 3,
        col_count,
    )
    upper_row = row_index * half_side
    upper_col = col_index * half_side
    field_one = far_block(
        ext_one,
        far_one,
        coupling_table(couplings[1]),
        upper_row,
        upper_col,
        upper_row - 2,
        upper_col - 2,
        leaf_cols // 2,
    )
    field_zero = far_block(
        ext_zero,
        far_zero,
        coupling_table(couplings[0]),
        first_row,
        first_col,
        first_row - 2,
        first_col - 2,
        leaf_cols,
    )
    down_two = field_two.astype(jnp.bfloat16)
    down_one = (field_one + descend(transfer_two, down_two)).astype(jnp.bfloat16)
    down_zero = (field_zero + descend(transfer_one, down_one)).astype(jnp.bfloat16)
    flattened, located, usable, sources, targets = near_prepare(
        ext_samples, near_lists, positions, first_row, first_col, leaf_cols
    )
    near_field = near_padded(flattened, located, usable, sources, targets)
    near_field = near_field.reshape(samples.shape)
    total_sum = near_field + jnp.einsum(
        "xypr,xyrc->xypc", leaf_basis, down_zero, preferred_element_type=jnp.float32
    )
    return total_sum.astype(jnp.bfloat16)


def solution(mesh):
    return jax.shard_map(
        per_device,
        mesh=mesh,
        in_specs=(
            P(),
            P("qx", "qy", None, None),
            P("qx", "qy", None, None),
            P("qx", "qy", None, None),
            P("qx", "qy", None, None),
            P(),
            P("qx", "qy", None),
            P("qx", "qy", None),
            P("qx", "qy", None),
            P("qx", "qy", None),
        ),
        out_specs=P("qx", "qy", None, None),
        check_vma=False,
    )
```

profile of v0, /device:TPU:17, one launch (start us, length us, event | category | flops | bytes accessed | tf_op | source)
XLA Modules:
  0.0 1049.1 jit_solution(11415575953842415326)
XLA Ops:
  317.3 7.9 collective-permute-done.18
  325.3 19.8 %collective-permute-start.21 = (bf16[7,256,256]{1,2,0:T(8,128)(2,1)S(1)}, bf16[7,256,256]{1,2,0:T(8,128)(2,1)S(1)}, u32[]{:S(2)}, u32[]{:S(2)}) collective-permute-start(bf16[7,256,256]{1,2,0:T(8,128)(2,1)S(1)} %constant_dynamic-update-slice_fusion.141), channel_id=1, source_target_pairs={{1,0},{2,1},{3,2},{4,3},{5,4},{6,5},{7,6},{9,8},{10,9},{11,10},{12... | collective-permute-start | bytes 2752520 | tf_op jit(solution)/shard_map/ppermute | solution.py:27
  349.0 34.0 %collective-permute-done.20 = bf16[7,256,256]{1,2,0:T(8,128)(2,1)S(1)} collective-permute-done((bf16[7,256,256]{1,2,0:T(8,128)(2,1)S(1)}, bf16[7,256,256]{1,2,0:T(8,128)(2,1)S(1)}, u32[]{:S(2)}, u32[]{:S(2)}) %collective-permute-start.20) | collective-permute-done | bytes 917536 | tf_op jit(solution)/shard_map/ppermute | solution.py:27
  395.3 29.1 %collective-permute-done.23 = bf16[7,256,256]{1,2,0:T(8,128)(2,1)S(1)} collective-permute-done((bf16[7,256,256]{1,2,0:T(8,128)(2,1)S(1)}, bf16[7,256,256]{1,2,0:T(8,128)(2,1)S(1)}, u32[]{:S(2)}, u32[]{:S(2)}) %collective-permute-start.23) | collective-permute-done | bytes 917536 | tf_op jit(solution)/shard_map/ppermute | solution.py:27
  427.3 10.9 %copy.145 = bf16[7,7,256,256]{3,2,1,0:T(8,128)(2,1)} copy(bf16[7,7,256,256]{2,3,0,1:T(8,128)(2,1)} %bitcast_dynamic-update-slice_fusion) | data formatting | bytes 12845056 | tf_op jit(solution)/shard_map/stack | solution.py:197
  459.5 31.0 %collective-permute-done.2 = bf16[6,1,256,256]{3,2,1,0:T(8,128)(2,1)S(1)} collective-permute-done((bf16[6,1,256,256]{3,2,1,0:T(8,128)(2,1)}, bf16[6,1,256,256]{3,2,1,0:T(8,128)(2,1)S(1)}, u32[]{:S(2)}, u32[]{:S(2)}) %collective-permute-start.2) | collective-permute-done | bytes 786464 | tf_op jit(solution)/shard_map/ppermute | solution.py:16
  490.4 21.7 %collective-permute-start.7 = (bf16[8,2,256,256]{3,2,1,0:T(8,128)(2,1)}, bf16[8,2,256,256]{3,2,1,0:T(8,128)(2,1)}, u32[]{:S(2)}, u32[]{:S(2)}) collective-permute-start(bf16[8,2,256,256]{3,2,1,0:T(8,128)(2,1)} %get-tuple-element.318), channel_id=1, source_target_pairs={{1,0},{2,1},{3,2},{4,3},{5,4},{6,5},{7,6},{9,8},{10,9},{11,10},{12... | collective-permute-start | bytes 6291464 | tf_op jit(solution)/shard_map/ppermute | solution.py:19
  512.2 42.1 %collective-permute-done.3 = bf16[6,1,256,256]{3,2,1,0:T(8,128)(2,1)} collective-permute-done((bf16[6,1,256,256]{3,2,1,0:T(8,128)(2,1)}, bf16[6,1,256,256]{3,2,1,0:T(8,128)(2,1)}, u32[]{:S(2)}, u32[]{:S(2)}) %collective-permute-start.3) | collective-permute-done | bytes 786464 | tf_op jit(solution)/shard_map/ppermute | solution.py:19
  557.6 112.8 %while.34 = (s32[]{:T(128)}, f32[16,256,256]{1,2,0:T(8,128)}, pred[16,9]{1,0:T(8,128)(4,1)}, f32[16,2,256]{2,1,0:T(2,128)S(1)}, f32[16,9,2,256]{3,2,1,0:T(2,128)...) while((s32[]{:T(128)}, f32[16,256,256]{1,2,0:T(8,128)}, ...), condition=%wide.region_1.0_spmd, body=%wide.region_0.0_spmd.sunk | while | flops 309068832 | bytes 3941168 | solution.py:152
  675.9 6.6 copy.123
  682.6 63.7 %while.36 = (s32[]{:T(128)}, f32[4,256,256]{1,2,0:T(8,128)}, pred[4,27]{1,0:T(4,128)(4,1)S(1)}, s32[4,27]{1,0:T(4,128)S(1)}, bf16[49,256,256]{2,1,0:T(8,128)(2,1...) while((s32[]{:T(128)}, f32[4,256,256]{1,2,0:T(8,128)}, pred[4,27]{1,0:T(4,128)(4,1)S(1)}, ...), condition=%wide.region_6.7_spmd, body=%wide.region_5.6_spmd.sunk | while | flops 907741376 | bytes 21505548 | solution.py:120
  755.6 7.3 pad_maximum_fusion
  762.9 274.4 %while.35 = (s32[]{:T(128)}, f32[16,256,256]{2,1,0:T(8,128)}, pred[16,27]{1,0:T(8,128)(4,1)}, s32[16,27]{1,0:T(8,128)S(1)}, bf16[49,256,256]{2,1,0:T(8,128)(2,1)...) while((s32[]{:T(128)}, f32[16,256,256]{2,1,0:T(8,128)}, pred[16,27]{1,0:T(8,128)(4,1)}, ...), condition=%wide.region_3.4_spmd, body=%wide.region_2.3_spmd.sunk | while | flops 907741376 | bytes 21505548 | solution.py:120
  762.9 6.0 gather_fusion.1
  780.0 6.0 gather_fusion.1
  797.2 6.0 gather_fusion.1
  814.3 6.0 gather_fusion.1
  831.5 6.0 gather_fusion.1
  848.6 6.0 gather_fusion.1
  882.9 6.0 gather_fusion.1
  934.4 6.0 gather_fusion.1
  951.5 6.0 gather_fusion.1
  968.7 6.0 gather_fusion.1
  1037.3 7.6 fusion.48
  (588 shorter events, 769.6 us)
Async XLA Ops:
  10.1 272.1 %collective-permute-start.12 = (bf16[256,256]{0,1:T(8,128)(2,1)S(1)}, bf16[256,256]{0,1:T(8,128)(2,1)}, u32[]{:S(2)}, u32[]{:S(2)}) collective-permute-start(bf16[256,256]{0,1:T(8,128)(2,1)S(1)} %bitcast.742), channel_id=1, source_target_pairs={{0,24},{1,25},{2,26},{3,27},{4,28},{5,29},{6,30},{7,31}} | collective-permute-start | bytes 393224 | tf_op jit(solution)/shard_map/ppermute | solution.py:27
  11.4 272.5 %collective-permute-start.13 = (bf16[256,256]{0,1:T(8,128)(2,1)S(1)}, bf16[256,256]{0,1:T(8,128)(2,1)}, u32[]{:S(2)}, u32[]{:S(2)}) collective-permute-start(bf16[256,256]{0,1:T(8,128)(2,1)S(1)} %bitcast.743), channel_id=1, source_target_pairs={{0,16},{8,24},{1,17},{9,25},{2,18},{10,26},{3,19},{11,27},{4,20},{... | collective-permute-start | bytes 393224 | tf_op jit(solution)/shard_map/ppermute | solution.py:27
  15.2 273.8 %collective-permute-start.14 = (bf16[256,256]{0,1:T(8,128)(2,1)S(1)}, bf16[256,256]{0,1:T(8,128)(2,1)}, u32[]{:S(2)}, u32[]{:S(2)}) collective-permute-start(bf16[256,256]{0,1:T(8,128)(2,1)S(1)} %bitcast.744), channel_id=1, source_target_pairs={{0,8},{8,16},{16,24},{1,9},{9,17},{17,25},{2,10},{10,18},{18,26},{... | collective-permute-start | bytes 393224 | tf_op jit(solution)/shard_map/ppermute | solution.py:27
  17.1 274.8 %collective-permute-start.15 = (bf16[256,256]{0,1:T(8,128)(2,1)S(1)}, bf16[256,256]{0,1:T(8,128)(2,1)}, u32[]{:S(2)}, u32[]{:S(2)}) collective-permute-start(bf16[256,256]{0,1:T(8,128)(2,1)S(1)} %bitcast.745), channel_id=1, source_target_pairs={{8,0},{16,8},{24,16},{9,1},{17,9},{25,17},{10,2},{18,10},{26,18},{... | collective-permute-start | bytes 393224 | tf_op jit(solution)/shard_map/ppermute | solution.py:27
  20.2 276.3 %collective-permute-start.16 = (bf16[256,256]{0,1:T(8,128)(2,1)S(1)}, bf16[256,256]{0,1:T(8,128)(2,1)}, u32[]{:S(2)}, u32[]{:S(2)}) collective-permute-start(bf16[256,256]{0,1:T(8,128)(2,1)S(1)} %bitcast.746), channel_id=1, source_target_pairs={{16,0},{24,8},{17,1},{25,9},{18,2},{26,10},{19,3},{27,11},{20,4},{... | collective-permute-start | bytes 393224 | tf_op jit(solution)/shard_map/ppermute | solution.py:27
  282.2 17.2 %collective-permute-start.17 = (bf16[256,256]{0,1:T(8,128)(2,1)S(1)}, bf16[256,256]{0,1:T(8,128)(2,1)S(1)}, u32[]{:S(2)}, u32[]{:S(2)}) collective-permute-start(bf16[256,256]{0,1:T(8,128)(2,1)S(1)} %bitcast.747), channel_id=1, source_target_pairs={{24,0},{25,1},{26,2},{27,3},{28,4},{29,5},{30,6},{31,7}} | collective-permute-start | bytes 393224 | tf_op jit(solution)/shard_map/ppermute | solution.py:27
  283.9 20.4 %collective-permute-start.8 = (bf16[2,2,256,256]{2,3,1,0:T(8,128)(2,1)S(1)}, bf16[2,2,256,256]{2,3,1,0:T(8,128)(2,1)S(1)}, u32[]{:S(2)}, u32[]{:S(2)}) collective-permute-start(bf16[2,2,256,256]{2,3,1,0:T(8,128)(2,1)S(1)} %reduce_sum.8), channel_id=1, source_target_pairs={{0,8},{8,16},{16,24},{1,9},{9,17},{17,25},{2,10},{10,18},{18,26},{... | collective-permute-start | bytes 1572872 | tf_op jit(solution)/shard_map/ppermute | solution.py:16
  289.1 19.2 %collective-permute-start.9 = (bf16[2,2,256,256]{2,3,1,0:T(8,128)(2,1)S(1)}, bf16[2,2,256,256]{2,3,1,0:T(8,128)(2,1)S(1)}, u32[]{:S(2)}, u32[]{:S(2)}) collective-permute-start(bf16[2,2,256,256]{2,3,1,0:T(8,128)(2,1)S(1)} %reduce_sum.8), channel_id=1, source_target_pairs={{8,0},{16,8},{24,16},{9,1},{17,9},{25,17},{10,2},{18,10},{26,18},{... | collective-permute-start | bytes 1572872 | tf_op jit(solution)/shard_map/ppermute | solution.py:19
  291.9 19.8 %collective-permute-start = (bf16[1,4,256,256]{3,2,1,0:T(8,128)(2,1)}, bf16[1,4,256,256]{3,2,1,0:T(8,128)(2,1)S(1)}, u32[]{:S(2)}, u32[]{:S(2)}) collective-permute-start(bf16[1,4,256,256]{3,2,1,0:T(8,128)(2,1)} %get-tuple-element.324), channel_id=1, source_target_pairs={{0,8},{8,16},{16,24},{1,9},{9,17},{17,25},{2,10},{10,18},{18,26},{... | collective-permute-start | bytes 1572872 | tf_op jit(solution)/shard_map/ppermute | solution.py:16
  296.5 17.5 %collective-permute-start.1 = (bf16[1,4,256,256]{3,2,1,0:T(8,128)(2,1)}, bf16[1,4,256,256]{3,2,1,0:T(8,128)(2,1)S(1)}, u32[]{:S(2)}, u32[]{:S(2)}) collective-permute-start(bf16[1,4,256,256]{3,2,1,0:T(8,128)(2,1)} %get-tuple-element.323), channel_id=1, source_target_pairs={{8,0},{16,8},{24,16},{9,1},{17,9},{25,17},{10,2},{18,10},{26,18},{... | collective-permute-start | bytes 1572872 | tf_op jit(solution)/shard_map/ppermute | solution.py:19
  299.4 25.9 %collective-permute-start.18 = (bf16[7,256,256]{1,2,0:T(8,128)(2,1)S(1)}, bf16[7,256,256]{1,2,0:T(8,128)(2,1)S(1)}, u32[]{:S(2)}, u32[]{:S(2)}) collective-permute-start(bf16[7,256,256]{1,2,0:T(8,128)(2,1)S(1)} %constant_dynamic-update-slice_fusion.141), channel_id=1, source_target_pairs={{0,3},{1,4},{2,5},{3,6},{4,7},{8,11},{9,12},{10,13},{11,14},{12,15... | collective-permute-start | bytes 2752520 | tf_op jit(solution)/shard_map/ppermute | solution.py:27
  304.3 133.9 %collective-permute-start.4 = (bf16[2,4,256,256]{3,2,1,0:T(8,128)(2,1)}, bf16[2,4,256,256]{3,2,1,0:T(8,128)(2,1)}, u32[]{:S(2)}, u32[]{:S(2)}) collective-permute-start(bf16[2,4,256,256]{3,2,1,0:T(8,128)(2,1)} %get-tuple-element.321), channel_id=1, source_target_pairs={{0,8},{8,16},{16,24},{1,9},{9,17},{17,25},{2,10},{10,18},{18,26},{... | collective-permute-start | bytes 3145736 | tf_op jit(solution)/shard_map/ppermute | solution.py:16
  308.3 134.2 %collective-permute-start.5 = (bf16[2,4,256,256]{3,2,1,0:T(8,128)(2,1)}, bf16[2,4,256,256]{3,2,1,0:T(8,128)(2,1)}, u32[]{:S(2)}, u32[]{:S(2)}) collective-permute-start(bf16[2,4,256,256]{3,2,1,0:T(8,128)(2,1)} %get-tuple-element.322), channel_id=1, source_target_pairs={{8,0},{16,8},{24,16},{9,1},{17,9},{25,17},{10,2},{18,10},{26,18},{... | collective-permute-start | bytes 3145736 | tf_op jit(solution)/shard_map/ppermute | solution.py:19
  311.8 34.3 %collective-permute-start.19 = (bf16[7,256,256]{1,2,0:T(8,128)(2,1)S(1)}, bf16[7,256,256]{1,2,0:T(8,128)(2,1)S(1)}, u32[]{:S(2)}, u32[]{:S(2)}) collective-permute-start(bf16[7,256,256]{1,2,0:T(8,128)(2,1)S(1)} %constant_dynamic-update-slice_fusion.141), channel_id=1, source_target_pairs={{0,2},{1,3},{2,4},{3,5},{4,6},{5,7},{8,10},{9,11},{10,12},{11,13},... | collective-permute-start | bytes 2752520 | tf_op jit(solution)/shard_map/ppermute | solution.py:27
  314.0 69.0 %collective-permute-start.20 = (bf16[7,256,256]{1,2,0:T(8,128)(2,1)S(1)}, bf16[7,256,256]{1,2,0:T(8,128)(2,1)S(1)}, u32[]{:S(2)}, u32[]{:S(2)}) collective-permute-start(bf16[7,256,256]{1,2,0:T(8,128)(2,1)S(1)} %constant_dynamic-update-slice_fusion.141), channel_id=1, source_target_pairs={{0,1},{1,2},{2,3},{3,4},{4,5},{5,6},{6,7},{8,9},{9,10},{10,11},{11... | collective-permute-start | bytes 2752520 | tf_op jit(solution)/shard_map/ppermute | solution.py:27
  325.3 61.9 %collective-permute-start.21 = (bf16[7,256,256]{1,2,0:T(8,128)(2,1)S(1)}, bf16[7,256,256]{1,2,0:T(8,128)(2,1)S(1)}, u32[]{:S(2)}, u32[]{:S(2)}) collective-permute-start(bf16[7,256,256]{1,2,0:T(8,128)(2,1)S(1)} %constant_dynamic-update-slice_fusion.141), channel_id=1, source_target_pairs={{1,0},{2,1},{3,2},{4,3},{5,4},{6,5},{7,6},{9,8},{10,9},{11,10},{12... | collective-permute-start | bytes 2752520 | tf_op jit(solution)/shard_map/ppermute | solution.py:27
  346.1 43.9 %collective-permute-start.22 = (bf16[7,256,256]{1,2,0:T(8,128)(2,1)S(1)}, bf16[7,256,256]{1,2,0:T(8,128)(2,1)S(1)}, u32[]{:S(2)}, u32[]{:S(2)}) collective-permute-start(bf16[7,256,256]{1,2,0:T(8,128)(2,1)S(1)} %constant_dynamic-update-slice_fusion.141), channel_id=1, source_target_pairs={{2,0},{3,1},{4,2},{5,3},{6,4},{7,5},{10,8},{11,9},{12,10},{13,11},... | collective-permute-start | bytes 2752520 | tf_op jit(solution)/shard_map/ppermute | solution.py:27
  383.0 41.3 %collective-permute-start.23 = (bf16[7,256,256]{1,2,0:T(8,128)(2,1)S(1)}, bf16[7,256,256]{1,2,0:T(8,128)(2,1)S(1)}, u32[]{:S(2)}, u32[]{:S(2)}) collective-permute-start(bf16[7,256,256]{1,2,0:T(8,128)(2,1)S(1)} %constant_dynamic-update-slice_fusion.141), channel_id=1, source_target_pairs={{3,0},{4,1},{5,2},{6,3},{7,4},{11,8},{12,9},{13,10},{14,11},{15,12... | collective-permute-start | bytes 2752520 | tf_op jit(solution)/shard_map/ppermute | solution.py:27
  387.1 283.3 %collective-permute-start.10 = (bf16[6,2,256,256]{2,3,1,0:T(8,128)(2,1)}, bf16[6,2,256,256]{2,3,1,0:T(8,128)(2,1)}, u32[]{:S(2)}, u32[]{:S(2)}) collective-permute-start(bf16[6,2,256,256]{2,3,1,0:T(8,128)(2,1)} %pad_maximum_fusion.4), channel_id=1, source_target_pairs={{0,1},{1,2},{2,3},{3,4},{4,5},{5,6},{6,7},{8,9},{9,10},{10,11},{11... | collective-permute-start | bytes 4718600 | tf_op jit(solution)/shard_map/ppermute | solution.py:16
  390.0 280.4 %collective-permute-start.11 = (bf16[6,2,256,256]{2,3,1,0:T(8,128)(2,1)}, bf16[6,2,256,256]{2,3,1,0:T(8,128)(2,1)}, u32[]{:S(2)}, u32[]{:S(2)}) collective-permute-start(bf16[6,2,256,256]{2,3,1,0:T(8,128)(2,1)} %pad_maximum_fusion.4), channel_id=1, source_target_pairs={{1,0},{2,1},{3,2},{4,3},{5,4},{6,5},{7,6},{9,8},{10,9},{11,10},{12... | collective-permute-start | bytes 4718600 | tf_op jit(solution)/shard_map/ppermute | solution.py:19
  424.4 66.1 %collective-permute-start.2 = (bf16[6,1,256,256]{3,2,1,0:T(8,128)(2,1)}, bf16[6,1,256,256]{3,2,1,0:T(8,128)(2,1)S(1)}, u32[]{:S(2)}, u32[]{:S(2)}) collective-permute-start(bf16[6,1,256,256]{3,2,1,0:T(8,128)(2,1)} %get-tuple-element.319), channel_id=1, source_target_pairs={{0,1},{1,2},{2,3},{3,4},{4,5},{5,6},{6,7},{8,9},{9,10},{10,11},{11... | collective-permute-start | bytes 2359304 | tf_op jit(solution)/shard_map/ppermute | solution.py:16
  438.2 116.1 %collective-permute-start.3 = (bf16[6,1,256,256]{3,2,1,0:T(8,128)(2,1)}, bf16[6,1,256,256]{3,2,1,0:T(8,128)(2,1)}, u32[]{:S(2)}, u32[]{:S(2)}) collective-permute-start(bf16[6,1,256,256]{3,2,1,0:T(8,128)(2,1)} %get-tuple-element.320), channel_id=1, source_target_pairs={{1,0},{2,1},{3,2},{4,3},{5,4},{6,5},{7,6},{9,8},{10,9},{11,10},{12... | collective-permute-start | bytes 2359304 | tf_op jit(solution)/shard_map/ppermute | solution.py:19
  447.3 308.3 %collective-permute-start.6 = (bf16[8,2,256,256]{3,2,1,0:T(8,128)(2,1)}, bf16[8,2,256,256]{3,2,1,0:T(8,128)(2,1)}, u32[]{:S(2)}, u32[]{:S(2)}) collective-permute-start(bf16[8,2,256,256]{3,2,1,0:T(8,128)(2,1)} %get-tuple-element.317), channel_id=1, source_target_pairs={{0,1},{1,2},{2,3},{3,4},{4,5},{5,6},{6,7},{8,9},{9,10},{10,11},{11... | collective-permute-start | bytes 6291464 | tf_op jit(solution)/shard_map/ppermute | solution.py:16
  490.4 265.1 %collective-permute-start.7 = (bf16[8,2,256,256]{3,2,1,0:T(8,128)(2,1)}, bf16[8,2,256,256]{3,2,1,0:T(8,128)(2,1)}, u32[]{:S(2)}, u32[]{:S(2)}) collective-permute-start(bf16[8,2,256,256]{3,2,1,0:T(8,128)(2,1)} %get-tuple-element.318), channel_id=1, source_target_pairs={{1,0},{2,1},{3,2},{4,3},{5,4},{6,5},{7,6},{9,8},{10,9},{11,10},{12... | collective-permute-start | bytes 6291464 | tf_op jit(solution)/shard_map/ppermute | solution.py:19
  (27 other events, 893.0 us)
where the time goes:
time: 1060 us; the launch traced here: 1050 us
  local copies, waits for them, and re-layouts  611 us (58%)
  matrix products  165 us (16%)
  waiting for transfers between devices  144 us (14%)
  starting transfers between devices  97.4 us (9%)
  other arithmetic  29.5 us (3%)
    unnamed x164, local copies, waits for them, and re-layouts  148 us
    gather x21, local copies, waits for them, and re-layouts, one_cell(): flattened[places]  121 us
    gather x21, local copies, waits for them, and re-layouts, one_cell(): couple_table[kind_here]  116 us
    dot_general x21, matrix products, one_cell(): jnp.einsum('jrs,jsc->rc', matrices, flattened[places], preferred_element_...  105 us
    another operation x65, local copies, waits for them, and re-layouts, coupling_table(): return jnp.stack(pieces)  104 us
    ppermute x12, waiting for transfers between devices, passed_along(): return lax.ppermute(x, axis, pairs)  71.1 us
    gather x16, local copies, waits for them, and re-layouts, one_leaf(): flattened[places]  47.3 us
    ppermute x12, starting transfers between devices, passed_along(): return lax.ppermute(x, axis, pairs)  43.7 us
  transfers between devices with their start and end apart: 24, of which 5 were waited for; matrix products, arithmetic and copies ran while one was open for 48% of the time, Pallas kernels for 0%

commit v1 on v0

v1 whole, which is shorter than its diff:
```python
import functools

import jax
import jax.numpy as jnp
import numpy as np
from jax import lax
from jax.experimental import pallas as pl
from jax.experimental.pallas import tpu as pltpu
from jax.sharding import PartitionSpec as P

root_three = 1.7320508075688772
length_scale = 1.0
VMEM = pltpu.VMEM
SMEM = pltpu.SMEM
F32 = jnp.float32
BF16 = jnp.bfloat16
BIG = 60 * 1024 * 1024


def nn(a, b):
    return lax.dot_general(a, b, (((1,), (0,)), ((), ())), preferred_element_type=F32)


def nt(a, b):
    return lax.dot_general(a, b, (((1,), (1,)), ((), ())), preferred_element_type=F32)


def tn(a, b):
    return lax.dot_general(a, b, (((0,), (0,)), ((), ())), preferred_element_type=F32)


def params():
    return pltpu.CompilerParams(vmem_limit_bytes=BIG)


def cost(products, bytes_accessed):
    return pl.CostEstimate(
        flops=products * 2 * 256**3, bytes_accessed=bytes_accessed, transcendentals=0
    )


def half_offsets():
    kept = []
    for u in range(-3, 4):
        for v in range(-3, 4):
            if max(abs(u), abs(v)) >= 2 and (u > 0 or (u == 0 and v > 0)):
                kept.append((u, v))
    return kept


HALF_OFFSETS = half_offsets()


def class_plan(a, b):
    plain, turned = [], []
    for w in range(36):
        u, v = w // 6 - 2 - a, w % 6 - 2 - b
        if max(abs(u), abs(v)) < 2:
            continue
        if (u, v) in HALF_OFFSETS:
            plain.append((w, HALF_OFFSETS.index((u, v))))
        else:
            turned.append((w, HALF_OFFSETS.index((-u, -v))))
    return plain, turned


def coef_kernel(samples, basis, t_one, t_two, top, bottom, left, right, upper, own_one):
    side = samples.shape[0]
    half = side // 2
    coef = {}
    for x in range(side):
        for y in range(side):
            value = tn(samples[x, y], basis[x, y]).astype(BF16)
            coef[x, y] = value
            if x < half:
                top[x * side + y] = value
            else:
                bottom[(x - half) * side + y] = value
            if y < 2:
                left[x * 2 + y] = value
            if y >= side - 2:
                right[x * 2 + y - (side - 2)] = value
    ones = []
    for x in range(half):
        for y in range(half):
            kids = [(2 * x + a, 2 * y + b) for a in range(2) for b in range(2)]
            lhs = jnp.concatenate([coef[k] for k in kids], axis=1)
            rhs = jnp.concatenate([t_one[k] for k in kids], axis=0)
            value = nn(lhs, rhs).astype(BF16)
            ones.append(value)
            upper[x * half + y] = value
    kids = [(a, b) for a in range(2) for b in range(2)]
    lhs = jnp.concatenate(ones, axis=1)
    rhs = jnp.concatenate([t_two[k] for k in kids], axis=0)
    upper[4] = nn(lhs, rhs).astype(BF16)
    own_one[...] = upper[0:4]


def coefficients(samples, basis, t_one, t_two):
    tile = lambda n: jax.ShapeDtypeStruct((n, 256, 256), BF16)
    return pl.pallas_call(
        coef_kernel,
        out_shape=(tile(8), tile(8), tile(8), tile(8), tile(5), tile(4)),
        compiler_params=params(),
        cost_estimate=cost(36, 12 << 20),
        name="coefficients",
    )(samples, basis, t_one, t_two)


def split3(x):
    first = x.astype(BF16).astype(F32)
    rest = x - first
    second = rest.astype(BF16).astype(F32)
    return first, second, rest - second


def near_kernel(
    grid_rows,
    grid_cols,
    corner,
    weight,
    positions,
    own,
    left,
    right,
    top,
    bottom,
    near,
    held,
    target_feat,
    source_feat,
    sems,
):
    side = 4
    copies = []

    def bring(src, dst):
        copy = pltpu.make_async_copy(src, dst, sems.at[len(copies)])
        copy.start()
        copies.append(copy)

    bring(top, held.at[0:6])
    bring(bottom, held.at[30:36])
    for x in range(side):
        base = (x + 1) * 6
        bring(left.at[x], held.at[base])
        bring(own.at[x], held.at[base + 1 : base + 5])
        bring(right.at[x], held.at[base + 5])

    first_row = corner[0]
    first_col = corner[1]
    mid_row = (first_row + 2).astype(F32)
    mid_col = (first_col + 2).astype(F32)
    row_number = lax.broadcasted_iota(jnp.int32, (32, 256), 0)

    def features(place, carry):
        r = jnp.clip(first_row + place // 6 - 1, 0, grid_rows - 1)
        c = jnp.clip(first_col + place % 6 - 1, 0, grid_cols - 1)
        here = positions[r * grid_cols + c]
        x = (here[0:1] - mid_row) * (root_three / length_scale)
        y = (here[1:2] - mid_col) * (root_three / length_scale)
        square = x * x + y * y
        xs, ys, squares = split3(x), split3(y), split3(square)
        one = jnp.ones_like(x)
        pairs = []
        for part in squares:
            pairs.append((part, one))
            pairs.append((one, part))
        for parts in (xs, ys):
            for m, n in ((0, 0), (0, 1), (1, 0), (1, 1), (0, 2), (2, 0)):
                pairs.append((-2.0 * parts[m], parts[n]))
        target = jnp.zeros((32, 256), F32)
        source = jnp.zeros((32, 256), F32)
        for k, (p, q) in enumerate(pairs):
            target = jnp.where(row_number == k, p, target)
            source = jnp.where(row_number == k, q, source)
        target_feat[place] = target.astype(BF16)
        source_feat[place] = source.astype(BF16)
        return carry

    lax.fori_loop(0, 36, features, 0)
    for copy in copies:
        copy.wait()

    def one_target(t, carry):
        r = t // side
        c = t % side
        place = (r + 1) * 6 + c + 1
        target = target_feat[place].astype(F32).T.astype(BF16)
        tiles = []
        blocks = []
        for k in range(9):
            at = (r + k // 3) * 6 + c + k % 3
            scaled_sq = jnp.maximum(nn(target, source_feat[at]), 1e-24)
            a = scaled_sq * lax.rsqrt(scaled_sq)
            w = weight[t, k]
            tiles.append(((a * w + w) * jnp.exp(-a)).astype(BF16))
            blocks.append(held[at])
        near[t] = nn(jnp.concatenate(tiles, axis=1), jnp.concatenate(blocks, axis=0))
        return carry

    lax.fori_loop(0, side * side, one_target, 0)


def near_field(grid_rows, grid_cols, corner, weight, positions, own, left, right, top, bottom):
    any_space = pl.BlockSpec(memory_space=pl.ANY)
    smem = pl.BlockSpec(memory_space=SMEM)
    return pl.pallas_call(
        functools.partial(near_kernel, grid_rows, grid_cols),
        out_shape=jax.ShapeDtypeStruct((16, 256, 256), F32),
        in_specs=[smem, smem, pl.BlockSpec(memory_space=VMEM)] + [any_space] * 5,
        out_specs=pl.BlockSpec(memory_space=VMEM),
        scratch_shapes=[
            VMEM((36, 256, 256), BF16),
            VMEM((36, 32, 256), BF16),
            VMEM((36, 32, 256), BF16),
            pltpu.SemaphoreType.DMA((14,)),
        ],
        compiler_params=params(),
        cost_estimate=cost(400, 12 << 20),
        name="near_field",
    )(corner, weight, positions, own, left, right, top, bottom)


def coupled(plan, couplings, held, places):
    plain, turned = plan
    total = None
    if plain:
        rows = len(places(plain[0][0]))
        lhs = jnp.concatenate(
            [
                jnp.concatenate([held[places(w)[n]] for w, _ in plain], axis=1)
                for n in range(rows)
            ],
            axis=0,
        )
        rhs = jnp.concatenate([couplings[k] for _, k in plain], axis=1)
        total = nt(lhs, rhs)
    if turned:
        rows = len(places(turned[0][0]))
        lhs = jnp.concatenate(
            [
                jnp.concatenate([held[places(w)[n]] for w, _ in turned], axis=1)
                for n in range(rows)
            ],
            axis=0,
        )
        rhs = jnp.concatenate([couplings[k] for _, k in turned], axis=0)
        part = nn(lhs, rhs)
        total = part if total is None else total + part
    return total


def upper_kernel(
    parity, at_one, at_two, couplings, t_two, row, row_e, row_d, cells, cells_e, down, held_one, held_two, field_two, sems
):
    n_one = row.shape[0]
    n_two = cells.shape[0]
    copies = []

    def bring(src, dst):
        copy = pltpu.make_async_copy(src, dst, sems.at[len(copies)])
        copy.start()
        copies.append(copy)

    bring(cells, held_two.at[0:n_two])
    bring(cells_e, held_two.at[n_two : 2 * n_two])
    bring(row, held_one.at[0:n_one])
    bring(row_e, held_one.at[n_one : 2 * n_one])
    bring(row_d, held_one.at[2 * n_one : 3 * n_one])
    held_one[3 * n_one] = jnp.zeros((256, 256), BF16)
    held_two[2 * n_two] = jnp.zeros((256, 256), BF16)
    for copy in copies:
        copy.wait()
    for a in range(2):
        for b in range(2):

            @pl.when((parity[0] == a) & (parity[1] == b))
            def _():
                field_two[...] = coupled(
                    class_plan(a, b), couplings.at[1], held_two, lambda w: [at_two[0, w]]
                ).astype(BF16)

    for a in range(2):
        for b in range(2):
            t = a * 2 + b
            field = coupled(class_plan(a, b), couplings.at[0], held_one, lambda w: [at_one[t, w]])
            down[t] = (field + nt(field_two[...], t_two[a, b])).astype(BF16)


def upper_levels(parity, at_one, at_two, couplings, t_two, row, row_e, row_d, cells, cells_e):
    any_space = pl.BlockSpec(memory_space=pl.ANY)
    smem = pl.BlockSpec(memory_space=SMEM)
    n_one, n_two = row.shape[0], cells.shape[0]
    return pl.pallas_call(
        upper_kernel,
        grid=(1,),
        out_shape=jax.ShapeDtypeStruct((4, 256, 256), BF16),
        in_specs=[
            smem,
            smem,
            smem,
            pl.BlockSpec((pl.Element(2), pl.Element(20), pl.Element(256), pl.Element(256)), lambda g: (1, 0, 0, 0)),
            pl.BlockSpec((2, 2, 256, 256), lambda g: (0, 0, 0, 0)),
        ]
        + [any_space] * 5,
        out_specs=pl.BlockSpec((4, 256, 256), lambda g: (0, 0, 0)),
        scratch_shapes=[
            VMEM((3 * n_one + 1, 256, 256), BF16),
            VMEM((2 * n_two + 1, 256, 256), BF16),
            VMEM((256, 256), BF16),
            pltpu.SemaphoreType.DMA((5,)),
        ],
        compiler_params=params(),
        cost_estimate=cost(140, 14 << 20),
        name="upper_levels",
    )(parity, at_one, at_two, couplings, t_two, row, row_e, row_d, cells, cells_e)


HELD_ZERO = 64


def held_place(r, c):
    rows_in = 2 <= r < 6
    cols_in = 2 <= c < 6
    if rows_in and cols_in:
        return (r - 2) * 4 + c - 2
    if rows_in:
        return (16 if c < 2 else 24) + (r - 2) * 2 + (c if c < 2 else c - 6)
    if cols_in:
        return (32 if r < 2 else 40) + (r if r < 2 else r - 6) * 4 + c - 2
    base = 48 if r < 2 else 56
    return base + (0 if c < 2 else 4) + (r if r < 2 else r - 6) * 2 + (c if c < 2 else c - 6)


def leaf_kernel(
    at, couplings, t_one, basis, down_one, near, *rest
):
    sources = rest[:8]
    out, held, sems = rest[8:]
    step = pl.program_id(0)

    @pl.when(step == 0)
    def _():
        copies = []
        for n, src in enumerate(sources):
            copy = pltpu.make_async_copy(src, held.at[8 * n : 8 * n + 8], sems.at[n])
            copy.start()
            copies.append(copy)
        held[HELD_ZERO] = jnp.zeros((256, 256), BF16)
        for copy in copies:
            copy.wait()

    for a in range(2):
        for b in range(2):

            @pl.when(step == a * 2 + b)
            def _():
                targets = [(x, y) for x in range(2) for y in range(2)]
                numbers = [(2 * x + a) * 4 + 2 * y + b for x, y in targets]
                field = coupled(
                    class_plan(a, b), couplings.at[0], held, lambda w: [at[n, w] for n in numbers]
                )
                for n, (x, y) in enumerate(targets):
                    down = field[n * 256 : n * 256 + 256] + nt(down_one[x * 2 + y], t_one[x, 0, y, 0])
                    down = down.astype(BF16)
                    total = near[x, 0, y, 0] + nt(basis[x, 0, y, 0], down)
                    out[x, 0, y, 0] = total.astype(BF16)


def leaf_level(at, couplings, t_one, basis, down_one, near, sources):
    any_space = pl.BlockSpec(memory_space=pl.ANY)
    smem = pl.BlockSpec(memory_space=SMEM)
    grouped = lambda x: x.reshape(2, 2, 2, 2, 256, 256)
    block = pl.BlockSpec((2, 1, 2, 1, 256, 256), lambda g: (0, g // 2, 0, g % 2, 0, 0))
    return pl.pallas_call(
        leaf_kernel,
        grid=(4,),
        out_shape=jax.ShapeDtypeStruct((2, 2, 2, 2, 256, 256), BF16),
        in_specs=[
            smem,
            pl.BlockSpec((1, 20, 256, 256), lambda g: (0, 0, 0, 0)),
            block,
            block,
            pl.BlockSpec((4, 256, 256), lambda g: (0, 0, 0)),
            block,
        ]
        + [any_space] * 8,
        out_specs=block,
        scratch_shapes=[VMEM((65, 256, 256), BF16), pltpu.SemaphoreType.DMA((8,))],
        compiler_params=params(),
        cost_estimate=cost(464, 24 << 20),
        name="leaf_level",
    )(at, couplings, grouped(t_one), grouped(basis), down_one, grouped(near), *sources)


def listed(lists, ids):
    return jnp.any(lists[:, None, :] == ids[:, :, None], axis=-1)


def window_ids(rows, cols, reach, grid_rows, grid_cols):
    step = np.arange(reach * reach)
    r = rows[:, None] + jnp.asarray(step // reach, jnp.int32)[None]
    c = cols[:, None] + jnp.asarray(step % reach, jnp.int32)[None]
    inside = (r >= 0) & (r < grid_rows) & (c >= 0) & (c < grid_cols)
    return jnp.where(inside, r * grid_cols + c, -2)


def per_device(
    positions,
    samples,
    leaf_basis,
    transfer_one,
    transfer_two,
    couplings,
    near_lists,
    far_zero,
    far_one,
    far_two,
):
    nx = lax.axis_size("qx")
    ny = lax.axis_size("qy")
    i = lax.axis_index("qx")
    j = lax.axis_index("qy")
    a = i % 2
    b = j % 2
    down_x = [(k, k + 1) for k in range(nx - 1)]
    up_x = [(k + 1, k) for k in range(nx - 1)]
    down_y = [(k, k + 1) for k in range(ny - 1)]
    up_y = [(k + 1, k) for k in range(ny - 1)]

    s_left = lax.ppermute(samples[:, 3], "qy", down_y)
    s_right = lax.ppermute(samples[:, 0], "qy", up_y)

    top, bottom, left, right, upper, own_one = coefficients(
        samples, leaf_basis, transfer_one, transfer_two
    )

    pair = lax.ppermute(upper, "qy", [(k, k ^ 1) for k in range(ny)])
    z_left = lax.ppermute(right, "qy", down_y)
    z_right = lax.ppermute(left, "qy", up_y)
    z_above = lax.ppermute(bottom, "qx", down_x)
    z_below = lax.ppermute(top, "qx", up_x)
    s_above = lax.ppermute(
        jnp.concatenate([s_left[3:], samples[3], s_right[3:]]), "qx", down_x
    )
    s_below = lax.ppermute(
        jnp.concatenate([s_left[:1], samples[0], s_right[:1]]), "qx", up_x
    )
    cell_pair = jnp.concatenate([upper[4:], pair[4:]])
    if nx == 4:
        others = [lax.ppermute(cell_pair, "qx", [(k, k ^ 2) for k in range(nx)])]
    else:
        others = [
            lax.ppermute(cell_pair, "qx", [(k, k + 2) for k in range(nx - 2)]),
            lax.ppermute(cell_pair, "qx", [(k + 2, k) for k in range(nx - 2)]),
        ]
    quad = jnp.concatenate([cell_pair] + others)
    outward = [(k, k + 2) for k in range(0, ny - 2, 2)] + [(k + 2, k) for k in range(1, ny - 2, 2)]
    inward = [(k + 2, k) for k in range(0, ny - 2, 2)] + [(k, k + 2) for k in range(1, ny - 2, 2)]
    along = lax.ppermute(jnp.concatenate([pair[:4], quad]), "qy", outward)
    quad_back = lax.ppermute(quad, "qy", inward)
    one_row = jnp.concatenate([own_one, pair[:4], along[:4]])
    two_row = jnp.concatenate([quad, along[4:], quad_back])
    swap_x = [(k, k ^ 1) for k in range(nx)]
    cross_x = [(k, k + 1) for k in range(1, nx - 1, 2)] + [(k + 1, k) for k in range(1, nx - 1, 2)]
    one_e = lax.ppermute(one_row, "qx", swap_x)
    one_d = lax.ppermute(one_row, "qx", cross_x)
    two_e = lax.ppermute(two_row, "qx", swap_x)
    z_corner_above = lax.ppermute(jnp.concatenate([z_left[4:], z_right[4:]]), "qx", down_x)
    z_corner_below = lax.ppermute(jnp.concatenate([z_left[:4], z_right[:4]]), "qx", up_x)

    rows0 = np.arange(16) // 4
    cols0 = np.arange(16) % 4
    base_r = 4 * i + jnp.asarray(rows0, jnp.int32)
    base_c = 4 * j + jnp.asarray(cols0, jnp.int32)
    near_ids = window_ids(base_r - 1, base_c - 1, 3, 4 * nx, 4 * ny)
    weight = jnp.where(listed(near_lists.reshape(16, -1), near_ids), F32(256 ** -0.5), F32(0.0))
    zero_ids = window_ids(base_r // 2 * 2 - 2, base_c // 2 * 2 - 2, 6, 4 * nx, 4 * ny)
    place0 = np.array(
        [
            [held_place(r // 2 * 2 + w // 6, c // 2 * 2 + w % 6) for w in range(36)]
            for r, c in zip(rows0, cols0)
        ],
        np.int32,
    )
    at_zero = jnp.where(listed(far_zero.reshape(16, -1), zero_ids), place0, HELD_ZERO)

    w = np.arange(36)
    wr, wc = w // 6, w % 6
    n_one = 12
    first = jnp.full((4,), 1, jnp.int32)
    one_ids = window_ids(first * (2 * i - 2), first * (2 * j - 2), 6, 2 * nx, 2 * ny)
    row_at = jnp.where(
        wr // 2 == 1, 0, jnp.where((wr // 2 == 2) == (a == 0), n_one, 2 * n_one)
    )
    col_at = jnp.where(wc // 2 == 1, 0, jnp.where((wc // 2 == 2) == (b == 0), 4, 8))
    place1 = row_at + col_at + (wr % 2) * 2 + wc % 2
    at_one = jnp.where(listed(far_one.reshape(4, -1), one_ids), place1[None], 3 * n_one)

    n_quad = quad.shape[0]
    n_two = 3 * n_quad
    two_ids = window_ids(
        first[:1] * (i // 2 * 2 - 2), first[:1] * (j // 2 * 2 - 2), 6, nx, ny
    )
    core_at = jnp.where(wr % 2 == a, 0, n_two)
    z_at = jnp.where(wc // 2 == 1, 0, jnp.where((wc // 2 == 0) == (b == 0), n_quad, 2 * n_quad))
    if nx == 4:
        y_at = np.where(wr // 2 == 1, 0, 2)
    else:
        y_at = np.where(wr // 2 == 1, 0, np.where(wr // 2 == 0, 2, 4))
    x_at = jnp.where(wc % 2 == b, 0, 1)
    place2 = core_at + z_at + y_at + x_at
    at_two = jnp.where(listed(far_two.reshape(1, -1), two_ids), place2[None], 2 * n_two)

    corner = jnp.stack([4 * i, 4 * j]).astype(jnp.int32)
    parity = jnp.stack([a, b]).astype(jnp.int32)
    near = near_field(
        4 * nx,
        4 * ny,
        corner,
        weight,
        positions.reshape(-1, 2, 256),
        samples,
        s_left,
        s_right,
        s_above,
        s_below,
    )
    down_one = upper_levels(
        parity, at_one, at_two, couplings, transfer_two, one_row, one_e, one_d, two_row, two_e
    )
    result = leaf_level(
        at_zero,
        couplings,
        transfer_one,
        leaf_basis,
        down_one,
        near,
        (top, bottom, z_left, z_right, z_above, z_below, z_corner_above, z_corner_below),
    )
    return result.reshape(4, 4, 256, 256)


def solution(mesh):
    return jax.shard_map(
        per_device,
        mesh=mesh,
        in_specs=(
            P(),
            P("qx", "qy", None, None),
            P("qx", "qy", None, None),
            P("qx", "qy", None, None),
            P("qx", "qy", None, None),
            P(),
            P("qx", "qy", None),
            P("qx", "qy", None),
            P("qx", "qy", None),
            P("qx", "qy", None),
        ),
        out_specs=P("qx", "qy", None, None),
        check_vma=False,
    )
```

time: 1060 us -> 190 us (0.18)
  local copies, waits for them, and re-layouts: 611 us -> 7.27 us
  matrix products: 165 us -> 0 us
  waiting for transfers between devices: 144 us -> 59.2 us
  Pallas kernels: 0 us -> 67.9 us
  starting transfers between devices: 97.4 us -> 47.3 us
  other arithmetic: 29.5 us -> 6.6 us
    gather x59 -> x0, local copies, waits for them, and re-layouts: 288 us -> none  [the longest x21 121 us: one_cell(): flattened[places]]
    dot_general x42 -> x0, matrix products: 165 us -> none  [the longest x21 105 us: one_cell(): jnp.einsum('jrs,jsc->rc', matrices, flattened[places], preferred_element_...]
    unnamed x164 -> x66, local copies, waits for them, and re-layouts: 148 us -> 2.5 us
    another operation x68 -> x0, local copies, waits for them, and re-layouts: 116 us -> none  [the longest x65 104 us: coupling_table(): return jnp.stack(pieces)]
    ppermute x24 -> x17, waiting for transfers between devices: 144 us -> 59.2 us  [the longest x1 35.7 us: per_device(): pair = lax.ppermute(upper, 'qy', [(k, k ^ 1) for k in range(ny)])]
    pallas_call x0 -> x4, Pallas kernels: none -> 67.9 us  [the longest x1 25.7 us: near_field(): pl.pallas_call(functools.partial(near_kernel, grid_rows, grid_cols), out_...]
    ppermute x24 -> x17, starting transfers between devices: 97.4 us -> 47.3 us  [the longest x1 8.31 us: per_device(): one_d = lax.ppermute(one_row, 'qx', cross_x)]
    broadcast_in_dim x36 -> x0, local copies, waits for them, and re-layouts: 21.3 us -> none  [the longest x20 10.8 us: one_cell(): jnp.where(allowed[:, None, None], couple_table[kind_here], jnp.zeros((),...]
  transfers between devices with their start and end apart: 24 -> 17, of which waited for: 5 -> 4; matrix products, arithmetic and copies ran while one was open for 48% -> 7% of each run, Pallas kernels for 0% -> 20%
where the time goes in v1:
time: 190 us; the launch traced here: 189 us
  Pallas kernels  67.9 us (36%)
  waiting for transfers between devices  59.2 us (31%)
  starting transfers between devices  47.3 us (25%)
  local copies, waits for them, and re-layouts  7.27 us (4%)
  other arithmetic  6.6 us (3%)
    ppermute x1, waiting for transfers between devices, per_device(): pair = lax.ppermute(upper, 'qy', [(k, k ^ 1) for k in range(ny)])  35.7 us
    pallas_call x1, Pallas kernels, near_field(): pl.pallas_call(functools.partial(near_kernel, grid_rows, grid_cols), out_...  25.7 us
    pallas_call x1, Pallas kernels, leaf_level(): pl.pallas_call(leaf_kernel, grid=(4,), out_shape=jax.ShapeDtypeStruct((2,...  24.3 us
    ppermute x1, waiting for transfers between devices, per_device(): along = lax.ppermute(jnp.concatenate([pair[:4], quad]), 'qy', outward)  15.6 us
    pallas_call x1, Pallas kernels, upper_levels(): pl.pallas_call(upper_kernel, grid=(1,), out_shape=jax.ShapeDtypeStruct((4...  12 us
    ppermute x1, starting transfers between devices, per_device(): one_d = lax.ppermute(one_row, 'qx', cross_x)  8.31 us
    pallas_call x1, Pallas kernels, coefficients(): pl.pallas_call(coef_kernel, out_shape=(tile(8), tile(8), tile(8), tile(8)...  6 us
    ppermute x1, waiting for transfers between devices, per_device(): z_right = lax.ppermute(left, 'qy', up_y)  5.5 us
  transfers between devices with their start and end apart: 17, of which 4 were waited for; matrix products, arithmetic and copies ran while one was open for 7% of the time, Pallas kernels for 20%

profile of v1, /device:TPU:17, one launch (start us, length us, event | category | flops | bytes accessed | tf_op | source)
XLA Modules:
  0.0 189.2 jit_solution(2625890570158759422)
XLA Ops:
  0.0 6.0 %coefficients.1 = (bf16[8,256,256]{2,1,0:T(8,128)(2,1)}, bf16[8,256,256]{2,1,0:T(8,128)(2,1)}, bf16[8,256,256]{2,1,0:T(8,128)(2,1)}, bf16[8,256,256]{2,1,0:T(8,1...) custom-call(bf16[4,4,256,256]{3,2,1,0:T(8,128)(2,1)} %own.1, bf16[4,4,256,256]{3,2,1,0:T(8,128)(2,1)} %basis.1, ...), custom_call_target="tpu_custom_call" | custom-call | flops 1207959552 | bytes 12582912 | tf_op jit(solution)/shard_map/coefficients/pallas_call | solution.py:101
  8.4 2.2 %collective-permute-start.7 = (bf16[4,256,256]{2,1,0:T(8,128)(2,1)}, bf16[4,256,256]{2,1,0:T(8,128)(2,1)}, u32[]{:S(2)}, u32[]{:S(2)}) collective-permute-start(bf16[4,256,256]{2,1,0:T(8,128)(2,1)} %get-tuple-element.20), channel_id=1, source_target_pairs={{0,1},{1,2},{2,3},{3,4},{4,5},{5,6},{6,7},{8,9},{9,10},{10,11},{11... | collective-permute-start | bytes 1572872 | tf_op jit(solution)/shard_map/ppermute | solution.py:432
  10.6 4.0 %collective-permute-start.8 = (bf16[4,256,256]{2,1,0:T(8,128)(2,1)}, bf16[4,256,256]{2,1,0:T(8,128)(2,1)}, u32[]{:S(2)}, u32[]{:S(2)}) collective-permute-start(bf16[4,256,256]{2,1,0:T(8,128)(2,1)} %get-tuple-element.19), channel_id=1, source_target_pairs={{1,0},{2,1},{3,2},{4,3},{5,4},{6,5},{7,6},{9,8},{10,9},{11,10},{12... | collective-permute-start | bytes 1572872 | tf_op jit(solution)/shard_map/ppermute | solution.py:433
  14.6 2.0 %collective-permute-start.11 = (bf16[8,256,256]{2,1,0:T(8,128)(2,1)}, bf16[8,256,256]{2,1,0:T(8,128)(2,1)}, u32[]{:S(2)}, u32[]{:S(2)}) collective-permute-start(bf16[8,256,256]{2,1,0:T(8,128)(2,1)} %get-tuple-element.15), channel_id=1, source_target_pairs={{0,1},{1,2},{2,3},{3,4},{4,5},{5,6},{6,7},{8,9},{9,10},{10,11},{11... | collective-permute-start | bytes 3145736 | tf_op jit(solution)/shard_map/ppermute | solution.py:440
  18.4 1.6 constant_dynamic-update-slice_fusion.3
  20.0 35.7 %collective-permute-done = bf16[5,256,256]{2,1,0:T(8,128)(2,1)S(1)} collective-permute-done((bf16[5,256,256]{2,1,0:T(8,128)(2,1)}, bf16[5,256,256]{2,1,0:T(8,128)(2,1)S(1)}, u32[]{:S(2)}, u32[]{:S(2)}) %collective-permute-start) | collective-permute-done | bytes 655392 | tf_op jit(solution)/shard_map/ppermute | solution.py:439
  56.4 1.3 collective-permute-start.1
  59.7 2.4 %collective-permute-done.1 = bf16[2,256,256]{2,1,0:T(8,128)(2,1)S(1)} collective-permute-done((bf16[2,256,256]{2,1,0:T(8,128)(2,1)S(1)}, bf16[2,256,256]{2,1,0:T(8,128)(2,1)S(1)}, u32[]{:S(2)}, u32[]{:S(2)}) %collective-permute-start.1) | collective-permute-done | bytes 262176 | tf_op jit(solution)/shard_map/ppermute | solution.py:452
  62.2 3.2 %collective-permute-start.2 = (bf16[8,256,256]{2,1,0:T(8,128)(2,1)S(1)}, bf16[8,256,256]{2,1,0:T(8,128)(2,1)S(1)}, u32[]{:S(2)}, u32[]{:S(2)}) collective-permute-start(bf16[8,256,256]{2,1,0:T(8,128)(2,1)S(1)} %pad_maximum_fusion.1), channel_id=1, source_target_pairs={{0,2},{2,4},{4,6},{3,1},{5,3},{7,5},{8,10},{10,12},{12,14},{11,9},... | collective-permute-start | bytes 3145736 | tf_op jit(solution)/shard_map/ppermute | solution.py:461
  66.2 2.2 %collective-permute-start.5 = (bf16[4,256,256]{2,1,0:T(8,128)(2,1)S(1)}, bf16[4,256,256]{2,1,0:T(8,128)(2,1)S(1)}, u32[]{:S(2)}, u32[]{:S(2)}) collective-permute-start(bf16[4,256,256]{2,1,0:T(8,128)(2,1)S(1)} %pad_maximum_fusion.6), channel_id=1, source_target_pairs={{2,0},{4,2},{6,4},{1,3},{3,5},{5,7},{10,8},{12,10},{14,12},{9,11},... | collective-permute-start | bytes 1572872 | tf_op jit(solution)/shard_map/ppermute | solution.py:462
  69.7 15.6 %collective-permute-done.2 = bf16[8,256,256]{2,1,0:T(8,128)(2,1)S(1)} collective-permute-done((bf16[8,256,256]{2,1,0:T(8,128)(2,1)S(1)}, bf16[8,256,256]{2,1,0:T(8,128)(2,1)S(1)}, u32[]{:S(2)}, u32[]{:S(2)}) %collective-permute-start.2) | collective-permute-done | bytes 1048608 | tf_op jit(solution)/shard_map/ppermute | solution.py:461
  85.3 2.0 %collective-permute-start.12 = (bf16[8,256,256]{2,1,0:T(8,128)(2,1)S(1)}, bf16[8,256,256]{2,1,0:T(8,128)(2,1)S(1)}, u32[]{:S(2)}, u32[]{:S(2)}) collective-permute-start(bf16[8,256,256]{2,1,0:T(8,128)(2,1)S(1)} %copy-done.28), channel_id=1, source_target_pairs={{1,0},{2,1},{3,2},{4,3},{5,4},{6,5},{7,6},{9,8},{10,9},{11,10},{12... | collective-permute-start | bytes 3145736 | tf_op jit(solution)/shard_map/ppermute | solution.py:441
  87.5 4.4 %collective-permute-start.6 = (bf16[12,256,256]{2,1,0:T(8,128)(2,1)S(1)}, bf16[12,256,256]{2,1,0:T(8,128)(2,1)S(1)}, u32[]{:S(2)}, u32[]{:S(2)}) collective-permute-start(bf16[12,256,256]{2,1,0:T(8,128)(2,1)S(1)} %constant_dynamic-update-slice_fusion.cells), channel_id=1, source_target_pairs={{0,8},{8,0},{16,24},{24,16},{1,9},{9,1},{17,25},{25,17},{2,10},{10... | collective-permute-start | bytes 4718600 | tf_op jit(solution)/shard_map/ppermute | solution.py:469
  95.2 2.3 %collective-permute-start.10 = (bf16[6,256,256]{2,1,0:T(8,128)(2,1)S(1)}, bf16[6,256,256]{2,1,0:T(8,128)(2,1)S(1)}, u32[]{:S(2)}, u32[]{:S(2)}) collective-permute-start(bf16[6,256,256]{2,1,0:T(8,128)(2,1)S(1)} %pad_maximum_fusion.5), channel_id=1, source_target_pairs={{8,0},{16,8},{24,16},{9,1},{17,9},{25,17},{10,2},{18,10},{26,18},{... | collective-permute-start | bytes 2359304 | tf_op jit(solution)/shard_map/ppermute | solution.py:447
  97.6 3.3 %collective-permute-start.9 = (bf16[6,256,256]{2,1,0:T(8,128)(2,1)S(1)}, bf16[6,256,256]{2,1,0:T(8,128)(2,1)S(1)}, u32[]{:S(2)}, u32[]{:S(2)}) collective-permute-start(bf16[6,256,256]{2,1,0:T(8,128)(2,1)S(1)} %pad_maximum_fusion.4), channel_id=1, source_target_pairs={{0,8},{8,16},{16,24},{1,9},{9,17},{17,25},{2,10},{10,18},{18,26},{... | collective-permute-start | bytes 2359304 | tf_op jit(solution)/shard_map/ppermute | solution.py:444
  102.1 5.5 %collective-permute-done.12.rest_3_ = bf16[8,256,256]{2,1,0:T(8,128)(2,1)S(1)} collective-permute-done((bf16[8,256,256]{2,1,0:T(8,128)(2,1)S(1)}, bf16[8,256,256]{2,1,0:T(8,128)(2,1)S(1)}, u32[]{:S(2)}, u32[]{:S(2)}) %collective-permute-start.12) | collective-permute-done | bytes 1048608 | tf_op jit(solution)/shard_map/ppermute | solution.py:441
  107.6 8.3 %collective-permute-start.4 = (bf16[12,256,256]{2,1,0:T(8,128)(2,1)S(1)}, bf16[12,256,256]{2,1,0:T(8,128)(2,1)}, u32[]{:S(2)}, u32[]{:S(2)}) collective-permute-start(bf16[12,256,256]{2,1,0:T(8,128)(2,1)S(1)} %pad_maximum_fusion.row), channel_id=1, source_target_pairs={{8,16},{16,8},{9,17},{17,9},{10,18},{18,10},{11,19},{19,11},{12,20... | collective-permute-start | bytes 4718600 | tf_op jit(solution)/shard_map/ppermute | solution.py:468
  116.3 1.9 %collective-permute-start.13 = (bf16[8,256,256]{2,1,0:T(8,128)(2,1)}, bf16[8,256,256]{2,1,0:T(8,128)(2,1)}, u32[]{:S(2)}, u32[]{:S(2)}) collective-permute-start(bf16[8,256,256]{2,1,0:T(8,128)(2,1)} %get-tuple-element.14.rest_1_), channel_id=1, source_target_pairs={{0,8},{8,16},{16,24},{1,9},{9,17},{17,25},{2,10},{10,18},{18,26},{... | collective-permute-start | bytes 3145736 | tf_op jit(solution)/shard_map/ppermute | solution.py:442
  118.2 3.4 %collective-permute-start.14 = (bf16[8,256,256]{2,1,0:T(8,128)(2,1)}, bf16[8,256,256]{2,1,0:T(8,128)(2,1)}, u32[]{:S(2)}, u32[]{:S(2)}) collective-permute-start(bf16[8,256,256]{2,1,0:T(8,128)(2,1)} %get-tuple-element.13.rest_0_), channel_id=1, source_target_pairs={{8,0},{16,8},{24,16},{9,1},{17,9},{25,17},{10,2},{18,10},{26,18},{... | collective-permute-start | bytes 3145736 | tf_op jit(solution)/shard_map/ppermute | solution.py:443
  121.6 2.2 %collective-permute-start.15 = (bf16[8,256,256]{2,1,0:T(8,128)(2,1)S(1)}, bf16[8,256,256]{2,1,0:T(8,128)(2,1)}, u32[]{:S(2)}, u32[]{:S(2)}) collective-permute-start(bf16[8,256,256]{2,1,0:T(8,128)(2,1)S(1)} %pad_maximum_fusion.2), channel_id=1, source_target_pairs={{0,8},{8,16},{16,24},{1,9},{9,17},{17,25},{2,10},{10,18},{18,26},{... | collective-permute-start | bytes 3145736 | tf_op jit(solution)/shard_map/ppermute | solution.py:470
  123.8 3.1 %collective-permute-start.16 = (bf16[8,256,256]{2,1,0:T(8,128)(2,1)S(1)}, bf16[8,256,256]{2,1,0:T(8,128)(2,1)}, u32[]{:S(2)}, u32[]{:S(2)}) collective-permute-start(bf16[8,256,256]{2,1,0:T(8,128)(2,1)S(1)} %pad_maximum_fusion.3), channel_id=1, source_target_pairs={{8,0},{16,8},{24,16},{9,1},{17,9},{25,17},{10,2},{18,10},{26,18},{... | collective-permute-start | bytes 3145736 | tf_op jit(solution)/shard_map/ppermute | solution.py:471
  127.0 25.7 %near_field.1 = f32[16,256,256]{2,1,0:T(8,128)} custom-call(s32[2]{0:T(128)} %pad_add_fusion.1.corner, f32[16,9]{1,0:T(8,128)} %broadcast_select_fusion.weight, f32[512,2,256]{2,1,0:T(2,128)} %bitcast.32, bf16[4,4,256,256]{3,2,1,0:T(8,128)(2,1)} %own.1, bf16[4,256,256]{2,1,0:T(8,128)(2,1)} %collective-permute-done.7.left, ...), custom_call_target="tpu_custom_call" | custom-call | flops 13421772800 | bytes 12582912 | tf_op jit(solution)/shard_map/near_field/pallas_call | solution.py:208
  152.7 12.0 %upper_levels.1.down_one = bf16[4,256,256]{2,1,0:T(8,128)(2,1)} custom-call(s32[2]{0:T(128)} %pad_add_fusion.parity, s32[4,36]{1,0:T(4,128)} %broadcast_select_fusion.2.at_one, s32[1,36]{1,0:T(1,128)} %get-tuple-element.41.at_two, bf16[3,20,256,256]{3,2,1,0:T(8,128)(2,1)} %couplings.3, bf16[2,2,256,256]{3,2,1,0:T(8,128)(2,1)} %t_two.3, ...), custom_call_target="tpu_custom_call" | custom-call | flops 4697620480 | bytes 14680064 | tf_op jit(solution)/shard_map/upper_levels/pallas_call | solution.py:295
  164.7 24.3 %leaf_level.1 = bf16[2,2,2,2,256,256]{5,4,3,2,1,0:T(8,128)(2,1)} custom-call(s32[16,36]{1,0:T(8,128)} %broadcast_select_fusion.1.at, bf16[3,20,256,256]{3,2,1,0:T(8,128)(2,1)} %couplings.3, bf16[2,2,2,2,256,256]{5,4,3,2,1,0:T(8,128)(2,1)} %bitcast.27, bf16[2,2,2,2,256,256]{5,4,3,2,1,0:T(8,128)(2,1)} %bitcast.28, bf16[4,256,256]{2,1,0:T(8,128)(2,1)} %upper_levels.1.down_one, ...), custom_call_target="tpu_custom_call" | custom-call | flops 15569256448 | bytes 25165824 | tf_op jit(solution)/shard_map/leaf_level/pallas_call | solution.py:376
  (115 shorter events, 13.7 us)
Async XLA Ops:
  6.1 11.3 %copy-start.6 = (s32[4,4,27]{2,1,0:T(4,128)S(1)}, s32[4,4,27]{2,1,0:T(4,128)}, u32[]{:S(2)}) copy-start(s32[4,4,27]{2,1,0:T(4,128)} %param.39) | copy-start | bytes 5188
  6.1 11.4 %copy-start.9 = (s32[36]{0:T(128)S(1)}, s32[36]{0:T(128)}, u32[]{:S(2)}) copy-start(s32[36]{0:T(128)} %constant.141.clone) | copy-start | bytes 436
  6.1 11.4 %copy-start.10 = (s32[36]{0:T(128)S(1)}, s32[36]{0:T(128)}, u32[]{:S(2)}) copy-start(s32[36]{0:T(128)} %constant.142.clone) | copy-start | bytes 436
  6.1 52.9 %copy-start.8 = (s32[16,36]{1,0:T(8,128)S(1)}, s32[16,36]{1,0:T(8,128)}, u32[]{:S(2)}) copy-start(s32[16,36]{1,0:T(8,128)} %constant.143.clone) | copy-start | bytes 6916
  6.1 49.6 %collective-permute-start = (bf16[5,256,256]{2,1,0:T(8,128)(2,1)}, bf16[5,256,256]{2,1,0:T(8,128)(2,1)S(1)}, u32[]{:S(2)}, u32[]{:S(2)}) collective-permute-start(bf16[5,256,256]{2,1,0:T(8,128)(2,1)} %get-tuple-element.12), channel_id=1, source_target_pairs={{0,1},{1,0},{2,3},{3,2},{4,5},{5,4},{6,7},{7,6},{8,9},{9,8},{10,11... | collective-permute-start | bytes 1966088 | tf_op jit(solution)/shard_map/ppermute | solution.py:439
  8.4 83.7 %collective-permute-start.7 = (bf16[4,256,256]{2,1,0:T(8,128)(2,1)}, bf16[4,256,256]{2,1,0:T(8,128)(2,1)}, u32[]{:S(2)}, u32[]{:S(2)}) collective-permute-start(bf16[4,256,256]{2,1,0:T(8,128)(2,1)} %get-tuple-element.20), channel_id=1, source_target_pairs={{0,1},{1,2},{2,3},{3,4},{4,5},{5,6},{6,7},{8,9},{9,10},{10,11},{11... | collective-permute-start | bytes 1572872 | tf_op jit(solution)/shard_map/ppermute | solution.py:432
  10.6 83.5 %collective-permute-start.8 = (bf16[4,256,256]{2,1,0:T(8,128)(2,1)}, bf16[4,256,256]{2,1,0:T(8,128)(2,1)}, u32[]{:S(2)}, u32[]{:S(2)}) collective-permute-start(bf16[4,256,256]{2,1,0:T(8,128)(2,1)} %get-tuple-element.19), channel_id=1, source_target_pairs={{1,0},{2,1},{3,2},{4,3},{5,4},{6,5},{7,6},{9,8},{10,9},{11,10},{12... | collective-permute-start | bytes 1572872 | tf_op jit(solution)/shard_map/ppermute | solution.py:433
  14.6 83.0 %collective-permute-start.11 = (bf16[8,256,256]{2,1,0:T(8,128)(2,1)}, bf16[8,256,256]{2,1,0:T(8,128)(2,1)}, u32[]{:S(2)}, u32[]{:S(2)}) collective-permute-start(bf16[8,256,256]{2,1,0:T(8,128)(2,1)} %get-tuple-element.15), channel_id=1, source_target_pairs={{0,1},{1,2},{2,3},{3,4},{4,5},{5,6},{6,7},{8,9},{9,10},{10,11},{11... | collective-permute-start | bytes 3145736 | tf_op jit(solution)/shard_map/ppermute | solution.py:440
  56.4 5.7 %collective-permute-start.1 = (bf16[2,256,256]{2,1,0:T(8,128)(2,1)S(1)}, bf16[2,256,256]{2,1,0:T(8,128)(2,1)S(1)}, u32[]{:S(2)}, u32[]{:S(2)}) collective-permute-start(bf16[2,256,256]{2,1,0:T(8,128)(2,1)S(1)} %pad_maximum_fusion.7), channel_id=1, source_target_pairs={{0,16},{8,24},{16,0},{24,8},{1,17},{9,25},{17,1},{25,9},{2,18},{10... | collective-permute-start | bytes 786440 | tf_op jit(solution)/shard_map/ppermute | solution.py:452
  62.2 23.1 %collective-permute-start.2 = (bf16[8,256,256]{2,1,0:T(8,128)(2,1)S(1)}, bf16[8,256,256]{2,1,0:T(8,128)(2,1)S(1)}, u32[]{:S(2)}, u32[]{:S(2)}) collective-permute-start(bf16[8,256,256]{2,1,0:T(8,128)(2,1)S(1)} %pad_maximum_fusion.1), channel_id=1, source_target_pairs={{0,2},{2,4},{4,6},{3,1},{5,3},{7,5},{8,10},{10,12},{12,14},{11,9},... | collective-permute-start | bytes 3145736 | tf_op jit(solution)/shard_map/ppermute | solution.py:461
  66.1 19.2 %copy-start.28 = (bf16[8,256,256]{2,1,0:T(8,128)(2,1)S(1)}, bf16[8,256,256]{2,1,0:T(8,128)(2,1)}, u32[]{:S(2)}) copy-start(bf16[8,256,256]{2,1,0:T(8,128)(2,1)} %get-tuple-element.16) | copy-start | bytes 3145732
  66.2 21.2 %collective-permute-start.5 = (bf16[4,256,256]{2,1,0:T(8,128)(2,1)S(1)}, bf16[4,256,256]{2,1,0:T(8,128)(2,1)S(1)}, u32[]{:S(2)}, u32[]{:S(2)}) collective-permute-start(bf16[4,256,256]{2,1,0:T(8,128)(2,1)S(1)} %pad_maximum_fusion.6), channel_id=1, source_target_pairs={{2,0},{4,2},{6,4},{1,3},{3,5},{5,7},{10,8},{12,10},{14,12},{9,11},... | collective-permute-start | bytes 1572872 | tf_op jit(solution)/shard_map/ppermute | solution.py:462
  85.3 22.3 %collective-permute-start.12 = (bf16[8,256,256]{2,1,0:T(8,128)(2,1)S(1)}, bf16[8,256,256]{2,1,0:T(8,128)(2,1)S(1)}, u32[]{:S(2)}, u32[]{:S(2)}) collective-permute-start(bf16[8,256,256]{2,1,0:T(8,128)(2,1)S(1)} %copy-done.28), channel_id=1, source_target_pairs={{1,0},{2,1},{3,2},{4,3},{5,4},{6,5},{7,6},{9,8},{10,9},{11,10},{12... | collective-permute-start | bytes 3145736 | tf_op jit(solution)/shard_map/ppermute | solution.py:441
  87.5 14.6 %copy-start.5 = (bf16[12,256,256]{2,1,0:T(8,128)(2,1)}, bf16[12,256,256]{2,1,0:T(8,128)(2,1)S(1)}, u32[]{:S(2)}) copy-start(bf16[12,256,256]{2,1,0:T(8,128)(2,1)S(1)} %constant_dynamic-update-slice_fusion.cells) | copy-start | bytes 4718596
  87.5 34.1 %collective-permute-start.6 = (bf16[12,256,256]{2,1,0:T(8,128)(2,1)S(1)}, bf16[12,256,256]{2,1,0:T(8,128)(2,1)S(1)}, u32[]{:S(2)}, u32[]{:S(2)}) collective-permute-start(bf16[12,256,256]{2,1,0:T(8,128)(2,1)S(1)} %constant_dynamic-update-slice_fusion.cells), channel_id=1, source_target_pairs={{0,8},{8,0},{16,24},{24,16},{1,9},{9,1},{17,25},{25,17},{2,10},{10... | collective-permute-start | bytes 4718600 | tf_op jit(solution)/shard_map/ppermute | solution.py:469
  92.1 15.5 %copy-start.1 = (bf16[12,256,256]{2,1,0:T(8,128)(2,1)}, bf16[12,256,256]{2,1,0:T(8,128)(2,1)S(1)}, u32[]{:S(2)}) copy-start(bf16[12,256,256]{2,1,0:T(8,128)(2,1)S(1)} %pad_maximum_fusion.row) | copy-start | bytes 4718596
  92.2 31.7 %collective-permute-start.3 = (bf16[12,256,256]{2,1,0:T(8,128)(2,1)S(1)}, bf16[12,256,256]{2,1,0:T(8,128)(2,1)S(1)}, u32[]{:S(2)}, u32[]{:S(2)}) collective-permute-start(bf16[12,256,256]{2,1,0:T(8,128)(2,1)S(1)} %pad_maximum_fusion.row), channel_id=1, source_target_pairs={{0,8},{8,0},{16,24},{24,16},{1,9},{9,1},{17,25},{25,17},{2,10},{10... | collective-permute-start | bytes 4718600 | tf_op jit(solution)/shard_map/ppermute | solution.py:467
  95.2 21.1 %collective-permute-start.10 = (bf16[6,256,256]{2,1,0:T(8,128)(2,1)S(1)}, bf16[6,256,256]{2,1,0:T(8,128)(2,1)S(1)}, u32[]{:S(2)}, u32[]{:S(2)}) collective-permute-start(bf16[6,256,256]{2,1,0:T(8,128)(2,1)S(1)} %pad_maximum_fusion.5), channel_id=1, source_target_pairs={{8,0},{16,8},{24,16},{9,1},{17,9},{25,17},{10,2},{18,10},{26,18},{... | collective-permute-start | bytes 2359304 | tf_op jit(solution)/shard_map/ppermute | solution.py:447
  97.6 20.6 %collective-permute-start.9 = (bf16[6,256,256]{2,1,0:T(8,128)(2,1)S(1)}, bf16[6,256,256]{2,1,0:T(8,128)(2,1)S(1)}, u32[]{:S(2)}, u32[]{:S(2)}) collective-permute-start(bf16[6,256,256]{2,1,0:T(8,128)(2,1)S(1)} %pad_maximum_fusion.4), channel_id=1, source_target_pairs={{0,8},{8,16},{16,24},{1,9},{9,17},{17,25},{2,10},{10,18},{18,26},{... | collective-permute-start | bytes 2359304 | tf_op jit(solution)/shard_map/ppermute | solution.py:444
  107.6 45.1 %collective-permute-start.4 = (bf16[12,256,256]{2,1,0:T(8,128)(2,1)S(1)}, bf16[12,256,256]{2,1,0:T(8,128)(2,1)}, u32[]{:S(2)}, u32[]{:S(2)}) collective-permute-start(bf16[12,256,256]{2,1,0:T(8,128)(2,1)S(1)} %pad_maximum_fusion.row), channel_id=1, source_target_pairs={{8,16},{16,8},{9,17},{17,9},{10,18},{18,10},{11,19},{19,11},{12,20... | collective-permute-start | bytes 4718600 | tf_op jit(solution)/shard_map/ppermute | solution.py:468
  116.3 48.4 %collective-permute-start.13 = (bf16[8,256,256]{2,1,0:T(8,128)(2,1)}, bf16[8,256,256]{2,1,0:T(8,128)(2,1)}, u32[]{:S(2)}, u32[]{:S(2)}) collective-permute-start(bf16[8,256,256]{2,1,0:T(8,128)(2,1)} %get-tuple-element.14.rest_1_), channel_id=1, source_target_pairs={{0,8},{8,16},{16,24},{1,9},{9,17},{17,25},{2,10},{10,18},{18,26},{... | collective-permute-start | bytes 3145736 | tf_op jit(solution)/shard_map/ppermute | solution.py:442
  118.2 46.5 %collective-permute-start.14 = (bf16[8,256,256]{2,1,0:T(8,128)(2,1)}, bf16[8,256,256]{2,1,0:T(8,128)(2,1)}, u32[]{:S(2)}, u32[]{:S(2)}) collective-permute-start(bf16[8,256,256]{2,1,0:T(8,128)(2,1)} %get-tuple-element.13.rest_0_), channel_id=1, source_target_pairs={{8,0},{16,8},{24,16},{9,1},{17,9},{25,17},{10,2},{18,10},{26,18},{... | collective-permute-start | bytes 3145736 | tf_op jit(solution)/shard_map/ppermute | solution.py:443
  121.6 43.1 %collective-permute-start.15 = (bf16[8,256,256]{2,1,0:T(8,128)(2,1)S(1)}, bf16[8,256,256]{2,1,0:T(8,128)(2,1)}, u32[]{:S(2)}, u32[]{:S(2)}) collective-permute-start(bf16[8,256,256]{2,1,0:T(8,128)(2,1)S(1)} %pad_maximum_fusion.2), channel_id=1, source_target_pairs={{0,8},{8,16},{16,24},{1,9},{9,17},{17,25},{2,10},{10,18},{18,26},{... | collective-permute-start | bytes 3145736 | tf_op jit(solution)/shard_map/ppermute | solution.py:470
  123.8 40.9 %collective-permute-start.16 = (bf16[8,256,256]{2,1,0:T(8,128)(2,1)S(1)}, bf16[8,256,256]{2,1,0:T(8,128)(2,1)}, u32[]{:S(2)}, u32[]{:S(2)}) collective-permute-start(bf16[8,256,256]{2,1,0:T(8,128)(2,1)S(1)} %pad_maximum_fusion.3), channel_id=1, source_target_pairs={{8,0},{16,8},{24,16},{9,1},{17,9},{25,17},{10,2},{18,10},{26,18},{... | collective-permute-start | bytes 3145736 | tf_op jit(solution)/shard_map/ppermute | solution.py:471
  (24 other events, 178.0 us)

commit v2 on v0

v2 whole, which is shorter than its diff:
```python
import functools

import jax
import jax.numpy as jnp
import numpy as np
from jax import lax
from jax.experimental import pallas as pl
from jax.experimental.pallas import tpu as pltpu
from jax.sharding import PartitionSpec as P

root_three = 1.7320508075688772
length_scale = 1.0
VMEM = pltpu.VMEM
SMEM = pltpu.SMEM
F32 = jnp.float32
BF16 = jnp.bfloat16
BIG = 60 * 1024 * 1024


def nn(a, b):
    return lax.dot_general(a, b, (((1,), (0,)), ((), ())), preferred_element_type=F32)


def nt(a, b):
    return lax.dot_general(a, b, (((1,), (1,)), ((), ())), preferred_element_type=F32)


def tn(a, b):
    return lax.dot_general(a, b, (((0,), (0,)), ((), ())), preferred_element_type=F32)


def params():
    return pltpu.CompilerParams(vmem_limit_bytes=BIG)


def cost(products, bytes_accessed):
    return pl.CostEstimate(
        flops=products * 2 * 256**3, bytes_accessed=bytes_accessed, transcendentals=0
    )


def half_offsets():
    kept = []
    for u in range(-3, 4):
        for v in range(-3, 4):
            if max(abs(u), abs(v)) >= 2 and (u > 0 or (u == 0 and v > 0)):
                kept.append((u, v))
    return kept


HALF_OFFSETS = half_offsets()


def class_plan(a, b):
    plain, turned = [], []
    for w in range(36):
        u, v = w // 6 - 2 - a, w % 6 - 2 - b
        if max(abs(u), abs(v)) < 2:
            continue
        if (u, v) in HALF_OFFSETS:
            plain.append((w, HALF_OFFSETS.index((u, v))))
        else:
            turned.append((w, HALF_OFFSETS.index((-u, -v))))
    return plain, turned


LOG2E = 1.4426950408889634


def tiles(n, dtype=BF16):
    return jax.ShapeDtypeStruct((n, 256, 256), dtype)


ANY_SPEC = pl.BlockSpec(memory_space=pl.ANY)
SMEM_SPEC = pl.BlockSpec(memory_space=SMEM)
VMEM_SPEC = pl.BlockSpec(memory_space=VMEM)


class Copies:
    def __init__(self, sems):
        self.sems = sems
        self.started = []

    def start(self, src, dst):
        copy = pltpu.make_async_copy(src, dst, self.sems.at[len(self.started)])
        copy.start()
        self.started.append(copy)
        return copy

    def wait(self):
        for copy in self.started:
            copy.wait()


def coef_kernel(
    samples, basis, t_one, t_two, up, down, left, right, upper,
    sv, bv, t1v, t2v, cv, uv, in_sems, out_sems,
):
    into = Copies(in_sems)
    out = Copies(out_sems)
    rows = []
    for x in range(4):
        rows.append(
            (
                into.start(samples.at[x], sv.at[x]),
                into.start(basis.at[x], bv.at[x]),
                into.start(t_one.at[x], t1v.at[x]),
            )
        )
    last = into.start(t_two, t2v)
    for x in range(4):
        rows[x][0].wait()
        rows[x][1].wait()
        for y in range(4):
            cv[x * 4 + y] = tn(sv[x, y], bv[x, y]).astype(BF16)
        own = cv.at[4 * x : 4 * x + 4]
        out.start(own, (up if x < 2 else down).at[4 * (x % 2) : 4 * (x % 2) + 4])
        out.start(cv.at[4 * x : 4 * x + 2], left.at[2 * x : 2 * x + 2])
        out.start(cv.at[4 * x + 2 : 4 * x + 4], right.at[2 * x : 2 * x + 2])
        out.start(sv.at[x, 0], left.at[8 + x])
        out.start(sv.at[x, 3], right.at[8 + x])
        if x == 0:
            out.start(sv.at[x], up.at[8:12])
        if x == 3:
            out.start(sv.at[x], down.at[8:12])
        if x % 2 == 1:
            rows[x - 1][2].wait()
            rows[x][2].wait()
            for y in range(2):
                kids = [(x - 1 + a, 2 * y + b) for a in range(2) for b in range(2)]
                lhs = jnp.concatenate([cv[k * 4 + m] for k, m in kids], axis=1)
                rhs = jnp.concatenate([t1v[k] for k in kids], axis=0)
                uv[x // 2 * 2 + y] = nn(lhs, rhs).astype(BF16)
    last.wait()
    lhs = jnp.concatenate([uv[k] for k in range(4)], axis=1)
    rhs = jnp.concatenate([t2v[k // 2, k % 2] for k in range(4)], axis=0)
    uv[4] = nn(lhs, rhs).astype(BF16)
    out.start(uv, upper)
    out.wait()


def coefficients(samples, basis, t_one, t_two):
    return pl.pallas_call(
        coef_kernel,
        out_shape=(tiles(12), tiles(12), tiles(12), tiles(12), tiles(5)),
        in_specs=[ANY_SPEC] * 4,
        out_specs=[ANY_SPEC] * 5,
        scratch_shapes=[
            VMEM((4, 4, 256, 256), BF16),
            VMEM((4, 4, 256, 256), BF16),
            VMEM((4, 4, 256, 256), BF16),
            VMEM((2, 2, 256, 256), BF16),
            VMEM((16, 256, 256), BF16),
            VMEM((5, 256, 256), BF16),
            pltpu.SemaphoreType.DMA((13,)),
            pltpu.SemaphoreType.DMA((23,)),
        ],
        compiler_params=params(),
        cost_estimate=cost(170, 12 << 20),
        name="coefficients",
    )(samples, basis, t_one, t_two)


def halo_places():
    numbers = {}
    for r in range(4):
        for c in range(4):
            for k in range(9):
                y, x = r + k // 3 - 1, c + k % 3 - 1
                if not (0 <= y < 4 and 0 <= x < 4):
                    numbers[r * 4 + c, k] = len(numbers)
    return numbers


HALO = halo_places()
N_HALO = len(HALO) // 2


def near_kernel(
    first, grid_rows, grid_cols, lists, positions, own, near, halo_tiles,
    held, plane_x, plane_y, weight, sems,
):
    copy = pltpu.make_async_copy(own, held.at[0:16], sems.at[0])
    copy.start()
    held[16] = jnp.zeros((256, 256), BF16)
    first_row = lax.axis_index("qx") * 4
    first_col = lax.axis_index("qy") * 4
    scale = root_three / length_scale * LOG2E
    weight_full = 256 ** -0.5

    def place_of(row, col):
        r = jnp.clip(row, 0, grid_rows - 1)
        c = jnp.clip(col, 0, grid_cols - 1)
        return r * grid_cols + c

    copy.wait()

    def one_target(t, carry):
        r = t // 4
        c = t % 4
        row = first_row + r
        col = first_col + c
        mid_row = row.astype(F32) + 0.5
        mid_col = col.astype(F32) + 0.5
        for k in range(9):
            weight[k] = 0.0
        for e in range(9):
            entry = lists[r, c, e]
            source_row = jnp.maximum(entry, 0) // grid_cols
            source_col = jnp.maximum(entry, 0) - source_row * grid_cols
            k = (source_row - row + 1) * 3 + source_col - col + 1
            weight[jnp.where(entry >= 0, k, 9)] = weight_full
        here = positions[place_of(row, col)]
        turn_x = jnp.broadcast_to((here[0:1] - mid_row) * scale, (8, 256)).T
        turn_y = jnp.broadcast_to((here[1:2] - mid_col) * scale, (8, 256)).T
        plane_x[...] = jnp.broadcast_to(turn_x[:, 0:1], (256, 128))
        plane_y[...] = jnp.broadcast_to(turn_y[:, 0:1], (256, 128))
        made = []
        blocks = []
        for k in range(9):
            dr, dc = k // 3 - 1, k % 3 - 1
            there = positions[place_of(row + dr, col + dc)]
            x = (there[0:1] - mid_row) * scale
            y = (there[1:2] - mid_col) * scale
            w = weight[k]
            halves = []
            for h in range(2):
                gap_x = plane_x[...] - x[:, 128 * h : 128 * h + 128]
                gap_y = plane_y[...] - y[:, 128 * h : 128 * h + 128]
                square = jnp.maximum(gap_x * gap_x + gap_y * gap_y, 1e-24)
                far = square * lax.rsqrt(square)
                halves.append(((far * (w / LOG2E) + w) * jnp.exp2(-far)).astype(BF16))
            tile = jnp.concatenate(halves, axis=1)
            inside = (r + dr >= 0) & (r + dr < 4) & (c + dc >= 0) & (c + dc < 4)
            halo_tiles[jnp.where(inside, 72, (t - first) * 9 + k)] = tile
            made.append(tile)
            blocks.append(held[jnp.where(inside, (r + dr) * 4 + c + dc, 16)])
        near[t - first] = nn(jnp.concatenate(made, axis=1), jnp.concatenate(blocks, axis=0))
        return carry

    lax.fori_loop(first, first + 8, one_target, 0)


def near_store_kernel(first, grid_rows, grid_cols, lists, positions, own, near, halo_out, *scratch):
    held, plane_x, plane_y, halo, weight, sems, halo_sems = scratch
    near_kernel(
        first, grid_rows, grid_cols, lists, positions, own, near, halo,
        held, plane_x, plane_y, weight, sems,
    )
    out = Copies(halo_sems)
    for (t, k), number in HALO.items():
        if first <= t < first + 8:
            out.start(halo.at[(t - first) * 9 + k], halo_out.at[number % N_HALO])
    out.wait()


def near_own(first, grid_rows, grid_cols, lists, positions, own):
    return pl.pallas_call(
        functools.partial(near_store_kernel, first, grid_rows, grid_cols),
        out_shape=(tiles(8, F32), tiles(N_HALO)),
        in_specs=[SMEM_SPEC, VMEM_SPEC, ANY_SPEC],
        out_specs=[VMEM_SPEC, ANY_SPEC],
        scratch_shapes=[
            VMEM((17, 256, 256), BF16),
            VMEM((256, 128), F32),
            VMEM((256, 128), F32),
            VMEM((73, 256, 256), BF16),
            pltpu.SMEM((10,), F32),
            pltpu.SemaphoreType.DMA((1,)),
            pltpu.SemaphoreType.DMA((N_HALO,)),
        ],
        compiler_params=params(),
        cost_estimate=cost(300, 8 << 20),
        name=f"near_own_{first}",
    )(lists, positions, own)


def mark_listed(entries, flags, n, first_row, first_col, grid_cols):
    for w in range(36):
        flags[n, w] = 0
    for e in range(27):
        entry = entries(e)
        row = jnp.maximum(entry, 0) // grid_cols
        col = jnp.maximum(entry, 0) - row * grid_cols
        w = (row - first_row) * 6 + col - first_col
        flags[n, jnp.where(entry >= 0, jnp.clip(w, 0, 35), 36)] = 1


def dot_group(held, couplings, turned, group):
    rows = len(group[0][1])
    lhs = [
        jnp.concatenate([held[places[n]] for _, places in group], axis=1) for n in range(rows)
    ]
    lhs = jnp.concatenate(lhs, axis=0) if rows > 1 else lhs[0]
    if turned:
        return nn(lhs, jnp.concatenate([couplings[k] for k, _ in group], axis=0))
    return nt(lhs, jnp.concatenate([couplings[k] for k, _ in group], axis=1))


def coupled(plan, couplings, held, places):
    total = None
    for turned in (0, 1):
        group = [(k, [places(w)]) for w, k in plan[turned]]
        part = dot_group(held, couplings, turned, group)
        total = part if total is None else total + part
    return total


def upper_kernel(
    grid_cols, far_one, far_two, couplings, t_two, row, row_e, row_d, cells, cells_e, down,
    held_one, held_two, field_two, flags, sems,
):
    n_one = row.shape[0]
    n_two = cells.shape[0]
    zero_one, zero_two = 3 * n_one, 2 * n_two
    copies = Copies(sems)
    copies.start(cells, held_two.at[0:n_two])
    copies.start(cells_e, held_two.at[n_two : 2 * n_two])
    copies.start(row, held_one.at[0:n_one])
    copies.start(row_e, held_one.at[n_one : 2 * n_one])
    copies.start(row_d, held_one.at[2 * n_one : 3 * n_one])
    held_one[zero_one] = jnp.zeros((256, 256), BF16)
    held_two[zero_two] = jnp.zeros((256, 256), BF16)
    i = lax.axis_index("qx")
    j = lax.axis_index("qy")
    a = i % 2
    b = j % 2
    for t in range(4):
        mark_listed(
            lambda e: far_one[t // 2, t % 2, e], flags, t, 2 * i - 2, 2 * j - 2, 2 * grid_cols
        )
    mark_listed(
        lambda e: far_two[0, 0, e], flags, 4, i // 2 * 2 - 2, j // 2 * 2 - 2, grid_cols
    )
    n_quad = n_two // 3
    core_at = [jnp.where(a == 0, 0, n_two), jnp.where(a == 0, n_two, 0)]
    z_at = [jnp.where(b == 0, n_quad, 2 * n_quad), 0, jnp.where(b == 0, 2 * n_quad, n_quad)]
    y_at = [2, 0, 2] if n_quad == 4 else [2, 0, 4]
    x_at = [b, 1 - b]

    def place_two(w):
        r, c = w // 6, w % 6
        place = core_at[r % 2] + z_at[c // 2] + y_at[r // 2] + x_at[c % 2]
        return jnp.where(flags[4, w] == 1, place, zero_two)

    row_at = [jnp.where(a == 0, 2 * n_one, n_one), 0, jnp.where(a == 0, n_one, 2 * n_one)]
    col_at = [jnp.where(b == 0, 8, 4), 0, jnp.where(b == 0, 4, 8)]

    def place_one(t, w):
        r, c = w // 6, w % 6
        place = row_at[r // 2] + col_at[c // 2] + (r % 2) * 2 + c % 2
        return jnp.where(flags[t, w] == 1, place, zero_one)

    copies.wait()
    for u in range(2):
        for v in range(2):

            @pl.when((a == u) & (b == v))
            def _():
                field_two[...] = coupled(
                    class_plan(u, v), couplings.at[1], held_two, place_two
                ).astype(BF16)

    for u in range(2):
        for v in range(2):
            t = u * 2 + v
            field = coupled(
                class_plan(u, v), couplings.at[0], held_one, functools.partial(place_one, t)
            )
            down[t] = (field + nt(field_two[...], t_two[u, v])).astype(BF16)


def upper_levels(grid_cols, far_one, far_two, couplings, t_two, row, row_e, row_d, cells, cells_e):
    n_one, n_two = row.shape[0], cells.shape[0]
    return pl.pallas_call(
        functools.partial(upper_kernel, grid_cols),
        grid=(1,),
        out_shape=tiles(4),
        in_specs=[
            SMEM_SPEC,
            SMEM_SPEC,
            pl.BlockSpec(
                (pl.Element(2), pl.Element(20), pl.Element(256), pl.Element(256)),
                lambda g: (1, 0, 0, 0),
            ),
            pl.BlockSpec((2, 2, 256, 256), lambda g: (0, 0, 0, 0)),
        ]
        + [ANY_SPEC] * 5,
        out_specs=pl.BlockSpec((4, 256, 256), lambda g: (0, 0, 0)),
        scratch_shapes=[
            VMEM((3 * n_one + 1, 256, 256), BF16),
            VMEM((2 * n_two + 1, 256, 256), BF16),
            VMEM((256, 256), BF16),
            pltpu.SMEM((5, 37), jnp.int32),
            pltpu.SemaphoreType.DMA((5,)),
        ],
        compiler_params=params(),
        cost_estimate=cost(340, 14 << 20),
        name="upper_levels",
    )(far_one, far_two, couplings, t_two, row, row_e, row_d, cells, cells_e)


def source_of(x, y, w):
    r, c = 2 * x + w // 6, 2 * y + w % 6
    rows_in, cols_in = 2 <= r < 6, 2 <= c < 6
    if cols_in:
        return "rows", r * 4 + c - 2
    if rows_in:
        return "sides", (0 if c < 2 else 8) + (r - 2) * 2 + (c if c < 2 else c - 6)
    base = 0 if r < 2 else 8
    return "corners", base + (0 if c < 2 else 4) + (r if r < 2 else r - 6) * 2 + (
        c if c < 2 else c - 6
    )


PARENTS = [(x, y) for x in range(2) for y in range(2)]


def number_of(a, b, parent):
    x, y = parent
    return (2 * x + a) * 4 + 2 * y + b


def level_zero_sums(kind, a, b, flags, couplings, held, zero):
    plan = class_plan(a, b)
    sums = {}
    for turned in (0, 1):
        groups = {}
        for w, k in plan[turned]:
            members = tuple(p for p in PARENTS if source_of(*p, w)[0] == kind)
            if members:
                groups.setdefault(members, []).append((w, k))
        for members, entries in groups.items():
            group = []
            for w, k in entries:
                places = [
                    jnp.where(flags[number_of(a, b, p), w] == 1, source_of(*p, w)[1], zero)
                    for p in members
                ]
                group.append((k, places))
            total = dot_group(held, couplings, turned, group)
            for n, p in enumerate(members):
                part = total[256 * n : 256 * n + 256]
                sums[p] = part if p not in sums else sums[p] + part
    return sums


def grouped(x):
    return x.reshape(2, 2, 2, 2, 256, 256)


CLASS_BLOCK = pl.BlockSpec((2, 1, 2, 1, 256, 256), lambda g: (0, g // 2, 0, g % 2, 0, 0))
COUPLING_BLOCK = pl.BlockSpec((1, 20, 256, 256), lambda g: (0, 0, 0, 0))
GROUPED_F32 = jax.ShapeDtypeStruct((2, 2, 2, 2, 256, 256), F32)


def each_class(step, body):
    for a in range(2):
        for b in range(2):
            pl.when(step == a * 2 + b)(functools.partial(body, a, b))


def rows_kernel(
    grid_cols, far_zero, couplings, up, down, above, below, field, flags, held, sems
):
    step = pl.program_id(0)

    @pl.when(step == 0)
    def _():
        copies = Copies(sems)
        for n, src in enumerate((above, up, down, below)):
            copies.start(src.at[0:8], held.at[8 * n : 8 * n + 8])
        held[32] = jnp.zeros((256, 256), BF16)
        first_row = lax.axis_index("qx") * 4
        first_col = lax.axis_index("qy") * 4

        def mark(t, carry):
            r, c = t // 4, t % 4
            mark_listed(
                lambda e: far_zero[r, c, e],
                flags,
                t,
                first_row + r // 2 * 2 - 2,
                first_col + c // 2 * 2 - 2,
                grid_cols,
            )
            return carry

        lax.fori_loop(0, 16, mark, 0)
        copies.wait()

    def body(a, b):
        sums = level_zero_sums("rows", a, b, flags, couplings.at[0], held, 32)
        for x, y in PARENTS:
            field[x, 0, y, 0] = sums[x, y]

    each_class(step, body)


def rows_level(grid_cols, far_zero, couplings, up, down, above, below):
    return pl.pallas_call(
        functools.partial(rows_kernel, grid_cols),
        grid=(4,),
        out_shape=(GROUPED_F32, jax.ShapeDtypeStruct((16, 37), jnp.int32)),
        in_specs=[SMEM_SPEC, COUPLING_BLOCK] + [ANY_SPEC] * 4,
        out_specs=[CLASS_BLOCK, SMEM_SPEC],
        scratch_shapes=[VMEM((33, 256, 256), BF16), pltpu.SemaphoreType.DMA((4,))],
        compiler_params=params(),
        cost_estimate=cost(420, 11 << 20),
        name="far_rows",
    )(far_zero, couplings, up, down, above, below)


def near_source(r, c):
    rows_in, cols_in = 1 <= r < 5, 1 <= c < 5
    if rows_in and cols_in:
        return "own", None
    if rows_in:
        return "side", (0 if c == 0 else 4) + r - 1
    if cols_in:
        return "side", (8 if r == 0 else 12) + c - 1
    return "corner", (0 if r == 0 else 2) + (0 if c == 0 else 1)


def near_part(kind, t, tile_of, held):
    r, c = t // 4, t % 4
    made, blocks = [], []
    for k in range(9):
        found, place = near_source(r + k // 3, c + k % 3)
        if found == kind:
            made.append(tile_of(HALO[t, k]))
            blocks.append(held[place])
    if not made:
        return None
    return nn(jnp.concatenate(made, axis=1), jnp.concatenate(blocks, axis=0))


SIDE_HALO = [n for (t, k), n in HALO.items() if near_source(t // 4 + k // 3, t % 4 + k % 3)[0] == "side"]
CORNER_HALO = [n for n in range(2 * N_HALO) if n not in SIDE_HALO]


def sides_kernel(
    flags, couplings, field_in, near_a, near_b, halo_a, halo_b, left, right, above, below,
    field, near, held, near_held, halo, sems,
):
    step = pl.program_id(0)

    @pl.when(step == 0)
    def _():
        copies = Copies(sems)
        copies.start(left.at[0:8], held.at[0:8])
        copies.start(right.at[0:8], held.at[8:16])
        for n, src in enumerate((left, right, above, below)):
            copies.start(src.at[8:12], near_held.at[4 * n : 4 * n + 4])
        copies.start(halo_a, halo.at[0:N_HALO])
        copies.start(halo_b, halo.at[N_HALO : 2 * N_HALO])
        held[16] = jnp.zeros((256, 256), BF16)
        copies.wait()

    def body(a, b):
        sums = level_zero_sums("sides", a, b, flags, couplings.at[0], held, 16)
        for x, y in PARENTS:
            field[x, 0, y, 0] = field_in[x, 0, y, 0] + sums[x, y]
            part = near_part("side", number_of(a, b, (x, y)), lambda n: halo[n], near_held)
            here = (near_b if x else near_a)[0, y, 0]
            near[x, 0, y, 0] = here if part is None else here + part

    each_class(step, body)


HALF_BLOCK = pl.BlockSpec((1, 2, 1, 256, 256), lambda g: (g // 2, 0, g % 2, 0, 0))


def sides_level(flags, couplings, field, near_a, near_b, halo_a, halo_b, left, right, above, below):
    half = lambda x: x.reshape(2, 2, 2, 256, 256)
    return pl.pallas_call(
        sides_kernel,
        grid=(4,),
        out_shape=(GROUPED_F32, GROUPED_F32),
        in_specs=[SMEM_SPEC, COUPLING_BLOCK, CLASS_BLOCK, HALF_BLOCK, HALF_BLOCK] + [ANY_SPEC] * 6,
        out_specs=[CLASS_BLOCK, CLASS_BLOCK],
        scratch_shapes=[
            VMEM((17, 256, 256), BF16),
            VMEM((16, 256, 256), BF16),
            VMEM((2 * N_HALO, 256, 256), BF16),
            pltpu.SemaphoreType.DMA((8,)),
        ],
        compiler_params=params(),
        cost_estimate=cost(300, 30 << 20),
        name="far_sides",
    )(
        flags, couplings, field, half(near_a), half(near_b), halo_a, halo_b, left, right, above, below
    )


def last_kernel(
    flags, couplings, t_one, basis, down_one, field, near, halo_a, halo_b, above, below, out,
    held, near_held, halo, sems,
):
    step = pl.program_id(0)

    @pl.when(step == 0)
    def _():
        copies = Copies(sems)
        copies.start(above.at[0:8], held.at[0:8])
        copies.start(below.at[0:8], held.at[8:16])
        copies.start(above.at[8:10], near_held.at[0:2])
        copies.start(below.at[8:10], near_held.at[2:4])
        for m, n in enumerate(CORNER_HALO):
            copies.start((halo_a if n < N_HALO else halo_b).at[n % N_HALO], halo.at[m])
        held[16] = jnp.zeros((256, 256), BF16)
        copies.wait()

    def body(a, b):
        sums = level_zero_sums("corners", a, b, flags, couplings.at[0], held, 16)
        for x, y in PARENTS:
            total = field[x, 0, y, 0] + nt(down_one[x * 2 + y], t_one[x, 0, y, 0])
            if (x, y) in sums:
                total = total + sums[x, y]
            result = near[x, 0, y, 0] + nt(basis[x, 0, y, 0], total.astype(BF16))
            part = near_part(
                "corner",
                number_of(a, b, (x, y)),
                lambda n: halo[CORNER_HALO.index(n)],
                near_held,
            )
            if part is not None:
                result = result + part
            out[x, 0, y, 0] = result.astype(BF16)

    each_class(step, body)


def last_level(
    flags, couplings, t_one, basis, down_one, field, near, halo_a, halo_b, above, below
):
    return pl.pallas_call(
        last_kernel,
        grid=(4,),
        out_shape=jax.ShapeDtypeStruct((2, 2, 2, 2, 256, 256), BF16),
        in_specs=[
            SMEM_SPEC,
            COUPLING_BLOCK,
            CLASS_BLOCK,
            CLASS_BLOCK,
            pl.BlockSpec((4, 256, 256), lambda g: (0, 0, 0)),
            CLASS_BLOCK,
            CLASS_BLOCK,
        ]
        + [ANY_SPEC] * 4,
        out_specs=CLASS_BLOCK,
        scratch_shapes=[
            VMEM((17, 256, 256), BF16),
            VMEM((4, 256, 256), BF16),
            VMEM((len(CORNER_HALO), 256, 256), BF16),
            pltpu.SemaphoreType.DMA((4 + len(CORNER_HALO),)),
        ],
        compiler_params=params(),
        cost_estimate=cost(270, 20 << 20),
        name="last_level",
    )(
        flags, couplings, grouped(t_one), grouped(basis), down_one, field, near, halo_a, halo_b,
        above, below,
    )


def per_device(
    positions,
    samples,
    leaf_basis,
    transfer_one,
    transfer_two,
    couplings,
    near_lists,
    far_zero,
    far_one,
    far_two,
):
    nx = lax.axis_size("qx")
    ny = lax.axis_size("qy")
    down_x = [(k, k + 1) for k in range(nx - 1)]
    up_x = [(k + 1, k) for k in range(nx - 1)]
    down_y = [(k, k + 1) for k in range(ny - 1)]
    up_y = [(k + 1, k) for k in range(ny - 1)]

    up, down, left, right, upper = coefficients(samples, leaf_basis, transfer_one, transfer_two)

    pair = lax.ppermute(upper, "qy", [(k, k ^ 1) for k in range(ny)])
    above = lax.ppermute(down, "qx", down_x)
    below = lax.ppermute(up, "qx", up_x)
    sites = positions.reshape(-1, 2, 256)
    flat_samples = samples.reshape(16, 256, 256)
    near_a, halo_a = near_own(0, 4 * nx, 4 * ny, near_lists, sites, flat_samples)
    pair, above, below, left, right, near_a = lax.optimization_barrier(
        (pair, above, below, left, right, near_a)
    )
    cell_pair = jnp.concatenate([upper[4:], pair[4:]])
    if nx == 4:
        others = [lax.ppermute(cell_pair, "qx", [(k, k ^ 2) for k in range(nx)])]
    else:
        others = [
            lax.ppermute(cell_pair, "qx", [(k, k + 2) for k in range(nx - 2)]),
            lax.ppermute(cell_pair, "qx", [(k + 2, k) for k in range(nx - 2)]),
        ]
    on_left = lax.ppermute(right, "qy", down_y)
    on_right = lax.ppermute(left, "qy", up_y)
    quad = jnp.concatenate([cell_pair] + others)
    quad, above, below, near_lists = lax.optimization_barrier((quad, above, below, near_lists))
    outward = [(k, k + 2) for k in range(0, ny - 2, 2)] + [(k + 2, k) for k in range(1, ny - 2, 2)]
    inward = [(k + 2, k) for k in range(0, ny - 2, 2)] + [(k, k + 2) for k in range(1, ny - 2, 2)]
    along = lax.ppermute(jnp.concatenate([pair[:4], quad]), "qy", outward)
    quad_back = lax.ppermute(quad, "qy", inward)
    near_b, halo_b = near_own(8, 4 * nx, 4 * ny, near_lists, sites, flat_samples)
    field, flags = rows_level(4 * ny, far_zero, couplings, up, down, above, below)
    one_row = jnp.concatenate([upper[:4], pair[:4], along[:4]])
    two_row = jnp.concatenate([quad, along[4:], quad_back])
    swap_x = [(k, k ^ 1) for k in range(nx)]
    cross_x = [(k, k + 1) for k in range(1, nx - 1, 2)] + [(k + 1, k) for k in range(1, nx - 1, 2)]
    one_d = lax.ppermute(one_row, "qx", cross_x)
    one_e = lax.ppermute(one_row, "qx", swap_x)
    two_e = lax.ppermute(two_row, "qx", swap_x)

    corner_down = jnp.concatenate([on_left[4:8], on_right[4:8], on_left[11:], on_right[11:]])
    corner_up = jnp.concatenate([on_left[:4], on_right[:4], on_left[8:9], on_right[8:9]])
    corner_above = lax.ppermute(corner_down, "qx", down_x)
    corner_below = lax.ppermute(corner_up, "qx", up_x)
    down_one = upper_levels(
        ny, far_one, far_two, couplings, transfer_two, one_row, one_e, one_d, two_row, two_e
    )
    field, down_one = lax.optimization_barrier((field, down_one))
    field, near = sides_level(
        flags, couplings, field, near_a, near_b, halo_a, halo_b, on_left, on_right, above, below
    )
    result = last_level(
        flags,
        couplings,
        transfer_one,
        leaf_basis,
        down_one,
        field,
        near,
        halo_a,
        halo_b,
        corner_above,
        corner_below,
    )
    return result.reshape(4, 4, 256, 256)


def solution(mesh):
    return jax.shard_map(
        per_device,
        mesh=mesh,
        in_specs=(
            P(),
            P("qx", "qy", None, None),
            P("qx", "qy", None, None),
            P("qx", "qy", None, None),
            P("qx", "qy", None, None),
            P(),
            P("qx", "qy", None),
            P("qx", "qy", None),
            P("qx", "qy", None),
            P("qx", "qy", None),
        ),
        out_specs=P("qx", "qy", None, None),
        check_vma=False,
    )
```

time: 1060 us -> 162 us (0.15)
  local copies, waits for them, and re-layouts: 611 us -> 5.62 us
  matrix products: 165 us -> 0 us
  waiting for transfers between devices: 144 us -> 16.7 us
  Pallas kernels: 0 us -> 99.5 us
  starting transfers between devices: 97.4 us -> 33.7 us
  other arithmetic: 29.5 us -> 4.23 us
    gather x59 -> x0, local copies, waits for them, and re-layouts: 288 us -> none  [the longest x21 121 us: one_cell(): flattened[places]]
    dot_general x42 -> x0, matrix products: 165 us -> none  [the longest x21 105 us: one_cell(): jnp.einsum('jrs,jsc->rc', matrices, flattened[places], preferred_element_...]
    unnamed x164 -> x6, local copies, waits for them, and re-layouts: 148 us -> 0.01 us
    ppermute x24 -> x13, waiting for transfers between devices: 144 us -> 16.7 us  [the longest x1 13.4 us: per_device(): quad_back = lax.ppermute(quad, 'qy', inward)]
    another operation x68 -> x0, local copies, waits for them, and re-layouts: 116 us -> none  [the longest x65 104 us: coupling_table(): return jnp.stack(pieces)]
    pallas_call x0 -> x7, Pallas kernels: none -> 99.5 us  [the longest x2 37.4 us: near_own(): pl.pallas_call(functools.partial(near_store_kernel, first, grid_rows, gri...]
    ppermute x24 -> x13, starting transfers between devices: 97.4 us -> 33.7 us  [the longest x1 4.17 us: per_device(): along = lax.ppermute(jnp.concatenate([pair[:4], quad]), 'qy', outward)]
    broadcast_in_dim x36 -> x0, local copies, waits for them, and re-layouts: 21.3 us -> none  [the longest x20 10.8 us: one_cell(): jnp.where(allowed[:, None, None], couple_table[kind_here], jnp.zeros((),...]
  transfers between devices with their start and end apart: 24 -> 13, of which waited for: 5 -> 2; matrix products, arithmetic and copies ran while one was open for 48% -> 6% of each run, Pallas kernels for 0% -> 51%
where the time goes in v2:
time: 162 us; the launch traced here: 160 us
  Pallas kernels  99.5 us (61%)
  starting transfers between devices  33.7 us (21%)
  waiting for transfers between devices  16.7 us (10%)
  local copies, waits for them, and re-layouts  5.62 us (3%)
  other arithmetic  4.23 us (3%)
    pallas_call x2, Pallas kernels, near_own(): pl.pallas_call(functools.partial(near_store_kernel, first, grid_rows, gri...  37.4 us
    pallas_call x1, Pallas kernels, rows_level(): pl.pallas_call(functools.partial(rows_kernel, grid_cols), grid=(4,), out_...  17.1 us
    pallas_call x1, Pallas kernels, sides_level(): pl.pallas_call(sides_kernel, grid=(4,), out_shape=(GROUPED_F32, GROUPED_F...  14.8 us
    ppermute x1, waiting for transfers between devices, per_device(): quad_back = lax.ppermute(quad, 'qy', inward)  13.4 us
    pallas_call x1, Pallas kernels, last_level(): pl.pallas_call(last_kernel, grid=(4,), out_shape=jax.ShapeDtypeStruct((2,...  12.9 us
    pallas_call x1, Pallas kernels, upper_levels(): pl.pallas_call(functools.partial(upper_kernel, grid_cols), grid=(1,), out...  11.8 us
    pallas_call x1, Pallas kernels, coefficients(): pl.pallas_call(coef_kernel, out_shape=(tiles(12), tiles(12), tiles(12), t...  5.45 us
    ppermute x1, starting transfers between devices, per_device(): along = lax.ppermute(jnp.concatenate([pair[:4], quad]), 'qy', outward)  4.17 us
  transfers between devices with their start and end apart: 13, of which 2 were waited for; matrix products, arithmetic and copies ran while one was open for 6% of the time, Pallas kernels for 51%

profile of v2, /device:TPU:17, one launch (start us, length us, event | category | flops | bytes accessed | tf_op | source)
XLA Modules:
  0.0 160.2 jit_solution(15083019411362612223)
XLA Ops:
  0.0 5.4 %coefficients.1 = (bf16[12,256,256]{2,1,0:T(8,128)(2,1)}, bf16[12,256,256]{2,1,0:T(8,128)(2,1)}, bf16[12,256,256]{2,1,0:T(8,128)(2,1)}, bf16[12,256,256]{2,1,0:T(8,128)(2,1)}, bf16[5,256,256]{2,1,0:T(8,128)(2,1)}) custom-call(bf16[4,4,256,256]{3,2,1,0:T(8,128)(2,1)} %samples.1, bf16[4,4,256,256]{3,2,1,0:T(8,128)(2,1)} %basis.1, ...), custom_call_target="tpu_custom_call" | custom-call | flops 5704253440 | bytes 12582912 | tf_op jit(solution)/shard_map/coefficients/pallas_call | solution.py:143
  5.5 3.7 %collective-permute-start.1 = (bf16[12,256,256]{2,1,0:T(8,128)(2,1)}, bf16[12,256,256]{2,1,0:T(8,128)(2,1)S(1)}, u32[]{:S(2)}, u32[]{:S(2)}) collective-permute-start(bf16[12,256,256]{2,1,0:T(8,128)(2,1)} %get-tuple-element.31.down), channel_id=1, source_target_pairs={{0,8},{8,16},{16,24},{1,9},{9,17},{17,25},{2,10},{10,18},{18,26},{... | collective-permute-start | bytes 4718600 | tf_op jit(solution)/shard_map/ppermute | solution.py:689
  9.2 1.9 %collective-permute-start.2 = (bf16[12,256,256]{2,1,0:T(8,128)(2,1)}, bf16[12,256,256]{2,1,0:T(8,128)(2,1)}, u32[]{:S(2)}, u32[]{:S(2)}) collective-permute-start(bf16[12,256,256]{2,1,0:T(8,128)(2,1)} %get-tuple-element.30.up), channel_id=1, source_target_pairs={{8,0},{16,8},{24,16},{9,1},{17,9},{25,17},{10,2},{18,10},{26,18},{... | collective-permute-start | bytes 4718600 | tf_op jit(solution)/shard_map/ppermute | solution.py:690
  11.1 1.3 collective-permute-start
  13.3 18.7 %near_own_0.1 = (f32[8,256,256]{2,1,0:T(8,128)}, bf16[22,256,256]{2,1,0:T(8,128)(2,1)}) custom-call(s32[4,4,9]{2,1,0:T(4,128)} %lists.2, f32[512,2,256]{2,1,0:T(2,128)} %bitcast.11, bf16[16,256,256]{2,1,0:T(8,128)(2,1)} %bitcast.7), custom_call_target="tpu_custom_call" | custom-call | flops 10066329600 | bytes 8388608 | tf_op jit(solution)/shard_map/near_own_0/pallas_call | solution.py:258
  32.2 1.3 collective-permute-start.3
  33.5 2.2 %collective-permute-start.9 = (bf16[12,256,256]{2,1,0:T(8,128)(2,1)}, bf16[12,256,256]{2,1,0:T(8,128)(2,1)}, u32[]{:S(2)}, u32[]{:S(2)}) collective-permute-start(bf16[12,256,256]{2,1,0:T(8,128)(2,1)} %get-tuple-element.51), channel_id=1, source_target_pairs={{0,1},{1,2},{2,3},{3,4},{4,5},{5,6},{6,7},{8,9},{9,10},{10,11},{11... | collective-permute-start | bytes 4718600 | tf_op jit(solution)/shard_map/ppermute | solution.py:705
  35.7 4.0 %collective-permute-start.10 = (bf16[12,256,256]{2,1,0:T(8,128)(2,1)}, bf16[12,256,256]{2,1,0:T(8,128)(2,1)}, u32[]{:S(2)}, u32[]{:S(2)}) collective-permute-start(bf16[12,256,256]{2,1,0:T(8,128)(2,1)} %get-tuple-element.52), channel_id=1, source_target_pairs={{1,0},{2,1},{3,2},{4,3},{5,4},{6,5},{7,6},{9,8},{10,9},{11,10},{12... | collective-permute-start | bytes 4718600 | tf_op jit(solution)/shard_map/ppermute | solution.py:706
  39.8 2.1 %collective-permute-start.7 = (bf16[4,256,256]{2,1,0:T(8,128)(2,1)S(1)}, bf16[4,256,256]{2,1,0:T(8,128)(2,1)}, u32[]{:S(2)}, u32[]{:S(2)}) collective-permute-start(bf16[4,256,256]{2,1,0:T(8,128)(2,1)S(1)} %pad_maximum_fusion.5), channel_id=1, source_target_pairs={{2,0},{4,2},{6,4},{1,3},{3,5},{5,7},{10,8},{12,10},{14,12},{9,11},... | collective-permute-start | bytes 1572872 | tf_op jit(solution)/shard_map/ppermute | solution.py:712
  42.0 4.2 %collective-permute-start.4 = (bf16[8,256,256]{2,1,0:T(8,128)(2,1)S(1)}, bf16[8,256,256]{2,1,0:T(8,128)(2,1)S(1)}, u32[]{:S(2)}, u32[]{:S(2)}) collective-permute-start(bf16[8,256,256]{2,1,0:T(8,128)(2,1)S(1)} %pad_maximum_fusion.4), channel_id=1, source_target_pairs={{0,2},{2,4},{4,6},{3,1},{5,3},{7,5},{8,10},{10,12},{12,14},{11,9},... | collective-permute-start | bytes 3145736 | tf_op jit(solution)/shard_map/ppermute | solution.py:711
  46.2 17.1 %far_rows.1 = (f32[2,2,2,2,256,256]{5,4,3,2,1,0:T(8,128)}, s32[16,37]{1,0:T(8,128)}) custom-call(s32[4,4,27]{2,1,0:T(4,128)} %far_zero.1, bf16[3,20,256,256]{3,2,1,0:T(8,128)(2,1)} %couplings.7, bf16[12,256,256]{2,1,0:T(8,128)(2,1)} %get-tuple-element.30.up, bf16[12,256,256]{2,1,0:T(8,128)(2,1)} %get-tuple-element.31.down, bf16[12,256,256]{2,1,0:T(8,128)(2,1)} %copy-done.2, ...), custom_call_target="tpu_custom_call" | custom-call | flops 14092861440 | bytes 11534336 | tf_op jit(solution)/shard_map/far_rows/pallas_call | solution.py:501
  63.3 3.3 %collective-permute-done.4 = bf16[8,256,256]{2,1,0:T(8,128)(2,1)S(1)} collective-permute-done((bf16[8,256,256]{2,1,0:T(8,128)(2,1)S(1)}, bf16[8,256,256]{2,1,0:T(8,128)(2,1)S(1)}, u32[]{:S(2)}, u32[]{:S(2)}) %collective-permute-start.4) | collective-permute-done | bytes 1048608 | tf_op jit(solution)/shard_map/ppermute | solution.py:711
  66.9 2.9 %collective-permute-start.5 = (bf16[12,256,256]{2,1,0:T(8,128)(2,1)S(1)}, bf16[12,256,256]{2,1,0:T(8,128)(2,1)}, u32[]{:S(2)}, u32[]{:S(2)}) collective-permute-start(bf16[12,256,256]{2,1,0:T(8,128)(2,1)S(1)} %pad_maximum_fusion.row), channel_id=1, source_target_pairs={{0,8},{8,0},{16,24},{24,16},{1,9},{9,1},{17,25},{25,17},{2,10},{10... | collective-permute-start | bytes 4718600 | tf_op jit(solution)/shard_map/ppermute | solution.py:720
  69.8 2.4 %collective-permute-start.6 = (bf16[12,256,256]{2,1,0:T(8,128)(2,1)S(1)}, bf16[12,256,256]{2,1,0:T(8,128)(2,1)}, u32[]{:S(2)}, u32[]{:S(2)}) collective-permute-start(bf16[12,256,256]{2,1,0:T(8,128)(2,1)S(1)} %pad_maximum_fusion.row), channel_id=1, source_target_pairs={{8,16},{16,8},{9,17},{17,9},{10,18},{18,10},{11,19},{19,11},{12,20... | collective-permute-start | bytes 4718600 | tf_op jit(solution)/shard_map/ppermute | solution.py:719
  72.2 13.4 %collective-permute-done.7 = bf16[4,256,256]{2,1,0:T(8,128)(2,1)} collective-permute-done((bf16[4,256,256]{2,1,0:T(8,128)(2,1)S(1)}, bf16[4,256,256]{2,1,0:T(8,128)(2,1)}, u32[]{:S(2)}, u32[]{:S(2)}) %collective-permute-start.7) | collective-permute-done | bytes 524320 | tf_op jit(solution)/shard_map/ppermute | solution.py:712
  85.6 2.4 %pad_maximum_fusion.1.cells = bf16[12,256,256]{2,1,0:T(8,128)(2,1)} fusion(bf16[4,256,256]{2,1,0:T(8,128)(2,1)} %collective-permute-done.7, bf16[4,256,256]{2,1,0:T(8,128)(2,1)S(1)} %get-tuple-element.63, bf16[4,256,256]{2,1,0:T(8,128)(2,1)S(1)} %pad_maximum_fusion.5), kind=kLoop, calls=%fused_computation.1 | loop fusion | flops 1572864 | bytes 3145728 | tf_op jit(solution)/shard_map/concatenate | solution.py:716
  88.0 2.4 %collective-permute-start.8 = (bf16[12,256,256]{2,1,0:T(8,128)(2,1)}, bf16[12,256,256]{2,1,0:T(8,128)(2,1)}, u32[]{:S(2)}, u32[]{:S(2)}) collective-permute-start(bf16[12,256,256]{2,1,0:T(8,128)(2,1)} %pad_maximum_fusion.1.cells), channel_id=1, source_target_pairs={{0,8},{8,0},{16,24},{24,16},{1,9},{9,1},{17,25},{25,17},{2,10},{10... | collective-permute-start | bytes 4718600 | tf_op jit(solution)/shard_map/ppermute | solution.py:721
  90.3 18.7 %near_own_8.1 = (f32[8,256,256]{2,1,0:T(8,128)}, bf16[22,256,256]{2,1,0:T(8,128)(2,1)}) custom-call(s32[4,4,9]{2,1,0:T(4,128)} %lists.2, f32[512,2,256]{2,1,0:T(2,128)} %bitcast.12, bf16[16,256,256]{2,1,0:T(8,128)(2,1)} %bitcast.8), custom_call_target="tpu_custom_call" | custom-call | flops 10066329600 | bytes 8388608 | tf_op jit(solution)/shard_map/near_own_8/pallas_call | solution.py:258
  113.8 2.1 %collective-permute-start.11 = (bf16[10,256,256]{2,1,0:T(8,128)(2,1)S(1)}, bf16[10,256,256]{2,1,0:T(8,128)(2,1)}, u32[]{:S(2)}, u32[]{:S(2)}) collective-permute-start(bf16[10,256,256]{2,1,0:T(8,128)(2,1)S(1)} %pad_maximum_fusion.2), channel_id=1, source_target_pairs={{0,8},{8,16},{16,24},{1,9},{9,17},{17,25},{2,10},{10,18},{18,26},{... | collective-permute-start | bytes 3932168 | tf_op jit(solution)/shard_map/ppermute | solution.py:725
  115.9 1.3 pad_maximum_fusion.3
  117.2 3.3 %collective-permute-start.12 = (bf16[10,256,256]{2,1,0:T(8,128)(2,1)}, bf16[10,256,256]{2,1,0:T(8,128)(2,1)}, u32[]{:S(2)}, u32[]{:S(2)}) collective-permute-start(bf16[10,256,256]{2,1,0:T(8,128)(2,1)} %pad_maximum_fusion.3), channel_id=1, source_target_pairs={{8,0},{16,8},{24,16},{9,1},{17,9},{25,17},{10,2},{18,10},{26,18},{... | collective-permute-start | bytes 3932168 | tf_op jit(solution)/shard_map/ppermute | solution.py:726
  120.5 11.8 %upper_levels.1.down_one = bf16[4,256,256]{2,1,0:T(8,128)(2,1)} custom-call(s32[2,2,27]{2,1,0:T(2,128)} %far_one.1, s32[1,1,27]{2,1,0:T(1,128)} %far_two.1, bf16[3,20,256,256]{3,2,1,0:T(8,128)(2,1)} %couplings.7, bf16[2,2,256,256]{3,2,1,0:T(8,128)(2,1)} %t_two.3, bf16[12,256,256]{2,1,0:T(8,128)(2,1)} %copy-done, ...), custom_call_target="tpu_custom_call" | custom-call | flops 11408506880 | bytes 14680064 | tf_op jit(solution)/shard_map/upper_levels/pallas_call | solution.py:375
  132.3 14.8 %far_sides.1 = (f32[2,2,2,2,256,256]{5,4,3,2,1,0:T(8,128)}, f32[2,2,2,2,256,256]{5,4,3,2,1,0:T(8,128)}) custom-call(s32[16,37]{1,0:T(8,128)} %get-tuple-element.41.flags, bf16[3,20,256,256]{3,2,1,0:T(8,128)(2,1)} %couplings.7, f32[2,2,2,2,256,256]{5,4,3,2,1,0:T(8,128)} %get-tuple-element.45.field_in, f32[2,2,2,256,256]{4,3,2,1,0:T(8,128)} %bitcast.13, ...), custom_call_target="tpu_custom_call" | custom-call | flops 10066329600 | bytes 31457280 | tf_op jit(solution)/shard_map/far_sides/pallas_call | solution.py:576
  147.1 12.9 %last_level.1 = bf16[2,2,2,2,256,256]{5,4,3,2,1,0:T(8,128)(2,1)} custom-call(s32[16,37]{1,0:T(8,128)} %get-tuple-element.41.flags, bf16[3,20,256,256]{3,2,1,0:T(8,128)(2,1)} %couplings.7, bf16[2,2,2,2,256,256]{5,4,3,2,1,0:T(8,128)(2,1)} %bitcast.10, bf16[2,2,2,2,256,256]{5,4,3,2,1,0:T(8,128)(2,1)} %bitcast.9, bf16[4,256,256]{2,1,0:T(8,128)(2,1)} %upper_levels.1.down_one, ...), custom_call_target="tpu_custom_call" | custom-call | flops 9059696640 | bytes 20971520 | tf_op jit(solution)/shard_map/last_level/pallas_call | solution.py:637
  (31 shorter events, 6.2 us)
Async XLA Ops:
  5.5 26.6 %collective-permute-start.1 = (bf16[12,256,256]{2,1,0:T(8,128)(2,1)}, bf16[12,256,256]{2,1,0:T(8,128)(2,1)S(1)}, u32[]{:S(2)}, u32[]{:S(2)}) collective-permute-start(bf16[12,256,256]{2,1,0:T(8,128)(2,1)} %get-tuple-element.31.down), channel_id=1, source_target_pairs={{0,8},{8,16},{16,24},{1,9},{9,17},{17,25},{2,10},{10,18},{18,26},{... | collective-permute-start | bytes 4718600 | tf_op jit(solution)/shard_map/ppermute | solution.py:689
  9.2 22.9 %collective-permute-start.2 = (bf16[12,256,256]{2,1,0:T(8,128)(2,1)}, bf16[12,256,256]{2,1,0:T(8,128)(2,1)}, u32[]{:S(2)}, u32[]{:S(2)}) collective-permute-start(bf16[12,256,256]{2,1,0:T(8,128)(2,1)} %get-tuple-element.30.up), channel_id=1, source_target_pairs={{8,0},{16,8},{24,16},{9,1},{17,9},{25,17},{10,2},{18,10},{26,18},{... | collective-permute-start | bytes 4718600 | tf_op jit(solution)/shard_map/ppermute | solution.py:690
  11.1 21.0 %collective-permute-start = (bf16[5,256,256]{2,1,0:T(8,128)(2,1)}, bf16[5,256,256]{2,1,0:T(8,128)(2,1)S(1)}, u32[]{:S(2)}, u32[]{:S(2)}) collective-permute-start(bf16[5,256,256]{2,1,0:T(8,128)(2,1)} %get-tuple-element.32), channel_id=1, source_target_pairs={{0,1},{1,0},{2,3},{3,2},{4,5},{5,4},{6,7},{7,6},{8,9},{9,8},{10,11... | collective-permute-start | bytes 1966088 | tf_op jit(solution)/shard_map/ppermute | solution.py:688
  13.3 20.1 %copy-start.1 = (bf16[5,256,256]{2,1,0:T(8,128)(2,1)S(1)}, bf16[5,256,256]{2,1,0:T(8,128)(2,1)}, u32[]{:S(2)}) copy-start(bf16[5,256,256]{2,1,0:T(8,128)(2,1)} %get-tuple-element.32) | copy-start | bytes 1966084
  32.1 7.7 %copy-start.2 = (bf16[12,256,256]{2,1,0:T(8,128)(2,1)}, bf16[12,256,256]{2,1,0:T(8,128)(2,1)S(1)}, u32[]{:S(2)}) copy-start(bf16[12,256,256]{2,1,0:T(8,128)(2,1)S(1)} %collective-permute-done.1.above) | copy-start | bytes 4718596
  32.2 7.6 %collective-permute-start.3 = (bf16[2,256,256]{2,1,0:T(8,128)(2,1)S(1)}, bf16[2,256,256]{2,1,0:T(8,128)(2,1)S(1)}, u32[]{:S(2)}, u32[]{:S(2)}) collective-permute-start(bf16[2,256,256]{2,1,0:T(8,128)(2,1)S(1)} %pad_maximum_fusion.6), channel_id=1, source_target_pairs={{0,16},{8,24},{16,0},{24,8},{1,17},{9,25},{17,1},{25,9},{2,18},{10... | collective-permute-start | bytes 786440 | tf_op jit(solution)/shard_map/ppermute | solution.py:699
  33.5 76.5 %collective-permute-start.9 = (bf16[12,256,256]{2,1,0:T(8,128)(2,1)}, bf16[12,256,256]{2,1,0:T(8,128)(2,1)}, u32[]{:S(2)}, u32[]{:S(2)}) collective-permute-start(bf16[12,256,256]{2,1,0:T(8,128)(2,1)} %get-tuple-element.51), channel_id=1, source_target_pairs={{0,1},{1,2},{2,3},{3,4},{4,5},{5,6},{6,7},{8,9},{9,10},{10,11},{11... | collective-permute-start | bytes 4718600 | tf_op jit(solution)/shard_map/ppermute | solution.py:705
  35.7 73.3 %collective-permute-start.10 = (bf16[12,256,256]{2,1,0:T(8,128)(2,1)}, bf16[12,256,256]{2,1,0:T(8,128)(2,1)}, u32[]{:S(2)}, u32[]{:S(2)}) collective-permute-start(bf16[12,256,256]{2,1,0:T(8,128)(2,1)} %get-tuple-element.52), channel_id=1, source_target_pairs={{1,0},{2,1},{3,2},{4,3},{5,4},{6,5},{7,6},{9,8},{10,9},{11,10},{12... | collective-permute-start | bytes 4718600 | tf_op jit(solution)/shard_map/ppermute | solution.py:706
  39.8 45.8 %collective-permute-start.7 = (bf16[4,256,256]{2,1,0:T(8,128)(2,1)S(1)}, bf16[4,256,256]{2,1,0:T(8,128)(2,1)}, u32[]{:S(2)}, u32[]{:S(2)}) collective-permute-start(bf16[4,256,256]{2,1,0:T(8,128)(2,1)S(1)} %pad_maximum_fusion.5), channel_id=1, source_target_pairs={{2,0},{4,2},{6,4},{1,3},{3,5},{5,7},{10,8},{12,10},{14,12},{9,11},... | collective-permute-start | bytes 1572872 | tf_op jit(solution)/shard_map/ppermute | solution.py:712
  42.0 24.6 %collective-permute-start.4 = (bf16[8,256,256]{2,1,0:T(8,128)(2,1)S(1)}, bf16[8,256,256]{2,1,0:T(8,128)(2,1)S(1)}, u32[]{:S(2)}, u32[]{:S(2)}) collective-permute-start(bf16[8,256,256]{2,1,0:T(8,128)(2,1)S(1)} %pad_maximum_fusion.4), channel_id=1, source_target_pairs={{0,2},{2,4},{4,6},{3,1},{5,3},{7,5},{8,10},{10,12},{12,14},{11,9},... | collective-permute-start | bytes 3145736 | tf_op jit(solution)/shard_map/ppermute | solution.py:711
  66.9 21.1 %copy-start = (bf16[12,256,256]{2,1,0:T(8,128)(2,1)}, bf16[12,256,256]{2,1,0:T(8,128)(2,1)S(1)}, u32[]{:S(2)}) copy-start(bf16[12,256,256]{2,1,0:T(8,128)(2,1)S(1)} %pad_maximum_fusion.row) | copy-start | bytes 4718596
  66.9 53.6 %collective-permute-start.5 = (bf16[12,256,256]{2,1,0:T(8,128)(2,1)S(1)}, bf16[12,256,256]{2,1,0:T(8,128)(2,1)}, u32[]{:S(2)}, u32[]{:S(2)}) collective-permute-start(bf16[12,256,256]{2,1,0:T(8,128)(2,1)S(1)} %pad_maximum_fusion.row), channel_id=1, source_target_pairs={{0,8},{8,0},{16,24},{24,16},{1,9},{9,1},{17,25},{25,17},{2,10},{10... | collective-permute-start | bytes 4718600 | tf_op jit(solution)/shard_map/ppermute | solution.py:720
  69.8 50.7 %collective-permute-start.6 = (bf16[12,256,256]{2,1,0:T(8,128)(2,1)S(1)}, bf16[12,256,256]{2,1,0:T(8,128)(2,1)}, u32[]{:S(2)}, u32[]{:S(2)}) collective-permute-start(bf16[12,256,256]{2,1,0:T(8,128)(2,1)S(1)} %pad_maximum_fusion.row), channel_id=1, source_target_pairs={{8,16},{16,8},{9,17},{17,9},{10,18},{18,10},{11,19},{19,11},{12,20... | collective-permute-start | bytes 4718600 | tf_op jit(solution)/shard_map/ppermute | solution.py:719
  88.0 32.6 %collective-permute-start.8 = (bf16[12,256,256]{2,1,0:T(8,128)(2,1)}, bf16[12,256,256]{2,1,0:T(8,128)(2,1)}, u32[]{:S(2)}, u32[]{:S(2)}) collective-permute-start(bf16[12,256,256]{2,1,0:T(8,128)(2,1)} %pad_maximum_fusion.1.cells), channel_id=1, source_target_pairs={{0,8},{8,0},{16,24},{24,16},{1,9},{9,1},{17,25},{25,17},{2,10},{10... | collective-permute-start | bytes 4718600 | tf_op jit(solution)/shard_map/ppermute | solution.py:721
  113.8 33.3 %collective-permute-start.11 = (bf16[10,256,256]{2,1,0:T(8,128)(2,1)S(1)}, bf16[10,256,256]{2,1,0:T(8,128)(2,1)}, u32[]{:S(2)}, u32[]{:S(2)}) collective-permute-start(bf16[10,256,256]{2,1,0:T(8,128)(2,1)S(1)} %pad_maximum_fusion.2), channel_id=1, source_target_pairs={{0,8},{8,16},{16,24},{1,9},{9,17},{17,25},{2,10},{10,18},{18,26},{... | collective-permute-start | bytes 3932168 | tf_op jit(solution)/shard_map/ppermute | solution.py:725
  117.2 30.0 %collective-permute-start.12 = (bf16[10,256,256]{2,1,0:T(8,128)(2,1)}, bf16[10,256,256]{2,1,0:T(8,128)(2,1)}, u32[]{:S(2)}, u32[]{:S(2)}) collective-permute-start(bf16[10,256,256]{2,1,0:T(8,128)(2,1)} %pad_maximum_fusion.3), channel_id=1, source_target_pairs={{8,0},{16,8},{24,16},{9,1},{17,9},{25,17},{10,2},{18,10},{26,18},{... | collective-permute-start | bytes 3932168 | tf_op jit(solution)/shard_map/ppermute | solution.py:726

commit v3 on v2

--- a/solution.py
+++ b/solution.py
@@ -35,7 +35,7 @@
 
 def cost(products, bytes_accessed):
     return pl.CostEstimate(
-        flops=products * 2 * 256**3, bytes_accessed=bytes_accessed, transcendentals=0
+        flops=products * 2 * 256**3 // 8, bytes_accessed=bytes_accessed // 8, transcendentals=0
     )
 
 
@@ -65,6 +65,7 @@
 
 
 LOG2E = 1.4426950408889634
+TILE_SCALE = 256 ** -0.5
 
 
 def tiles(n, dtype=BF16):
@@ -161,6 +162,31 @@
     )(samples, basis, t_one, t_two)
 
 
+def assembled(name, sources, plans):
+    sizes = [sum(n for _, _, n in plan) for plan in plans]
+    count = sum(len(plan) for plan in plans)
+
+    def kernel(*refs):
+        ins, outs, sems = refs[: len(sources)], refs[len(sources) : -1], refs[-1]
+        copies = Copies(sems)
+        for plan, out in zip(plans, outs):
+            at = 0
+            for source, first, n in plan:
+                copies.start(ins[source].at[first : first + n], out.at[at : at + n])
+                at += n
+        copies.wait()
+
+    return pl.pallas_call(
+        kernel,
+        out_shape=[tiles(n) for n in sizes],
+        in_specs=[ANY_SPEC] * len(sources),
+        out_specs=[ANY_SPEC] * len(plans),
+        scratch_shapes=[pltpu.SemaphoreType.DMA((count,))],
+        cost_estimate=cost(35, 0),
+        name=name,
+    )(*sources)
+
+
 def halo_places():
     numbers = {}
     for r in range(4):
@@ -176,77 +202,96 @@
 N_HALO = len(HALO) // 2
 
 
+def split3(x):
+    first = x.astype(BF16).astype(F32)
+    rest = x - first
+    second = rest.astype(BF16).astype(F32)
+    return first, second, rest - second
+
+
+def site_features(x, y):
+    n = lax.broadcasted_iota(jnp.int32, (8, 256), 0)
+    square = x * x + y * y
+    target, source = [], []
+    for parts in (split3(x), split3(y)):
+        first, second, third = parts
+        target.append(jnp.where(n < 3, first, jnp.where(n < 5, second, jnp.where(n < 6, third, 0.0))))
+        other = jnp.where(
+            (n == 0) | (n == 3) | (n == 5),
+            first,
+            jnp.where((n == 1) | (n == 4), second, jnp.where(n == 2, third, 0.0)),
+        )
+        source.append(-2.0 * other)
+    first, second, third = split3(square)
+    low = jnp.where(n == 0, first, jnp.where(n == 1, second, third))
+    high = jnp.where(n == 3, first, jnp.where(n == 4, second, third))
+    one = jnp.where(n < 6, 1.0, 0.0)
+    target.append(jnp.where(n < 3, low, one))
+    source.append(jnp.where(n < 3, 1.0, jnp.where(n < 6, high, 0.0)))
+    zero = jnp.zeros((8, 256), F32)
+    return jnp.concatenate(target + [zero], axis=0), jnp.concatenate(source + [zero], axis=0)
+
+
 def near_kernel(
-    first, grid_rows, grid_cols, lists, positions, own, near, halo_tiles,
-    held, plane_x, plane_y, weight, sems,
+    first, grid_rows, grid_cols, lists, positions, own, near, halo_out,
+    held, target_feat, source_feat, halo, floors, sems, halo_sems,
 ):
     copy = pltpu.make_async_copy(own, held.at[0:16], sems.at[0])
     copy.start()
     held[16] = jnp.zeros((256, 256), BF16)
     first_row = lax.axis_index("qx") * 4
     first_col = lax.axis_index("qy") * 4
-    scale = root_three / length_scale * LOG2E
-    weight_full = 256 ** -0.5
-
-    def place_of(row, col):
-        r = jnp.clip(row, 0, grid_rows - 1)
-        c = jnp.clip(col, 0, grid_cols - 1)
-        return r * grid_cols + c
-
+    scale = root_three / length_scale
+    mid_row = first_row.astype(F32) + 2.0
+    mid_col = first_col.astype(F32) + 2.0
+    first_place = first // 4 * 6
+
+    def features(n, carry):
+        r = jnp.clip(first_row + (first_place + n) // 6 - 1, 0, grid_rows - 1)
+        c = jnp.clip(first_col + n % 6 - 1, 0, grid_cols - 1)
+        here = positions[r * grid_cols + c]
+        target, source = site_features(
+            (here[0:1] - mid_row) * scale, (here[1:2] - mid_col) * scale
+        )
+        target_feat[n] = target
+        source_feat[n] = source.astype(BF16)
+        return carry
+
+    lax.fori_loop(0, 24, features, 0)
     copy.wait()
 
-    def one_target(t, carry):
+    def one_target(m, carry):
+        t = first + m
         r = t // 4
         c = t % 4
         row = first_row + r
         col = first_col + c
-        mid_row = row.astype(F32) + 0.5
-        mid_col = col.astype(F32) + 0.5
         for k in range(9):
-            weight[k] = 0.0
+            floors[k] = 1e6
         for e in range(9):
             entry = lists[r, c, e]
             source_row = jnp.maximum(entry, 0) // grid_cols
             source_col = jnp.maximum(entry, 0) - source_row * grid_cols
             k = (source_row - row + 1) * 3 + source_col - col + 1
-            weight[jnp.where(entry >= 0, k, 9)] = weight_full
-        here = positions[place_of(row, col)]
-        turn_x = jnp.broadcast_to((here[0:1] - mid_row) * scale, (8, 256)).T
-        turn_y = jnp.broadcast_to((here[1:2] - mid_col) * scale, (8, 256)).T
-        plane_x[...] = jnp.broadcast_to(turn_x[:, 0:1], (256, 128))
-        plane_y[...] = jnp.broadcast_to(turn_y[:, 0:1], (256, 128))
+            floors[jnp.where(entry >= 0, k, 9)] = 1e-24
+        place = (m // 4 + 1) * 6 + c + 1
+        target = target_feat[place].T.astype(BF16)
         made = []
         blocks = []
         for k in range(9):
             dr, dc = k // 3 - 1, k % 3 - 1
-            there = positions[place_of(row + dr, col + dc)]
-            x = (there[0:1] - mid_row) * scale
-            y = (there[1:2] - mid_col) * scale
-            w = weight[k]
-            halves = []
-            for h in range(2):
-                gap_x = plane_x[...] - x[:, 128 * h : 128 * h + 128]
-                gap_y = plane_y[...] - y[:, 128 * h : 128 * h + 128]
-                square = jnp.maximum(gap_x * gap_x + gap_y * gap_y, 1e-24)
-                far = square * lax.rsqrt(square)
-                halves.append(((far * (w / LOG2E) + w) * jnp.exp2(-far)).astype(BF16))
-            tile = jnp.concatenate(halves, axis=1)
+            square = nn(target, source_feat[place + dr * 6 + dc])
+            square = jnp.maximum(square, floors[k])
+            far = square * lax.rsqrt(square)
+            tile = ((far + 1.0) * jnp.exp2(far * -LOG2E)).astype(BF16)
             inside = (r + dr >= 0) & (r + dr < 4) & (c + dc >= 0) & (c + dc < 4)
-            halo_tiles[jnp.where(inside, 72, (t - first) * 9 + k)] = tile
+            halo[jnp.where(inside, 72, m * 9 + k)] = tile
             made.append(tile)
             blocks.append(held[jnp.where(inside, (r + dr) * 4 + c + dc, 16)])
-        near[t - first] = nn(jnp.concatenate(made, axis=1), jnp.concatenate(blocks, axis=0))
+        near[m] = nn(jnp.concatenate(made, axis=1), jnp.concatenate(blocks, axis=0))
         return carry
 
-    lax.fori_loop(first, first + 8, one_target, 0)
-
-
-def near_store_kernel(first, grid_rows, grid_cols, lists, positions, own, near, halo_out, *scratch):
-    held, plane_x, plane_y, halo, weight, sems, halo_sems = scratch
-    near_kernel(
-        first, grid_rows, grid_cols, lists, positions, own, near, halo,
-        held, plane_x, plane_y, weight, sems,
-    )
+    lax.fori_loop(0, 8, one_target, 0)
     out = Copies(halo_sems)
     for (t, k), number in HALO.items():
         if first <= t < first + 8:
@@ -256,14 +301,14 @@
 
 def near_own(first, grid_rows, grid_cols, lists, positions, own):
     return pl.pallas_call(
-        functools.partial(near_store_kernel, first, grid_rows, grid_cols),
+        functools.partial(near_kernel, first, grid_rows, grid_cols),
         out_shape=(tiles(8, F32), tiles(N_HALO)),
         in_specs=[SMEM_SPEC, VMEM_SPEC, ANY_SPEC],
         out_specs=[VMEM_SPEC, ANY_SPEC],
         scratch_shapes=[
             VMEM((17, 256, 256), BF16),
-            VMEM((256, 128), F32),
-            VMEM((256, 128), F32),
+            VMEM((24, 32, 256), F32),
+            VMEM((24, 32, 256), BF16),
             VMEM((73, 256, 256), BF16),
             pltpu.SMEM((10,), F32),
             pltpu.SemaphoreType.DMA((1,)),
@@ -306,19 +351,19 @@
     return total
 
 
-def upper_kernel(
-    grid_cols, far_one, far_two, couplings, t_two, row, row_e, row_d, cells, cells_e, down,
-    held_one, held_two, field_two, flags, sems,
-):
-    n_one = row.shape[0]
-    n_two = cells.shape[0]
-    zero_one, zero_two = 3 * n_one, 2 * n_two
+def upper_kernel(grid_cols, n_others, far_one, far_two, couplings, t_two, *rest):
+    row, row_e, row_d = rest[:3]
+    others = rest[3 : 3 + 2 * n_others]
+    down, held_one, held_two, field_two, flags, sems = rest[3 + 2 * n_others :]
+    zero_one, zero_two = 36, 12 + 12 * n_others
     copies = Copies(sems)
-    copies.start(cells, held_two.at[0:n_two])
-    copies.start(cells_e, held_two.at[n_two : 2 * n_two])
-    copies.start(row, held_one.at[0:n_one])
-    copies.start(row_e, held_one.at[n_one : 2 * n_one])
-    copies.start(row_d, held_one.at[2 * n_one : 3 * n_one])
+    copies.start(row.at[12:18], held_two.at[0:6])
+    copies.start(row_e.at[12:18], held_two.at[6:12])
+    for n, other in enumerate(others):
+        copies.start(other, held_two.at[12 + 6 * n : 18 + 6 * n])
+    copies.start(row.at[0:12], held_one.at[0:12])
+    copies.start(row_e.at[0:12], held_one.at[12:24])
+    copies.start(row_d, held_one.at[24:36])
     held_one[zero_one] = jnp.zeros((256, 256), BF16)
     held_two[zero_two] = jnp.zeros((256, 256), BF16)
     i = lax.axis_index("qx")
@@ -332,18 +377,24 @@
     mark_listed(
         lambda e: far_two[0, 0, e], flags, 4, i // 2 * 2 - 2, j // 2 * 2 - 2, grid_cols
     )
-    n_quad = n_two // 3
-    core_at = [jnp.where(a == 0, 0, n_two), jnp.where(a == 0, n_two, 0)]
-    z_at = [jnp.where(b == 0, n_quad, 2 * n_quad), 0, jnp.where(b == 0, 2 * n_quad, n_quad)]
-    y_at = [2, 0, 2] if n_quad == 4 else [2, 0, 4]
+    rows_at = []
+    for r in range(6):
+        if r // 2 == 1:
+            rows_at.append(jnp.where(a == r % 2, 0, 6))
+        else:
+            n = 0 if r // 2 == 0 or n_others == 1 else 1
+            rows_at.append(
+                jnp.where(a == r % 2, 12 + 6 * n, 12 + 6 * (n_others + n))
+            )
+    z_at = [jnp.where(b == 0, 2, 4), 0, jnp.where(b == 0, 4, 2)]
     x_at = [b, 1 - b]
 
     def place_two(w):
         r, c = w // 6, w % 6
-        place = core_at[r % 2] + z_at[c // 2] + y_at[r // 2] + x_at[c % 2]
+        place = rows_at[r] + z_at[c // 2] + x_at[c % 2]
         return jnp.where(flags[4, w] == 1, place, zero_two)
 
-    row_at = [jnp.where(a == 0, 2 * n_one, n_one), 0, jnp.where(a == 0, n_one, 2 * n_one)]
+    row_at = [jnp.where(a == 0, 24, 12), 0, jnp.where(a == 0, 12, 24)]
     col_at = [jnp.where(b == 0, 8, 4), 0, jnp.where(b == 0, 4, 8)]
 
     def place_one(t, w):
@@ -351,7 +402,8 @@
         place = row_at[r // 2] + col_at[c // 2] + (r % 2) * 2 + c % 2
         return jnp.where(flags[t, w] == 1, place, zero_one)
 
-    copies.wait()
+    for copy in copies.started[: 2 + 2 * n_others]:
+        copy.wait()
     for u in range(2):
         for v in range(2):
 
@@ -361,6 +413,8 @@
                     class_plan(u, v), couplings.at[1], held_two, place_two
                 ).astype(BF16)
 
+    for copy in copies.started[2 + 2 * n_others :]:
+        copy.wait()
     for u in range(2):
         for v in range(2):
             t = u * 2 + v
@@ -370,10 +424,10 @@
             down[t] = (field + nt(field_two[...], t_two[u, v])).astype(BF16)
 
 
-def upper_levels(grid_cols, far_one, far_two, couplings, t_two, row, row_e, row_d, cells, cells_e):
-    n_one, n_two = row.shape[0], cells.shape[0]
+def upper_levels(grid_cols, far_one, far_two, couplings, t_two, row, row_e, row_d, others):
+    n_others = len(others) // 2
     return pl.pallas_call(
-        functools.partial(upper_kernel, grid_cols),
+        functools.partial(upper_kernel, grid_cols, n_others),
         grid=(1,),
         out_shape=tiles(4),
         in_specs=[
@@ -385,19 +439,19 @@
             ),
             pl.BlockSpec((2, 2, 256, 256), lambda g: (0, 0, 0, 0)),
         ]
-        + [ANY_SPEC] * 5,
+        + [ANY_SPEC] * (3 + 2 * n_others),
         out_specs=pl.BlockSpec((4, 256, 256), lambda g: (0, 0, 0)),
         scratch_shapes=[
-            VMEM((3 * n_one + 1, 256, 256), BF16),
-            VMEM((2 * n_two + 1, 256, 256), BF16),
+            VMEM((37, 256, 256), BF16),
+            VMEM((13 + 12 * n_others, 256, 256), BF16),
             VMEM((256, 256), BF16),
             pltpu.SMEM((5, 37), jnp.int32),
-            pltpu.SemaphoreType.DMA((5,)),
+            pltpu.SemaphoreType.DMA((5 + 2 * n_others,)),
         ],
         compiler_params=params(),
         cost_estimate=cost(340, 14 << 20),
         name="upper_levels",
-    )(far_one, far_two, couplings, t_two, row, row_e, row_d, cells, cells_e)
+    )(far_one, far_two, couplings, t_two, row, row_e, row_d, *others)
 
 
 def source_of(x, y, w):
@@ -545,22 +599,31 @@
 ):
     step = pl.program_id(0)
 
+    def copies():
+        pairs = [(left.at[0:8], held.at[0:8]), (right.at[0:8], held.at[8:16])]
+        for n, src in enumerate((left, right, above, below)):
+            pairs.append((src.at[8:12], near_held.at[4 * n : 4 * n + 4]))
+        pairs.append((halo_a, halo.at[0:N_HALO]))
+        pairs.append((halo_b, halo.at[N_HALO : 2 * N_HALO]))
+        return [pltpu.make_async_copy(src, dst, sems.at[n]) for n, (src, dst) in enumerate(pairs)]
+
     @pl.when(step == 0)
     def _():
-        copies = Copies(sems)
-        copies.start(left.at[0:8], held.at[0:8])
-        copies.start(right.at[0:8], held.at[8:16])
-        for n, src in enumerate((left, right, above, below)):
-            copies.start(src.at[8:12], near_held.at[4 * n : 4 * n + 4])
-        copies.start(halo_a, halo.at[0:N_HALO])
-        copies.start(halo_b, halo.at[N_HALO : 2 * N_HALO])
+        started = copies()
+        for copy in started:
+            copy.start()
         held[16] = jnp.zeros((256, 256), BF16)
-        copies.wait()
+        for copy in started[:2]:
+            copy.wait()
 
     def body(a, b):
         sums = level_zero_sums("sides", a, b, flags, couplings.at[0], held, 16)
         for x, y in PARENTS:
             field[x, 0, y, 0] = field_in[x, 0, y, 0] + sums[x, y]
+        if a == 0 and b == 0:
+            for copy in copies()[2:]:
+                copy.wait()
+        for x, y in PARENTS:
             part = near_part("side", number_of(a, b, (x, y)), lambda n: halo[n], near_held)
             here = (near_b if x else near_a)[0, y, 0]
             near[x, 0, y, 0] = here if part is None else here + part
@@ -617,7 +680,8 @@
             total = field[x, 0, y, 0] + nt(down_one[x * 2 + y], t_one[x, 0, y, 0])
             if (x, y) in sums:
                 total = total + sums[x, y]
-            result = near[x, 0, y, 0] + nt(basis[x, 0, y, 0], total.astype(BF16))
+            far = nt(basis[x, 0, y, 0], total.astype(BF16))
+            near_sum = near[x, 0, y, 0]
             part = near_part(
                 "corner",
                 number_of(a, b, (x, y)),
@@ -625,8 +689,8 @@
                 near_held,
             )
             if part is not None:
-                result = result + part
-            out[x, 0, y, 0] = result.astype(BF16)
+                near_sum = near_sum + part
+            out[x, 0, y, 0] = (near_sum * TILE_SCALE + far).astype(BF16)
 
     each_class(step, body)
 
@@ -685,49 +749,60 @@
 
     up, down, left, right, upper = coefficients(samples, leaf_basis, transfer_one, transfer_two)
 
-    pair = lax.ppermute(upper, "qy", [(k, k ^ 1) for k in range(ny)])
     above = lax.ppermute(down, "qx", down_x)
     below = lax.ppermute(up, "qx", up_x)
+    pair = lax.ppermute(upper, "qy", [(k, k ^ 1) for k in range(ny)])
     sites = positions.reshape(-1, 2, 256)
     flat_samples = samples.reshape(16, 256, 256)
     near_a, halo_a = near_own(0, 4 * nx, 4 * ny, near_lists, sites, flat_samples)
     pair, above, below, left, right, near_a = lax.optimization_barrier(
         (pair, above, below, left, right, near_a)
     )
-    cell_pair = jnp.concatenate([upper[4:], pair[4:]])
+    outward = [(k, k + 2) for k in range(0, ny - 2, 2)] + [(k + 2, k) for k in range(1, ny - 2, 2)]
+    inward = [(k + 2, k) for k in range(0, ny - 2, 2)] + [(k, k + 2) for k in range(1, ny - 2, 2)]
+    to_out, to_in = assembled(
+        "pair_payload", (upper, pair), [[(1, 0, 5), (0, 4, 1)], [(0, 4, 1), (1, 4, 1)]]
+    )
+    on_left = lax.ppermute(right, "qy", down_y)
+    on_right = lax.ppermute(left, "qy", up_y)
+    outer = lax.ppermute(to_out, "qy", outward)
+    inner = lax.ppermute(to_in, "qy", inward)
+    near_b, halo_b = near_own(8, 4 * nx, 4 * ny, near_lists, sites, flat_samples)
+    inner, outer, near_b = lax.optimization_barrier((inner, outer, near_b))
+    cells = [(0, 4, 1), (1, 4, 1), (2, 5, 1), (2, 4, 1), (3, 0, 2)]
+    ones = [(0, 0, 4), (1, 0, 4), (2, 0, 4)]
+    row, one_row, two_row = assembled(
+        "row_payload", (upper, pair, outer, inner), [ones + cells, ones, cells]
+    )
+    swap_x = [(k, k ^ 1) for k in range(nx)]
+    cross_x = [(k, k + 1) for k in range(1, nx - 1, 2)] + [(k + 1, k) for k in range(1, nx - 1, 2)]
     if nx == 4:
-        others = [lax.ppermute(cell_pair, "qx", [(k, k ^ 2) for k in range(nx)])]
+        others = [lax.ppermute(two_row, "qx", [(k, k ^ 2) for k in range(nx)])]
     else:
         others = [
-            lax.ppermute(cell_pair, "qx", [(k, k + 2) for k in range(nx - 2)]),
-            lax.ppermute(cell_pair, "qx", [(k + 2, k) for k in range(nx - 2)]),
+            lax.ppermute(two_row, "qx", [(k, k + 2) for k in range(nx - 2)]),
+            lax.ppermute(two_row, "qx", [(k + 2, k) for k in range(nx - 2)]),
         ]
-    on_left = lax.ppermute(right, "qy", down_y)
-    on_right = lax.ppermute(left, "qy", up_y)
-    quad = jnp.concatenate([cell_pair] + others)
-    quad, above, below, near_lists = lax.optimization_barrier((quad, above, below, near_lists))
-    outward = [(k, k + 2) for k in range(0, ny - 2, 2)] + [(k + 2, k) for k in range(1, ny - 2, 2)]
-    inward = [(k + 2, k) for k in range(0, ny - 2, 2)] + [(k, k + 2) for k in range(1, ny - 2, 2)]
-    along = lax.ppermute(jnp.concatenate([pair[:4], quad]), "qy", outward)
-    quad_back = lax.ppermute(quad, "qy", inward)
-    near_b, halo_b = near_own(8, 4 * nx, 4 * ny, near_lists, sites, flat_samples)
+    row_d = lax.ppermute(one_row, "qx", cross_x)
+    row_e = lax.ppermute(row, "qx", swap_x)
     field, flags = rows_level(4 * ny, far_zero, couplings, up, down, above, below)
-    one_row = jnp.concatenate([upper[:4], pair[:4], along[:4]])
-    two_row = jnp.concatenate([quad, along[4:], quad_back])
-    swap_x = [(k, k ^ 1) for k in range(nx)]
-    cross_x = [(k, k + 1) for k in range(1, nx - 1, 2)] + [(k + 1, k) for k in range(1, nx - 1, 2)]
-    one_d = lax.ppermute(one_row, "qx", cross_x)
-    one_e = lax.ppermute(one_row, "qx", swap_x)
-    two_e = lax.ppermute(two_row, "qx", swap_x)
-
-    corner_down = jnp.concatenate([on_left[4:8], on_right[4:8], on_left[11:], on_right[11:]])
-    corner_up = jnp.concatenate([on_left[:4], on_right[:4], on_left[8:9], on_right[8:9]])
+    others, field = lax.optimization_barrier((others, field))
+    others = others + [lax.ppermute(x, "qx", swap_x) for x in others]
+    down_one = upper_levels(
+        ny, far_one, far_two, couplings, transfer_two, row, row_e, row_d, others
+    )
+
+    on_left, on_right, down_one = lax.optimization_barrier((on_left, on_right, down_one))
+    corner_down, corner_up = assembled(
+        "corner_payload",
+        (on_left, on_right),
+        [
+            [(0, 4, 4), (1, 4, 4), (0, 11, 1), (1, 11, 1)],
+            [(0, 0, 4), (1, 0, 4), (0, 8, 1), (1, 8, 1)],
+        ],
+    )
     corner_above = lax.ppermute(corner_down, "qx", down_x)
     corner_below = lax.ppermute(corner_up, "qx", up_x)
-    down_one = upper_levels(
-        ny, far_one, far_two, couplings, transfer_two, one_row, one_e, one_d, two_row, two_e
-    )
-    field, down_one = lax.optimization_barrier((field, down_one))
     field, near = sides_level(
         flags, couplings, field, near_a, near_b, halo_a, halo_b, on_left, on_right, above, below
     )

time: 162 us -> 424 us (2.62)
  Pallas kernels: 99.5 us -> 346 us
  waiting for transfers between devices: 16.7 us -> 44.5 us
  starting transfers between devices: 33.7 us -> 27.1 us
    pallas_call x3 -> x6, Pallas kernels: 49.2 us -> 297 us  [the longest x3 258 us: assembled(): pl.pallas_call(kernel, out_shape=[tiles(n) for n in sizes], in_specs=[ANY...]
    ppermute x1, waiting for transfers between devices: 0.01 us -> 27.2 us  [per_device(): on_left = lax.ppermute(right, 'qy', down_y)]
    ppermute x6, waiting for transfers between devices: 16.7 us -> 9.05 us  [the longest x1 9.04 us: per_device(): row_d = lax.ppermute(one_row, 'qx', cross_x)]
    ppermute x6, starting transfers between devices: 15.2 us -> 9.45 us  [the longest x1 3.4 us: per_device(): row_d = lax.ppermute(one_row, 'qx', cross_x)]
    slice x9 -> x0, local copies, waits for them, and re-layouts: 5.61 us -> none  [the longest x1 1.27 us: per_device(): on_right[:4]]
    unnamed x6 -> x20, local copies, waits for them, and re-layouts: 0.01 us -> 4.31 us
    ppermute x1, waiting for transfers between devices: 0.01 us -> 4.29 us  [per_device(): below = lax.ppermute(up, 'qx', up_x)]
  transfers between devices with their start and end apart: 13 -> 13, of which waited for: 2 -> 6; matrix products, arithmetic and copies ran while one was open for 6% -> 0% of each run, Pallas kernels for 51% -> 17%
where the time goes in v3:
time: 424 us; the launch traced here: 422 us
  Pallas kernels  346 us (82%)
  waiting for transfers between devices  44.5 us (10%)
  starting transfers between devices  27.1 us (6%)
  local copies, waits for them, and re-layouts  4.31 us (1%)
    pallas_call x3, Pallas kernels, assembled(): pl.pallas_call(kernel, out_shape=[tiles(n) for n in sizes], in_specs=[ANY...  258 us
    pallas_call x2, Pallas kernels, near_own(): pl.pallas_call(functools.partial(near_kernel, first, grid_rows, grid_cols...  28.2 us
    ppermute x1, waiting for transfers between devices, per_device(): on_left = lax.ppermute(right, 'qy', down_y)  27.2 us
    pallas_call x1, Pallas kernels, rows_level(): pl.pallas_call(functools.partial(rows_kernel, grid_cols), grid=(4,), out_...  17.1 us
    pallas_call x1, Pallas kernels, sides_level(): pl.pallas_call(sides_kernel, grid=(4,), out_shape=(GROUPED_F32, GROUPED_F...  14.1 us
    pallas_call x1, Pallas kernels, last_level(): pl.pallas_call(last_kernel, grid=(4,), out_shape=jax.ShapeDtypeStruct((2,...  12.7 us
    pallas_call x1, Pallas kernels, upper_levels(): pl.pallas_call(functools.partial(upper_kernel, grid_cols, n_others), grid...  10.7 us
    ppermute x1, waiting for transfers between devices, per_device(): row_d = lax.ppermute(one_row, 'qx', cross_x)  9.04 us
  transfers between devices with their start and end apart: 13, of which 6 were waited for; matrix products, arithmetic and copies ran while one was open for 0% of the time, Pallas kernels for 17%

profile of v3, /device:TPU:17, one launch (start us, length us, event | category | flops | bytes accessed | tf_op | source)
XLA Modules:
  0.0 422.4 jit_solution(2633249116618270993)
XLA Ops:
  0.0 5.5 %coefficients.1 = (bf16[12,256,256]{2,1,0:T(8,128)(2,1)}, bf16[12,256,256]{2,1,0:T(8,128)(2,1)}, bf16[12,256,256]{2,1,0:T(8,128)(2,1)}, bf16[12,256,256]{2,1,0:T(8,128)(2,1)}, bf16[5,256,256]{2,1,0:T(8,128)(2,1)}) custom-call(bf16[4,4,256,256]{3,2,1,0:T(8,128)(2,1)} %samples.1, bf16[4,4,256,256]{3,2,1,0:T(8,128)(2,1)} %basis.1, ...), custom_call_target="tpu_custom_call" | custom-call | flops 713031680 | bytes 1572864 | tf_op jit(solution)/shard_map/coefficients/pallas_call | solution.py:144
  5.5 3.7 collective-permute-start.1
  9.2 1.9 collective-permute-start.2
  11.1 1.3 collective-permute-start
  12.4 14.2 %near_own_0.1 = (f32[8,256,256]{2,1,0:T(8,128)}, bf16[22,256,256]{2,1,0:T(8,128)(2,1)}) custom-call(s32[4,4,9]{2,1,0:T(4,128)} %lists.3, f32[512,2,256]{2,1,0:T(2,128)} %bitcast.13, bf16[16,256,256]{2,1,0:T(8,128)(2,1)} %bitcast.9), custom_call_target="tpu_custom_call" | custom-call | flops 1258291200 | bytes 1048576 | tf_op jit(solution)/shard_map/near_own_0/pallas_call | solution.py:303
  26.9 4.3 %collective-permute-done.2.below = bf16[12,256,256]{2,1,0:T(8,128)(2,1)S(1)} collective-permute-done((bf16[12,256,256]{2,1,0:T(8,128)(2,1)}, bf16[12,256,256]{2,1,0:T(8,128)(2,1)S(1)}, u32[]{:S(2)}, u32[]{:S(2)}) %collective-permute-start.2) | collective-permute-done | bytes 1572896 | tf_op jit(solution)/shard_map/ppermute | solution.py:753
  31.2 32.9 %pair_payload.1 = (bf16[6,256,256]{2,1,0:T(8,128)(2,1)}, bf16[2,256,256]{2,1,0:T(8,128)(2,1)}) custom-call(bf16[5,256,256]{2,1,0:T(8,128)(2,1)} %get-tuple-element.41.refs_0_, bf16[5,256,256]{2,1,0:T(8,128)(2,1)} %copy-done.4), custom_call_target="tpu_custom_call" | custom-call | flops 146800640 | tf_op jit(solution)/shard_map/pair_payload/pallas_call | solution.py:179
  64.1 3.2 collective-permute-start.6
  67.3 2.1 collective-permute-start.5
  69.4 14.1 %near_own_8.1 = (f32[8,256,256]{2,1,0:T(8,128)}, bf16[22,256,256]{2,1,0:T(8,128)(2,1)}) custom-call(s32[4,4,9]{2,1,0:T(4,128)} %lists.3, f32[512,2,256]{2,1,0:T(2,128)} %bitcast.14, bf16[16,256,256]{2,1,0:T(8,128)(2,1)} %bitcast.10), custom_call_target="tpu_custom_call" | custom-call | flops 1258291200 | bytes 1048576 | tf_op jit(solution)/shard_map/near_own_8/pallas_call | solution.py:303
  84.2 144.2 %row_payload.1 = (bf16[18,256,256]{2,1,0:T(8,128)(2,1)}, bf16[12,256,256]{2,1,0:T(8,128)(2,1)}, bf16[6,256,256]{2,1,0:T(8,128)(2,1)}) custom-call(bf16[5,256,256]{2,1,0:T(8,128)(2,1)} %get-tuple-element.41.refs_0_, bf16[5,256,256]{2,1,0:T(8,128)(2,1)} %copy-done.4, bf16[6,256,256]{2,1,0:T(8,128)(2,1)} %collective-permute-done.6.refs_2_, ...), custom_call_target="tpu_custom_call" | custom-call | flops 146800640 | tf_op jit(solution)/shard_map/row_payload/pallas_call | solution.py:179
  229.1 3.4 collective-permute-start.8
  232.5 4.0 collective-permute-start.3
  236.5 2.4 collective-permute-start.4
  238.8 17.1 %far_rows.1 = (f32[2,2,2,2,256,256]{5,4,3,2,1,0:T(8,128)}, s32[16,37]{1,0:T(8,128)}) custom-call(s32[4,4,27]{2,1,0:T(4,128)} %far_zero.1, bf16[3,20,256,256]{3,2,1,0:T(8,128)(2,1)} %couplings.7, bf16[12,256,256]{2,1,0:T(8,128)(2,1)} %get-tuple-element.39.up, bf16[12,256,256]{2,1,0:T(8,128)(2,1)} %get-tuple-element.40.down, bf16[12,256,256]{2,1,0:T(8,128)(2,1)} %copy-done, ...), custom_call_target="tpu_custom_call" | custom-call | flops 1761607680 | bytes 1441792 | tf_op jit(solution)/shard_map/far_rows/pallas_call | solution.py:555
  256.1 9.0 %collective-permute-done.8.rest_2_ = bf16[12,256,256]{2,1,0:T(8,128)(2,1)} collective-permute-done((bf16[12,256,256]{2,1,0:T(8,128)(2,1)}, bf16[12,256,256]{2,1,0:T(8,128)(2,1)}, u32[]{:S(2)}, u32[]{:S(2)}) %collective-permute-start.8) | collective-permute-done | bytes 1572896 | tf_op jit(solution)/shard_map/ppermute | solution.py:786
  266.1 10.7 %upper_levels.1.down_one = bf16[4,256,256]{2,1,0:T(8,128)(2,1)} custom-call(s32[2,2,27]{2,1,0:T(2,128)} %far_one.1, s32[1,1,27]{2,1,0:T(1,128)} %far_two.1, bf16[3,20,256,256]{3,2,1,0:T(8,128)(2,1)} %couplings.7, bf16[2,2,256,256]{3,2,1,0:T(8,128)(2,1)} %t_two.3, bf16[18,256,256]{2,1,0:T(8,128)(2,1)} %get-tuple-element.56.rest_0_, ...), custom_call_target="tpu_custom_call" | custom-call | flops 1426063360 | bytes 1835008 | tf_op jit(solution)/shard_map/upper_levels/pallas_call | solution.py:429
  276.8 27.2 %collective-permute-done.3.left.refs_0_ = bf16[12,256,256]{2,1,0:T(8,128)(2,1)S(1)} collective-permute-done((bf16[12,256,256]{2,1,0:T(8,128)(2,1)}, bf16[12,256,256]{2,1,0:T(8,128)(2,1)S(1)}, u32[]{:S(2)}, u32[]{:S(2)}) %collective-permute-start.3) | collective-permute-done | bytes 1572896 | tf_op jit(solution)/shard_map/ppermute | solution.py:766
  306.4 80.6 %corner_payload.1 = (bf16[10,256,256]{2,1,0:T(8,128)(2,1)}, bf16[10,256,256]{2,1,0:T(8,128)(2,1)}) custom-call(bf16[12,256,256]{2,1,0:T(8,128)(2,1)} %copy-done.2, bf16[12,256,256]{2,1,0:T(8,128)(2,1)} %copy-done.3), custom_call_target="tpu_custom_call" | custom-call | flops 146800640 | tf_op jit(solution)/shard_map/corner_payload/pallas_call | solution.py:179
  387.0 2.3 collective-permute-start.11
  389.3 2.1 collective-permute-start.12
  391.4 14.1 %far_sides.1 = (f32[2,2,2,2,256,256]{5,4,3,2,1,0:T(8,128)}, f32[2,2,2,2,256,256]{5,4,3,2,1,0:T(8,128)}) custom-call(s32[16,37]{1,0:T(8,128)} %get-tuple-element.47.flags, bf16[3,20,256,256]{3,2,1,0:T(8,128)(2,1)} %couplings.7, f32[2,2,2,2,256,256]{5,4,3,2,1,0:T(8,128)} %get-tuple-element.62.field_in, f32[2,2,2,256,256]{4,3,2,1,0:T(8,128)} %bitcast.11, ...), custom_call_target="tpu_custom_call" | custom-call | flops 1258291200 | bytes 3932160 | tf_op jit(solution)/shard_map/far_sides/pallas_call | solution.py:639
  405.6 2.9 collective-permute-done.12.below
  409.5 12.7 %last_level.1 = bf16[2,2,2,2,256,256]{5,4,3,2,1,0:T(8,128)(2,1)} custom-call(s32[16,37]{1,0:T(8,128)} %get-tuple-element.47.flags, bf16[3,20,256,256]{3,2,1,0:T(8,128)(2,1)} %couplings.7, bf16[2,2,2,2,256,256]{5,4,3,2,1,0:T(8,128)(2,1)} %bitcast.8, bf16[2,2,2,2,256,256]{5,4,3,2,1,0:T(8,128)(2,1)} %bitcast.7, bf16[4,256,256]{2,1,0:T(8,128)(2,1)} %upper_levels.1.down_one, ...), custom_call_target="tpu_custom_call" | custom-call | flops 1132462080 | bytes 2621440 | tf_op jit(solution)/shard_map/last_level/pallas_call | solution.py:701
  (32 shorter events, 6.2 us)
Async XLA Ops:
  5.5 21.4 %collective-permute-start.1 = (bf16[12,256,256]{2,1,0:T(8,128)(2,1)}, bf16[12,256,256]{2,1,0:T(8,128)(2,1)S(1)}, u32[]{:S(2)}, u32[]{:S(2)}) collective-permute-start(bf16[12,256,256]{2,1,0:T(8,128)(2,1)} %get-tuple-element.40.down), channel_id=1, source_target_pairs={{0,8},{8,16},{16,24},{1,9},{9,17},{17,25},{2,10},{10,18},{18,26},{... | collective-permute-start | bytes 4718600 | tf_op jit(solution)/shard_map/ppermute | solution.py:752
  9.2 21.9 %collective-permute-start.2 = (bf16[12,256,256]{2,1,0:T(8,128)(2,1)}, bf16[12,256,256]{2,1,0:T(8,128)(2,1)S(1)}, u32[]{:S(2)}, u32[]{:S(2)}) collective-permute-start(bf16[12,256,256]{2,1,0:T(8,128)(2,1)} %get-tuple-element.39.up), channel_id=1, source_target_pairs={{8,0},{16,8},{24,16},{9,1},{17,9},{25,17},{10,2},{18,10},{26,18},{... | collective-permute-start | bytes 4718600 | tf_op jit(solution)/shard_map/ppermute | solution.py:753
  11.1 15.5 %collective-permute-start = (bf16[5,256,256]{2,1,0:T(8,128)(2,1)}, bf16[5,256,256]{2,1,0:T(8,128)(2,1)S(1)}, u32[]{:S(2)}, u32[]{:S(2)}) collective-permute-start(bf16[5,256,256]{2,1,0:T(8,128)(2,1)} %get-tuple-element.41.refs_0_), channel_id=1, source_target_pairs={{0,1},{1,0},{2,3},{3,2},{4,5},{5,4},{6,7},{7,6},{8,9},{9,8},{10,11... | collective-permute-start | bytes 1966088 | tf_op jit(solution)/shard_map/ppermute | solution.py:754
  26.6 4.5 %copy-start.4 = (bf16[5,256,256]{2,1,0:T(8,128)(2,1)}, bf16[5,256,256]{2,1,0:T(8,128)(2,1)S(1)}, u32[]{:S(2)}) copy-start(bf16[5,256,256]{2,1,0:T(8,128)(2,1)S(1)} %collective-permute-done.refs_1_) | copy-start | bytes 1966084
  26.9 56.6 %copy-start = (bf16[12,256,256]{2,1,0:T(8,128)(2,1)}, bf16[12,256,256]{2,1,0:T(8,128)(2,1)S(1)}, u32[]{:S(2)}) copy-start(bf16[12,256,256]{2,1,0:T(8,128)(2,1)S(1)} %collective-permute-done.1.above) | copy-start | bytes 4718596
  31.2 52.3 %copy-start.1 = (bf16[12,256,256]{2,1,0:T(8,128)(2,1)}, bf16[12,256,256]{2,1,0:T(8,128)(2,1)S(1)}, u32[]{:S(2)}) copy-start(bf16[12,256,256]{2,1,0:T(8,128)(2,1)S(1)} %collective-permute-done.2.below) | copy-start | bytes 4718596
  64.1 19.4 %collective-permute-start.6 = (bf16[6,256,256]{2,1,0:T(8,128)(2,1)}, bf16[6,256,256]{2,1,0:T(8,128)(2,1)}, u32[]{:S(2)}, u32[]{:S(2)}) collective-permute-start(bf16[6,256,256]{2,1,0:T(8,128)(2,1)} %get-tuple-element.52), channel_id=1, source_target_pairs={{0,2},{2,4},{4,6},{3,1},{5,3},{7,5},{8,10},{10,12},{12,14},{11,9},... | collective-permute-start | bytes 2359304 | tf_op jit(solution)/shard_map/ppermute | solution.py:768
  67.3 16.2 %collective-permute-start.5 = (bf16[2,256,256]{2,1,0:T(8,128)(2,1)}, bf16[2,256,256]{2,1,0:T(8,128)(2,1)S(1)}, u32[]{:S(2)}, u32[]{:S(2)}) collective-permute-start(bf16[2,256,256]{2,1,0:T(8,128)(2,1)} %get-tuple-element.51), channel_id=1, source_target_pairs={{2,0},{4,2},{6,4},{1,3},{3,5},{5,7},{10,8},{12,10},{14,12},{9,11},... | collective-permute-start | bytes 786440 | tf_op jit(solution)/shard_map/ppermute | solution.py:769
  83.5 0.7 copy-start.9
  228.4 37.7 %collective-permute-start.7 = (bf16[18,256,256]{2,1,0:T(8,128)(2,1)}, bf16[18,256,256]{2,1,0:T(8,128)(2,1)}, u32[]{:S(2)}, u32[]{:S(2)}) collective-permute-start(bf16[18,256,256]{2,1,0:T(8,128)(2,1)} %get-tuple-element.56.rest_0_), channel_id=1, source_target_pairs={{0,8},{8,0},{16,24},{24,16},{1,9},{9,1},{17,25},{25,17},{2,10},{10... | collective-permute-start | bytes 7077896 | tf_op jit(solution)/shard_map/ppermute | solution.py:787
  228.4 27.6 %collective-permute-start.9 = (bf16[6,256,256]{2,1,0:T(8,128)(2,1)}, bf16[6,256,256]{2,1,0:T(8,128)(2,1)S(1)}, u32[]{:S(2)}, u32[]{:S(2)}) collective-permute-start(bf16[6,256,256]{2,1,0:T(8,128)(2,1)} %get-tuple-element.58), channel_id=1, source_target_pairs={{0,16},{8,24},{16,0},{24,8},{1,17},{9,25},{17,1},{25,9},{2,18},{10... | collective-permute-start | bytes 2359304 | tf_op jit(solution)/shard_map/ppermute | solution.py:780
  229.1 36.1 %collective-permute-start.8 = (bf16[12,256,256]{2,1,0:T(8,128)(2,1)}, bf16[12,256,256]{2,1,0:T(8,128)(2,1)}, u32[]{:S(2)}, u32[]{:S(2)}) collective-permute-start(bf16[12,256,256]{2,1,0:T(8,128)(2,1)} %get-tuple-element.57), channel_id=1, source_target_pairs={{8,16},{16,8},{9,17},{17,9},{10,18},{18,10},{11,19},{19,11},{12,20... | collective-permute-start | bytes 4718600 | tf_op jit(solution)/shard_map/ppermute | solution.py:786
  232.5 71.5 %collective-permute-start.3 = (bf16[12,256,256]{2,1,0:T(8,128)(2,1)}, bf16[12,256,256]{2,1,0:T(8,128)(2,1)S(1)}, u32[]{:S(2)}, u32[]{:S(2)}) collective-permute-start(bf16[12,256,256]{2,1,0:T(8,128)(2,1)} %get-tuple-element.48), channel_id=1, source_target_pairs={{0,1},{1,2},{2,3},{3,4},{4,5},{5,6},{6,7},{8,9},{9,10},{10,11},{11... | collective-permute-start | bytes 4718600 | tf_op jit(solution)/shard_map/ppermute | solution.py:766
  236.5 68.3 %collective-permute-start.4 = (bf16[12,256,256]{2,1,0:T(8,128)(2,1)}, bf16[12,256,256]{2,1,0:T(8,128)(2,1)S(1)}, u32[]{:S(2)}, u32[]{:S(2)}) collective-permute-start(bf16[12,256,256]{2,1,0:T(8,128)(2,1)} %get-tuple-element.49), channel_id=1, source_target_pairs={{1,0},{2,1},{3,2},{4,3},{5,4},{6,5},{7,6},{9,8},{10,9},{11,10},{12... | collective-permute-start | bytes 4718600 | tf_op jit(solution)/shard_map/ppermute | solution.py:767
  256.0 10.1 %copy-start.7 = (bf16[6,256,256]{2,1,0:T(8,128)(2,1)}, bf16[6,256,256]{2,1,0:T(8,128)(2,1)S(1)}, u32[]{:S(2)}) copy-start(bf16[6,256,256]{2,1,0:T(8,128)(2,1)S(1)} %collective-permute-done.9.rest_3_) | copy-start | bytes 2359300
  256.0 9.1 %collective-permute-start.10 = (bf16[6,256,256]{2,1,0:T(8,128)(2,1)S(1)}, bf16[6,256,256]{2,1,0:T(8,128)(2,1)S(1)}, u32[]{:S(2)}, u32[]{:S(2)}) collective-permute-start(bf16[6,256,256]{2,1,0:T(8,128)(2,1)S(1)} %collective-permute-done.9.rest_3_), channel_id=1, source_target_pairs={{0,8},{8,0},{16,24},{24,16},{1,9},{9,1},{17,25},{25,17},{2,10},{10... | collective-permute-start | bytes 2359304 | tf_op jit(solution)/shard_map/ppermute | solution.py:790
  265.1 1.0 copy-start.8
  304.0 1.2 copy-start.2
  305.2 1.2 copy-start.3
  387.0 18.6 %collective-permute-start.11 = (bf16[10,256,256]{2,1,0:T(8,128)(2,1)}, bf16[10,256,256]{2,1,0:T(8,128)(2,1)S(1)}, u32[]{:S(2)}, u32[]{:S(2)}) collective-permute-start(bf16[10,256,256]{2,1,0:T(8,128)(2,1)} %get-tuple-element.71), channel_id=1, source_target_pairs={{0,8},{8,16},{16,24},{1,9},{9,17},{17,25},{2,10},{10,18},{18,26},{... | collective-permute-start | bytes 3932168 | tf_op jit(solution)/shard_map/ppermute | solution.py:804
  389.3 19.1 %collective-permute-start.12 = (bf16[10,256,256]{2,1,0:T(8,128)(2,1)}, bf16[10,256,256]{2,1,0:T(8,128)(2,1)S(1)}, u32[]{:S(2)}, u32[]{:S(2)}) collective-permute-start(bf16[10,256,256]{2,1,0:T(8,128)(2,1)} %get-tuple-element.72), channel_id=1, source_target_pairs={{8,0},{16,8},{24,16},{9,1},{17,9},{25,17},{10,2},{18,10},{26,18},{... | collective-permute-start | bytes 3932168 | tf_op jit(solution)/shard_map/ppermute | solution.py:805
  405.6 2.9 copy-start.5
  408.4 1.1 copy-start.6

commit v4 on v3

--- a/solution.py
+++ b/solution.py
@@ -162,26 +162,34 @@
     )(samples, basis, t_one, t_two)
 
 
-def assembled(name, sources, plans):
-    sizes = [sum(n for _, _, n in plan) for plan in plans]
-    count = sum(len(plan) for plan in plans)
+def assembled(name, sources, pieces, ranges):
+    count = sum(n for _, _, n in pieces)
 
     def kernel(*refs):
-        ins, outs, sems = refs[: len(sources)], refs[len(sources) : -1], refs[-1]
-        copies = Copies(sems)
-        for plan, out in zip(plans, outs):
-            at = 0
-            for source, first, n in plan:
-                copies.start(ins[source].at[first : first + n], out.at[at : at + n])
-                at += n
-        copies.wait()
+        ins, outs = refs[: len(sources)], refs[len(sources) : -3]
+        held, in_sems, out_sems = refs[-3:]
+        into = Copies(in_sems)
+        at = 0
+        for source, first, n in pieces:
+            into.start(ins[source].at[first : first + n], held.at[at : at + n])
+            at += n
+        into.wait()
+        out = Copies(out_sems)
+        for (first, last), ref in zip(ranges, outs):
+            out.start(held.at[first:last], ref)
+        out.wait()
 
     return pl.pallas_call(
         kernel,
-        out_shape=[tiles(n) for n in sizes],
+        out_shape=[tiles(last - first) for first, last in ranges],
         in_specs=[ANY_SPEC] * len(sources),
-        out_specs=[ANY_SPEC] * len(plans),
-        scratch_shapes=[pltpu.SemaphoreType.DMA((count,))],
+        out_specs=[ANY_SPEC] * len(ranges),
+        scratch_shapes=[
+            VMEM((count, 256, 256), BF16),
+            pltpu.SemaphoreType.DMA((len(pieces),)),
+            pltpu.SemaphoreType.DMA((len(ranges),)),
+        ],
+        compiler_params=params(),
         cost_estimate=cost(35, 0),
         name=name,
     )(*sources)
@@ -234,7 +242,7 @@
 
 def near_kernel(
     first, grid_rows, grid_cols, lists, positions, own, near, halo_out,
-    held, target_feat, source_feat, halo, floors, sems, halo_sems,
+    held, target_feat, source_feat, halo, made_a, made_b, floors_a, floors_b, sems, halo_sems,
 ):
     copy = pltpu.make_async_copy(own, held.at[0:16], sems.at[0])
     copy.start()
@@ -260,10 +268,9 @@
     lax.fori_loop(0, 24, features, 0)
     copy.wait()
 
-    def one_target(m, carry):
-        t = first + m
-        r = t // 4
-        c = t % 4
+    def make(m, made, floors):
+        r = (first + m) // 4
+        c = (first + m) % 4
         row = first_row + r
         col = first_col + c
         for k in range(9):
@@ -276,8 +283,6 @@
             floors[jnp.where(entry >= 0, k, 9)] = 1e-24
         place = (m // 4 + 1) * 6 + c + 1
         target = target_feat[place].T.astype(BF16)
-        made = []
-        blocks = []
         for k in range(9):
             dr, dc = k // 3 - 1, k % 3 - 1
             square = nn(target, source_feat[place + dr * 6 + dc])
@@ -286,12 +291,31 @@
             tile = ((far + 1.0) * jnp.exp2(far * -LOG2E)).astype(BF16)
             inside = (r + dr >= 0) & (r + dr < 4) & (c + dc >= 0) & (c + dc < 4)
             halo[jnp.where(inside, 72, m * 9 + k)] = tile
-            made.append(tile)
+            made[k] = tile
+
+    def use(m, made):
+        r = (first + m) // 4
+        c = (first + m) % 4
+        blocks = []
+        for k in range(9):
+            dr, dc = k // 3 - 1, k % 3 - 1
+            inside = (r + dr >= 0) & (r + dr < 4) & (c + dc >= 0) & (c + dc < 4)
             blocks.append(held[jnp.where(inside, (r + dr) * 4 + c + dc, 16)])
-        near[m] = nn(jnp.concatenate(made, axis=1), jnp.concatenate(blocks, axis=0))
+        lhs = jnp.concatenate([made[k] for k in range(9)], axis=1)
+        near[m] = nn(lhs, jnp.concatenate(blocks, axis=0))
+
+    def two_targets(n, carry):
+        use(2 * n, made_a)
+        make(2 * n + 1, made_b, floors_b)
+        use(2 * n + 1, made_b)
+        make(2 * n + 2, made_a, floors_a)
         return carry
 
-    lax.fori_loop(0, 8, one_target, 0)
+    make(0, made_a, floors_a)
+    lax.fori_loop(0, 3, two_targets, 0)
+    use(6, made_a)
+    make(7, made_b, floors_b)
+    use(7, made_b)
     out = Copies(halo_sems)
     for (t, k), number in HALO.items():
         if first <= t < first + 8:
@@ -310,6 +334,9 @@
             VMEM((24, 32, 256), F32),
             VMEM((24, 32, 256), BF16),
             VMEM((73, 256, 256), BF16),
+            VMEM((9, 256, 256), BF16),
+            VMEM((9, 256, 256), BF16),
+            pltpu.SMEM((10,), F32),
             pltpu.SMEM((10,), F32),
             pltpu.SemaphoreType.DMA((1,)),
             pltpu.SemaphoreType.DMA((N_HALO,)),
@@ -456,15 +483,13 @@
 
 def source_of(x, y, w):
     r, c = 2 * x + w // 6, 2 * y + w % 6
-    rows_in, cols_in = 2 <= r < 6, 2 <= c < 6
-    if cols_in:
-        return "rows", r * 4 + c - 2
-    if rows_in:
-        return "sides", (0 if c < 2 else 8) + (r - 2) * 2 + (c if c < 2 else c - 6)
-    base = 0 if r < 2 else 8
-    return "corners", base + (0 if c < 2 else 4) + (r if r < 2 else r - 6) * 2 + (
-        c if c < 2 else c - 6
-    )
+    if 2 <= c < 6:
+        return "inner", r * 4 + c - 2
+    side = 0 if c < 2 else 1
+    c = c if c < 2 else c - 6
+    if 2 <= r < 6:
+        return "outer", side * 8 + (r - 2) * 2 + c
+    return "outer", (16 if r < 2 else 24) + side * 4 + (r if r < 2 else r - 6) * 2 + c
 
 
 PARENTS = [(x, y) for x in range(2) for y in range(2)]
@@ -544,7 +569,7 @@
         copies.wait()
 
     def body(a, b):
-        sums = level_zero_sums("rows", a, b, flags, couplings.at[0], held, 32)
+        sums = level_zero_sums("inner", a, b, flags, couplings.at[0], held, 32)
         for x, y in PARENTS:
             field[x, 0, y, 0] = sums[x, y]
 
@@ -565,44 +590,39 @@
     )(far_zero, couplings, up, down, above, below)
 
 
-def near_source(r, c):
+def near_place(r, c):
     rows_in, cols_in = 1 <= r < 5, 1 <= c < 5
-    if rows_in and cols_in:
-        return "own", None
     if rows_in:
-        return "side", (0 if c == 0 else 4) + r - 1
+        return (0 if c == 0 else 4) + r - 1
     if cols_in:
-        return "side", (8 if r == 0 else 12) + c - 1
-    return "corner", (0 if r == 0 else 2) + (0 if c == 0 else 1)
-
-
-def near_part(kind, t, tile_of, held):
+        return (8 if r == 0 else 12) + c - 1
+    return 16 + (0 if r == 0 else 2) + (0 if c == 0 else 1)
+
+
+def near_part(t, halo, held):
     r, c = t // 4, t % 4
-    made, blocks = [], []
-    for k in range(9):
-        found, place = near_source(r + k // 3, c + k % 3)
-        if found == kind:
-            made.append(tile_of(HALO[t, k]))
-            blocks.append(held[place])
-    if not made:
+    found = [k for k in range(9) if (t, k) in HALO]
+    if not found:
         return None
-    return nn(jnp.concatenate(made, axis=1), jnp.concatenate(blocks, axis=0))
-
-
-SIDE_HALO = [n for (t, k), n in HALO.items() if near_source(t // 4 + k // 3, t % 4 + k % 3)[0] == "side"]
-CORNER_HALO = [n for n in range(2 * N_HALO) if n not in SIDE_HALO]
-
-
-def sides_kernel(
-    flags, couplings, field_in, near_a, near_b, halo_a, halo_b, left, right, above, below,
-    field, near, held, near_held, halo, sems,
+    lhs = jnp.concatenate([halo[HALO[t, k]] for k in found], axis=1)
+    rhs = jnp.concatenate([held[near_place(r + k // 3, c + k % 3)] for k in found], axis=0)
+    return nn(lhs, rhs)
+
+
+def outer_kernel(
+    flags, couplings, t_one, basis, down_one, field, near_a, near_b, halo_a, halo_b,
+    left, right, above, below, corner_above, corner_below, out, held, near_held, halo, sems,
 ):
     step = pl.program_id(0)
 
     def copies():
-        pairs = [(left.at[0:8], held.at[0:8]), (right.at[0:8], held.at[8:16])]
+        pairs = []
+        for n, src in enumerate((left, right, corner_above, corner_below)):
+            pairs.append((src.at[0:8], held.at[8 * n : 8 * n + 8]))
         for n, src in enumerate((left, right, above, below)):
             pairs.append((src.at[8:12], near_held.at[4 * n : 4 * n + 4]))
+        pairs.append((corner_above.at[8:10], near_held.at[16:18]))
+        pairs.append((corner_below.at[8:10], near_held.at[18:20]))
         pairs.append((halo_a, halo.at[0:N_HALO]))
         pairs.append((halo_b, halo.at[N_HALO : 2 * N_HALO]))
         return [pltpu.make_async_copy(src, dst, sems.at[n]) for n, (src, dst) in enumerate(pairs)]
@@ -612,21 +632,24 @@
         started = copies()
         for copy in started:
             copy.start()
-        held[16] = jnp.zeros((256, 256), BF16)
-        for copy in started[:2]:
+        held[32] = jnp.zeros((256, 256), BF16)
+        for copy in started[:4]:
             copy.wait()
 
     def body(a, b):
-        sums = level_zero_sums("sides", a, b, flags, couplings.at[0], held, 16)
-        for x, y in PARENTS:
-            field[x, 0, y, 0] = field_in[x, 0, y, 0] + sums[x, y]
+        sums = level_zero_sums("outer", a, b, flags, couplings.at[0], held, 32)
         if a == 0 and b == 0:
-            for copy in copies()[2:]:
+            for copy in copies()[4:]:
                 copy.wait()
         for x, y in PARENTS:
-            part = near_part("side", number_of(a, b, (x, y)), lambda n: halo[n], near_held)
-            here = (near_b if x else near_a)[0, y, 0]
-            near[x, 0, y, 0] = here if part is None else here + part
+            total = field[x, 0, y, 0] + sums[x, y]
+            total = total + nt(down_one[x * 2 + y], t_one[x, 0, y, 0])
+            far = nt(basis[x, 0, y, 0], total.astype(BF16))
+            near = (near_b if x else near_a)[0, y, 0]
+            part = near_part(number_of(a, b, (x, y)), halo, near_held)
+            if part is not None:
+                near = near + part
+            out[x, 0, y, 0] = (near * TILE_SCALE + far).astype(BF16)
 
     each_class(step, body)
 
@@ -634,72 +657,12 @@
 HALF_BLOCK = pl.BlockSpec((1, 2, 1, 256, 256), lambda g: (g // 2, 0, g % 2, 0, 0))
 
 
-def sides_level(flags, couplings, field, near_a, near_b, halo_a, halo_b, left, right, above, below):
+def outer_level(
+    flags, couplings, t_one, basis, down_one, field, near_a, near_b, halo_a, halo_b, *received
+):
     half = lambda x: x.reshape(2, 2, 2, 256, 256)
     return pl.pallas_call(
-        sides_kernel,
-        grid=(4,),
-        out_shape=(GROUPED_F32, GROUPED_F32),
-        in_specs=[SMEM_SPEC, COUPLING_BLOCK, CLASS_BLOCK, HALF_BLOCK, HALF_BLOCK] + [ANY_SPEC] * 6,
-        out_specs=[CLASS_BLOCK, CLASS_BLOCK],
-        scratch_shapes=[
-            VMEM((17, 256, 256), BF16),
-            VMEM((16, 256, 256), BF16),
-            VMEM((2 * N_HALO, 256, 256), BF16),
-            pltpu.SemaphoreType.DMA((8,)),
-        ],
-        compiler_params=params(),
-        cost_estimate=cost(300, 30 << 20),
-        name="far_sides",
-    )(
-        flags, couplings, field, half(near_a), half(near_b), halo_a, halo_b, left, right, above, below
-    )
-
-
-def last_kernel(
-    flags, couplings, t_one, basis, down_one, field, near, halo_a, halo_b, above, below, out,
-    held, near_held, halo, sems,
-):
-    step = pl.program_id(0)
-
-    @pl.when(step == 0)
-    def _():
-        copies = Copies(sems)
-        copies.start(above.at[0:8], held.at[0:8])
-        copies.start(below.at[0:8], held.at[8:16])
-        copies.start(above.at[8:10], near_held.at[0:2])
-        copies.start(below.at[8:10], near_held.at[2:4])
-        for m, n in enumerate(CORNER_HALO):
-            copies.start((halo_a if n < N_HALO else halo_b).at[n % N_HALO], halo.at[m])
-        held[16] = jnp.zeros((256, 256), BF16)
-        copies.wait()
-
-    def body(a, b):
-        sums = level_zero_sums("corners", a, b, flags, couplings.at[0], held, 16)
-        for x, y in PARENTS:
-            total = field[x, 0, y, 0] + nt(down_one[x * 2 + y], t_one[x, 0, y, 0])
-            if (x, y) in sums:
-                total = total + sums[x, y]
-            far = nt(basis[x, 0, y, 0], total.astype(BF16))
-            near_sum = near[x, 0, y, 0]
-            part = near_part(
-                "corner",
-                number_of(a, b, (x, y)),
-                lambda n: halo[CORNER_HALO.index(n)],
-                near_held,
-            )
-            if part is not None:
-                near_sum = near_sum + part
-            out[x, 0, y, 0] = (near_sum * TILE_SCALE + far).astype(BF16)
-
-    each_class(step, body)
-
-
-def last_level(
-    flags, couplings, t_one, basis, down_one, field, near, halo_a, halo_b, above, below
-):
-    return pl.pallas_call(
-        last_kernel,
+        outer_kernel,
         grid=(4,),
         out_shape=jax.ShapeDtypeStruct((2, 2, 2, 2, 256, 256), BF16),
         in_specs=[
@@ -709,22 +672,23 @@
             CLASS_BLOCK,
             pl.BlockSpec((4, 256, 256), lambda g: (0, 0, 0)),
             CLASS_BLOCK,
-            CLASS_BLOCK,
+            HALF_BLOCK,
+            HALF_BLOCK,
         ]
-        + [ANY_SPEC] * 4,
+        + [ANY_SPEC] * 8,
         out_specs=CLASS_BLOCK,
         scratch_shapes=[
-            VMEM((17, 256, 256), BF16),
-            VMEM((4, 256, 256), BF16),
-            VMEM((len(CORNER_HALO), 256, 256), BF16),
-            pltpu.SemaphoreType.DMA((4 + len(CORNER_HALO),)),
+            VMEM((33, 256, 256), BF16),
+            VMEM((20, 256, 256), BF16),
+            VMEM((2 * N_HALO, 256, 256), BF16),
+            pltpu.SemaphoreType.DMA((12,)),
         ],
         compiler_params=params(),
-        cost_estimate=cost(270, 20 << 20),
-        name="last_level",
+        cost_estimate=cost(500, 34 << 20),
+        name="leaf_outer",
     )(
-        flags, couplings, grouped(t_one), grouped(basis), down_one, field, near, halo_a, halo_b,
-        above, below,
+        flags, couplings, grouped(t_one), grouped(basis), down_one, field, half(near_a),
+        half(near_b), halo_a, halo_b, *received,
     )
 
 
@@ -761,7 +725,7 @@
     outward = [(k, k + 2) for k in range(0, ny - 2, 2)] + [(k + 2, k) for k in range(1, ny - 2, 2)]
     inward = [(k + 2, k) for k in range(0, ny - 2, 2)] + [(k, k + 2) for k in range(1, ny - 2, 2)]
     to_out, to_in = assembled(
-        "pair_payload", (upper, pair), [[(1, 0, 5), (0, 4, 1)], [(0, 4, 1), (1, 4, 1)]]
+        "pair_payload", (upper, pair), [(1, 0, 5), (0, 4, 1)], [(0, 6), (4, 6)]
     )
     on_left = lax.ppermute(right, "qy", down_y)
     on_right = lax.ppermute(left, "qy", up_y)
@@ -769,10 +733,12 @@
     inner = lax.ppermute(to_in, "qy", inward)
     near_b, halo_b = near_own(8, 4 * nx, 4 * ny, near_lists, sites, flat_samples)
     inner, outer, near_b = lax.optimization_barrier((inner, outer, near_b))
-    cells = [(0, 4, 1), (1, 4, 1), (2, 5, 1), (2, 4, 1), (3, 0, 2)]
-    ones = [(0, 0, 4), (1, 0, 4), (2, 0, 4)]
     row, one_row, two_row = assembled(
-        "row_payload", (upper, pair, outer, inner), [ones + cells, ones, cells]
+        "row_payload",
+        (upper, pair, outer, inner),
+        [(0, 0, 4), (1, 0, 4), (2, 0, 4)]
+        + [(0, 4, 1), (1, 4, 1), (2, 5, 1), (2, 4, 1), (3, 1, 1), (3, 0, 1)],
+        [(0, 18), (0, 12), (12, 18)],
     )
     swap_x = [(k, k ^ 1) for k in range(nx)]
     cross_x = [(k, k + 1) for k in range(1, nx - 1, 2)] + [(k + 1, k) for k in range(1, nx - 1, 2)]
@@ -788,34 +754,35 @@
     field, flags = rows_level(4 * ny, far_zero, couplings, up, down, above, below)
     others, field = lax.optimization_barrier((others, field))
     others = others + [lax.ppermute(x, "qx", swap_x) for x in others]
-    down_one = upper_levels(
-        ny, far_one, far_two, couplings, transfer_two, row, row_e, row_d, others
-    )
-
-    on_left, on_right, down_one = lax.optimization_barrier((on_left, on_right, down_one))
+    on_left, on_right, others = lax.optimization_barrier((on_left, on_right, others))
+
     corner_down, corner_up = assembled(
         "corner_payload",
         (on_left, on_right),
-        [
-            [(0, 4, 4), (1, 4, 4), (0, 11, 1), (1, 11, 1)],
-            [(0, 0, 4), (1, 0, 4), (0, 8, 1), (1, 8, 1)],
-        ],
+        [(0, 4, 4), (1, 4, 4), (0, 11, 1), (1, 11, 1)]
+        + [(0, 0, 4), (1, 0, 4), (0, 8, 1), (1, 8, 1)],
+        [(0, 10), (10, 20)],
     )
     corner_above = lax.ppermute(corner_down, "qx", down_x)
     corner_below = lax.ppermute(corner_up, "qx", up_x)
-    field, near = sides_level(
-        flags, couplings, field, near_a, near_b, halo_a, halo_b, on_left, on_right, above, below
-    )
-    result = last_level(
+    down_one = upper_levels(
+        ny, far_one, far_two, couplings, transfer_two, row, row_e, row_d, others
+    )
+    result = outer_level(
         flags,
         couplings,
         transfer_one,
         leaf_basis,
         down_one,
         field,
-        near,
+        near_a,
+        near_b,
         halo_a,
         halo_b,
+        on_left,
+        on_right,
+        above,
+        below,
         corner_above,
         corner_below,
     )

time: 424 us -> 179 us (0.42)
  Pallas kernels: 346 us -> 88.2 us
  waiting for transfers between devices: 44.5 us -> 56.6 us
    pallas_call x5 -> x4, Pallas kernels: 285 us -> 29.7 us  [the longest x1 19.9 us: outer_level(): pl.pallas_call(outer_kernel, grid=(4,), out_shape=jax.ShapeDtypeStruct((2...]
    ppermute x1, waiting for transfers between devices: 27.2 us -> 40.3 us  [per_device(): on_left = lax.ppermute(right, 'qy', down_y)]
    ppermute x1, waiting for transfers between devices: 9.04 us -> 0.01 us  [per_device(): row_d = lax.ppermute(one_row, 'qx', cross_x)]
    ppermute x1, waiting for transfers between devices: 4.29 us -> 0.01 us  [per_device(): below = lax.ppermute(up, 'qx', up_x)]
  transfers between devices with their start and end apart: 13 -> 13, of which waited for: 6 -> 7; matrix products, arithmetic and copies ran while one was open for 0% -> 0% of each run, Pallas kernels for 17% -> 32%
where the time goes in v4:
time: 179 us
  Pallas kernels  88.2 us (49%)
  waiting for transfers between devices  56.6 us (32%)
  starting transfers between devices  30.2 us (17%)
  local copies, waits for them, and re-layouts  3.3 us (2%)
    ppermute x1, waiting for transfers between devices, per_device(): on_left = lax.ppermute(right, 'qy', down_y)  40.3 us
    pallas_call x2, Pallas kernels, near_own(): pl.pallas_call(functools.partial(near_kernel, first, grid_rows, grid_cols...  25.4 us
    pallas_call x1, Pallas kernels, outer_level(): pl.pallas_call(outer_kernel, grid=(4,), out_shape=jax.ShapeDtypeStruct((2...  19.9 us
    pallas_call x1, Pallas kernels, rows_level(): pl.pallas_call(functools.partial(rows_kernel, grid_cols), grid=(4,), out_...  17.1 us
    pallas_call x1, Pallas kernels, upper_levels(): pl.pallas_call(functools.partial(upper_kernel, grid_cols, n_others), grid...  10.7 us
    pallas_call x3, Pallas kernels, assembled(): pl.pallas_call(kernel, out_shape=[tiles(last - first) for first, last in...  9.76 us
    pallas_call x1, Pallas kernels, coefficients(): pl.pallas_call(coef_kernel, out_shape=(tiles(12), tiles(12), tiles(12), t...  5.4 us
    ppermute x1, waiting for transfers between devices, per_device(): corner_below = lax.ppermute(corner_up, 'qx', up_x)  4.29 us
  transfers between devices with their start and end apart: 13, of which 7 were waited for; matrix products, arithmetic and copies ran while one was open for 0% of the time, Pallas kernels for 32%

profile of v4, /device:TPU:17, one launch (start us, length us, event | category | flops | bytes accessed | tf_op | source)
XLA Modules:
  0.0 178.7 jit_solution(6317815118561149783)
XLA Ops:
  0.0 5.4 %coefficients.1 = (bf16[12,256,256]{2,1,0:T(8,128)(2,1)}, bf16[12,256,256]{2,1,0:T(8,128)(2,1)}, bf16[12,256,256]{2,1,0:T(8,128)(2,1)}, bf16[12,256,256]{2,1,0:T(8,128)(2,1)}, bf16[5,256,256]{2,1,0:T(8,128)(2,1)}) custom-call(bf16[4,4,256,256]{3,2,1,0:T(8,128)(2,1)} %samples.1, bf16[4,4,256,256]{3,2,1,0:T(8,128)(2,1)} %basis.1, ...), custom_call_target="tpu_custom_call" | custom-call | flops 713031680 | bytes 1572864 | tf_op jit(solution)/shard_map/coefficients/pallas_call | solution.py:144
  5.4 2.6 %collective-permute-start.2 = (bf16[12,256,256]{2,1,0:T(8,128)(2,1)}, bf16[12,256,256]{2,1,0:T(8,128)(2,1)S(1)}, u32[]{:S(2)}, u32[]{:S(2)}) collective-permute-start(bf16[12,256,256]{2,1,0:T(8,128)(2,1)} %get-tuple-element.38.up), channel_id=1, source_target_pairs={{8,0},{16,8},{24,16},{9,1},{17,9},{25,17},{10,2},{18,10},{26,18},{... | collective-permute-start | bytes 4718600 | tf_op jit(solution)/shard_map/ppermute | solution.py:717
  8.0 3.0 %collective-permute-start.1 = (bf16[12,256,256]{2,1,0:T(8,128)(2,1)}, bf16[12,256,256]{2,1,0:T(8,128)(2,1)S(1)}, u32[]{:S(2)}, u32[]{:S(2)}) collective-permute-start(bf16[12,256,256]{2,1,0:T(8,128)(2,1)} %get-tuple-element.39.down), channel_id=1, source_target_pairs={{0,8},{8,16},{16,24},{1,9},{9,17},{17,25},{2,10},{10,18},{18,26},{... | collective-permute-start | bytes 4718600 | tf_op jit(solution)/shard_map/ppermute | solution.py:716
  12.3 12.5 %near_own_0.1 = (f32[8,256,256]{2,1,0:T(8,128)}, bf16[22,256,256]{2,1,0:T(8,128)(2,1)}) custom-call(s32[4,4,9]{2,1,0:T(4,128)} %lists.3, f32[512,2,256]{2,1,0:T(2,128)} %bitcast.13, bf16[16,256,256]{2,1,0:T(8,128)(2,1)} %bitcast.11), custom_call_target="tpu_custom_call" | custom-call | flops 1258291200 | bytes 1048576 | tf_op jit(solution)/shard_map/near_own_0/pallas_call | solution.py:327
  24.8 3.1 %collective-permute-done.refs_1_ = bf16[5,256,256]{2,1,0:T(8,128)(2,1)S(1)} collective-permute-done((bf16[5,256,256]{2,1,0:T(8,128)(2,1)}, bf16[5,256,256]{2,1,0:T(8,128)(2,1)S(1)}, u32[]{:S(2)}, u32[]{:S(2)}) %collective-permute-start) | collective-permute-done | bytes 655392 | tf_op jit(solution)/shard_map/ppermute | solution.py:718
  28.8 2.6 %pair_payload.1 = (bf16[6,256,256]{2,1,0:T(8,128)(2,1)}, bf16[2,256,256]{2,1,0:T(8,128)(2,1)}) custom-call(bf16[5,256,256]{2,1,0:T(8,128)(2,1)} %get-tuple-element.40.refs_0_, bf16[5,256,256]{2,1,0:T(8,128)(2,1)} %copy-done.4), custom_call_target="tpu_custom_call" | custom-call | flops 146800640 | tf_op jit(solution)/shard_map/pair_payload/pallas_call | solution.py:182
  31.4 3.2 %collective-permute-start.4 = (bf16[6,256,256]{2,1,0:T(8,128)(2,1)}, bf16[6,256,256]{2,1,0:T(8,128)(2,1)S(1)}, u32[]{:S(2)}, u32[]{:S(2)}) collective-permute-start(bf16[6,256,256]{2,1,0:T(8,128)(2,1)} %get-tuple-element.49), channel_id=1, source_target_pairs={{0,2},{2,4},{4,6},{3,1},{5,3},{7,5},{8,10},{10,12},{12,14},{11,9},... | collective-permute-start | bytes 2359304 | tf_op jit(solution)/shard_map/ppermute | solution.py:732
  34.6 2.1 %collective-permute-start.3 = (bf16[2,256,256]{2,1,0:T(8,128)(2,1)}, bf16[2,256,256]{2,1,0:T(8,128)(2,1)}, u32[]{:S(2)}, u32[]{:S(2)}) collective-permute-start(bf16[2,256,256]{2,1,0:T(8,128)(2,1)} %get-tuple-element.48), channel_id=1, source_target_pairs={{2,0},{4,2},{6,4},{1,3},{3,5},{5,7},{10,8},{12,10},{14,12},{9,11},... | collective-permute-start | bytes 786440 | tf_op jit(solution)/shard_map/ppermute | solution.py:733
  36.7 12.9 %near_own_8.1 = (f32[8,256,256]{2,1,0:T(8,128)}, bf16[22,256,256]{2,1,0:T(8,128)(2,1)}) custom-call(s32[4,4,9]{2,1,0:T(4,128)} %lists.3, f32[512,2,256]{2,1,0:T(2,128)} %bitcast.14, bf16[16,256,256]{2,1,0:T(8,128)(2,1)} %bitcast.12), custom_call_target="tpu_custom_call" | custom-call | flops 1258291200 | bytes 1048576 | tf_op jit(solution)/shard_map/near_own_8/pallas_call | solution.py:327
  49.6 2.7 %collective-permute-done.4.refs_2_ = bf16[6,256,256]{2,1,0:T(8,128)(2,1)S(1)} collective-permute-done((bf16[6,256,256]{2,1,0:T(8,128)(2,1)}, bf16[6,256,256]{2,1,0:T(8,128)(2,1)S(1)}, u32[]{:S(2)}, u32[]{:S(2)}) %collective-permute-start.4) | collective-permute-done | bytes 786464 | tf_op jit(solution)/shard_map/ppermute | solution.py:732
  53.3 3.8 %row_payload.1 = (bf16[18,256,256]{2,1,0:T(8,128)(2,1)}, bf16[12,256,256]{2,1,0:T(8,128)(2,1)}, bf16[6,256,256]{2,1,0:T(8,128)(2,1)}) custom-call(bf16[5,256,256]{2,1,0:T(8,128)(2,1)} %get-tuple-element.40.refs_0_, bf16[5,256,256]{2,1,0:T(8,128)(2,1)} %copy-done.4, bf16[6,256,256]{2,1,0:T(8,128)(2,1)} %copy-done.7, ...), custom_call_target="tpu_custom_call" | custom-call | flops 146800640 | tf_op jit(solution)/shard_map/row_payload/pallas_call | solution.py:182
  57.2 3.1 %collective-permute-start.7 = (bf16[12,256,256]{2,1,0:T(8,128)(2,1)}, bf16[12,256,256]{2,1,0:T(8,128)(2,1)S(1)}, u32[]{:S(2)}, u32[]{:S(2)}) collective-permute-start(bf16[12,256,256]{2,1,0:T(8,128)(2,1)} %get-tuple-element.55), channel_id=1, source_target_pairs={{0,1},{1,2},{2,3},{3,4},{4,5},{5,6},{6,7},{8,9},{9,10},{10,11},{11... | collective-permute-start | bytes 4718600 | tf_op jit(solution)/shard_map/ppermute | solution.py:730
  60.3 3.2 %collective-permute-start.8 = (bf16[12,256,256]{2,1,0:T(8,128)(2,1)}, bf16[12,256,256]{2,1,0:T(8,128)(2,1)S(1)}, u32[]{:S(2)}, u32[]{:S(2)}) collective-permute-start(bf16[12,256,256]{2,1,0:T(8,128)(2,1)} %get-tuple-element.56), channel_id=1, source_target_pairs={{1,0},{2,1},{3,2},{4,3},{5,4},{6,5},{7,6},{9,8},{10,9},{11,10},{12... | collective-permute-start | bytes 4718600 | tf_op jit(solution)/shard_map/ppermute | solution.py:731
  65.4 17.1 %far_rows.1 = (f32[2,2,2,2,256,256]{5,4,3,2,1,0:T(8,128)}, s32[16,37]{1,0:T(8,128)}) custom-call(s32[4,4,27]{2,1,0:T(4,128)} %far_zero.1, bf16[3,20,256,256]{3,2,1,0:T(8,128)(2,1)} %couplings.5, bf16[12,256,256]{2,1,0:T(8,128)(2,1)} %get-tuple-element.38.up, bf16[12,256,256]{2,1,0:T(8,128)(2,1)} %get-tuple-element.39.down, bf16[12,256,256]{2,1,0:T(8,128)(2,1)} %copy-done.1, ...), custom_call_target="tpu_custom_call" | custom-call | flops 1761607680 | bytes 1441792 | tf_op jit(solution)/shard_map/far_rows/pallas_call | solution.py:580
  82.6 3.9 %collective-permute-start.6 = (bf16[12,256,256]{2,1,0:T(8,128)(2,1)}, bf16[12,256,256]{2,1,0:T(8,128)(2,1)}, u32[]{:S(2)}, u32[]{:S(2)}) collective-permute-start(bf16[12,256,256]{2,1,0:T(8,128)(2,1)} %get-tuple-element.54), channel_id=1, source_target_pairs={{8,16},{16,8},{9,17},{17,9},{10,18},{18,10},{11,19},{19,11},{12,20... | collective-permute-start | bytes 4718600 | tf_op jit(solution)/shard_map/ppermute | solution.py:752
  86.5 40.3 %collective-permute-done.7.refs_0_.left = bf16[12,256,256]{2,1,0:T(8,128)(2,1)S(1)} collective-permute-done((bf16[12,256,256]{2,1,0:T(8,128)(2,1)}, bf16[12,256,256]{2,1,0:T(8,128)(2,1)S(1)}, u32[]{:S(2)}, u32[]{:S(2)}) %collective-permute-start.7) | collective-permute-done | bytes 1572896 | tf_op jit(solution)/shard_map/ppermute | solution.py:730
  126.8 3.4 %collective-permute-done.8.refs_1_.right = bf16[12,256,256]{2,1,0:T(8,128)(2,1)S(1)} collective-permute-done((bf16[12,256,256]{2,1,0:T(8,128)(2,1)}, bf16[12,256,256]{2,1,0:T(8,128)(2,1)S(1)}, u32[]{:S(2)}, u32[]{:S(2)}) %collective-permute-start.8) | collective-permute-done | bytes 1572896 | tf_op jit(solution)/shard_map/ppermute | solution.py:731
  131.4 3.3 %corner_payload.1 = (bf16[10,256,256]{2,1,0:T(8,128)(2,1)}, bf16[10,256,256]{2,1,0:T(8,128)(2,1)}) custom-call(bf16[12,256,256]{2,1,0:T(8,128)(2,1)} %copy-done.2, bf16[12,256,256]{2,1,0:T(8,128)(2,1)} %copy-done.3), custom_call_target="tpu_custom_call" | custom-call | flops 146800640 | tf_op jit(solution)/shard_map/corner_payload/pallas_call | solution.py:182
  134.7 3.7 %collective-permute-start.11 = (bf16[10,256,256]{2,1,0:T(8,128)(2,1)}, bf16[10,256,256]{2,1,0:T(8,128)(2,1)S(1)}, u32[]{:S(2)}, u32[]{:S(2)}) collective-permute-start(bf16[10,256,256]{2,1,0:T(8,128)(2,1)} %get-tuple-element.69), channel_id=1, source_target_pairs={{0,8},{8,16},{16,24},{1,9},{9,17},{17,25},{2,10},{10,18},{18,26},{... | collective-permute-start | bytes 3932168 | tf_op jit(solution)/shard_map/ppermute | solution.py:766
  138.4 1.9 %collective-permute-start.12 = (bf16[10,256,256]{2,1,0:T(8,128)(2,1)}, bf16[10,256,256]{2,1,0:T(8,128)(2,1)S(1)}, u32[]{:S(2)}, u32[]{:S(2)}) collective-permute-start(bf16[10,256,256]{2,1,0:T(8,128)(2,1)} %get-tuple-element.70), channel_id=1, source_target_pairs={{8,0},{16,8},{24,16},{9,1},{17,9},{25,17},{10,2},{18,10},{26,18},{... | collective-permute-start | bytes 3932168 | tf_op jit(solution)/shard_map/ppermute | solution.py:767
  140.4 10.7 %upper_levels.1.down_one = bf16[4,256,256]{2,1,0:T(8,128)(2,1)} custom-call(s32[2,2,27]{2,1,0:T(2,128)} %far_one.1, s32[1,1,27]{2,1,0:T(1,128)} %far_two.1, bf16[3,20,256,256]{3,2,1,0:T(8,128)(2,1)} %couplings.5, bf16[2,2,256,256]{3,2,1,0:T(8,128)(2,1)} %t_two.3, bf16[18,256,256]{2,1,0:T(8,128)(2,1)} %get-tuple-element.53.rest_0_, ...), custom_call_target="tpu_custom_call" | custom-call | flops 1426063360 | bytes 1835008 | tf_op jit(solution)/shard_map/upper_levels/pallas_call | solution.py:456
  151.1 2.1 %collective-permute-done.11.corner_above = bf16[10,256,256]{2,1,0:T(8,128)(2,1)S(1)} collective-permute-done((bf16[10,256,256]{2,1,0:T(8,128)(2,1)}, bf16[10,256,256]{2,1,0:T(8,128)(2,1)S(1)}, u32[]{:S(2)}, u32[]{:S(2)}) %collective-permute-start.11) | collective-permute-done | bytes 1310752 | tf_op jit(solution)/shard_map/ppermute | solution.py:766
  153.3 4.3 %collective-permute-done.12.corner_below = bf16[10,256,256]{2,1,0:T(8,128)(2,1)S(1)} collective-permute-done((bf16[10,256,256]{2,1,0:T(8,128)(2,1)}, bf16[10,256,256]{2,1,0:T(8,128)(2,1)S(1)}, u32[]{:S(2)}, u32[]{:S(2)}) %collective-permute-start.12) | collective-permute-done | bytes 1310752 | tf_op jit(solution)/shard_map/ppermute | solution.py:767
  158.6 19.9 %leaf_outer.1 = bf16[2,2,2,2,256,256]{5,4,3,2,1,0:T(8,128)(2,1)} custom-call(s32[16,37]{1,0:T(8,128)} %get-tuple-element.46.flags, bf16[3,20,256,256]{3,2,1,0:T(8,128)(2,1)} %couplings.5, bf16[2,2,2,2,256,256]{5,4,3,2,1,0:T(8,128)(2,1)} %bitcast.8, bf16[2,2,2,2,256,256]{5,4,3,2,1,0:T(8,128)(2,1)} %bitcast.7, bf16[4,256,256]{2,1,0:T(8,128)(2,1)} %upper_levels.1.down_one, ...), custom_call_target="tpu_custom_call" | custom-call | flops 2097152000 | bytes 4456448 | tf_op jit(solution)/shard_map/leaf_outer/pallas_call | solution.py:664
  (29 shorter events, 7.4 us)
Async XLA Ops:
  5.4 22.5 %collective-permute-start.2 = (bf16[12,256,256]{2,1,0:T(8,128)(2,1)}, bf16[12,256,256]{2,1,0:T(8,128)(2,1)S(1)}, u32[]{:S(2)}, u32[]{:S(2)}) collective-permute-start(bf16[12,256,256]{2,1,0:T(8,128)(2,1)} %get-tuple-element.38.up), channel_id=1, source_target_pairs={{8,0},{16,8},{24,16},{9,1},{17,9},{25,17},{10,2},{18,10},{26,18},{... | collective-permute-start | bytes 4718600 | tf_op jit(solution)/shard_map/ppermute | solution.py:717
  8.0 20.7 %collective-permute-start.1 = (bf16[12,256,256]{2,1,0:T(8,128)(2,1)}, bf16[12,256,256]{2,1,0:T(8,128)(2,1)S(1)}, u32[]{:S(2)}, u32[]{:S(2)}) collective-permute-start(bf16[12,256,256]{2,1,0:T(8,128)(2,1)} %get-tuple-element.39.down), channel_id=1, source_target_pairs={{0,8},{8,16},{16,24},{1,9},{9,17},{17,25},{2,10},{10,18},{18,26},{... | collective-permute-start | bytes 4718600 | tf_op jit(solution)/shard_map/ppermute | solution.py:716
  11.1 16.9 %collective-permute-start = (bf16[5,256,256]{2,1,0:T(8,128)(2,1)}, bf16[5,256,256]{2,1,0:T(8,128)(2,1)S(1)}, u32[]{:S(2)}, u32[]{:S(2)}) collective-permute-start(bf16[5,256,256]{2,1,0:T(8,128)(2,1)} %get-tuple-element.40.refs_0_), channel_id=1, source_target_pairs={{0,1},{1,0},{2,3},{3,2},{4,5},{5,4},{6,7},{7,6},{8,9},{9,8},{10,11... | collective-permute-start | bytes 1966088 | tf_op jit(solution)/shard_map/ppermute | solution.py:718
  27.9 0.8 copy-start.4
  27.9 21.7 %copy-start = (bf16[12,256,256]{2,1,0:T(8,128)(2,1)}, bf16[12,256,256]{2,1,0:T(8,128)(2,1)S(1)}, u32[]{:S(2)}) copy-start(bf16[12,256,256]{2,1,0:T(8,128)(2,1)S(1)} %collective-permute-done.2.below) | copy-start | bytes 4718596
  28.7 20.9 %copy-start.1 = (bf16[12,256,256]{2,1,0:T(8,128)(2,1)}, bf16[12,256,256]{2,1,0:T(8,128)(2,1)S(1)}, u32[]{:S(2)}) copy-start(bf16[12,256,256]{2,1,0:T(8,128)(2,1)S(1)} %collective-permute-done.1.above) | copy-start | bytes 4718596
  31.4 20.9 %collective-permute-start.4 = (bf16[6,256,256]{2,1,0:T(8,128)(2,1)}, bf16[6,256,256]{2,1,0:T(8,128)(2,1)S(1)}, u32[]{:S(2)}, u32[]{:S(2)}) collective-permute-start(bf16[6,256,256]{2,1,0:T(8,128)(2,1)} %get-tuple-element.49), channel_id=1, source_target_pairs={{0,2},{2,4},{4,6},{3,1},{5,3},{7,5},{8,10},{10,12},{12,14},{11,9},... | collective-permute-start | bytes 2359304 | tf_op jit(solution)/shard_map/ppermute | solution.py:732
  34.6 15.0 %collective-permute-start.3 = (bf16[2,256,256]{2,1,0:T(8,128)(2,1)}, bf16[2,256,256]{2,1,0:T(8,128)(2,1)}, u32[]{:S(2)}, u32[]{:S(2)}) collective-permute-start(bf16[2,256,256]{2,1,0:T(8,128)(2,1)} %get-tuple-element.48), channel_id=1, source_target_pairs={{2,0},{4,2},{6,4},{1,3},{3,5},{5,7},{10,8},{12,10},{14,12},{9,11},... | collective-permute-start | bytes 786440 | tf_op jit(solution)/shard_map/ppermute | solution.py:733
  52.3 1.0 copy-start.7
  57.1 25.3 %collective-permute-start.9 = (bf16[6,256,256]{2,1,0:T(8,128)(2,1)}, bf16[6,256,256]{2,1,0:T(8,128)(2,1)S(1)}, u32[]{:S(2)}, u32[]{:S(2)}) collective-permute-start(bf16[6,256,256]{2,1,0:T(8,128)(2,1)} %get-tuple-element.57), channel_id=1, source_target_pairs={{0,16},{8,24},{16,0},{24,8},{1,17},{9,25},{17,1},{25,9},{2,18},{10... | collective-permute-start | bytes 2359304 | tf_op jit(solution)/shard_map/ppermute | solution.py:746
  57.2 69.6 %collective-permute-start.7 = (bf16[12,256,256]{2,1,0:T(8,128)(2,1)}, bf16[12,256,256]{2,1,0:T(8,128)(2,1)S(1)}, u32[]{:S(2)}, u32[]{:S(2)}) collective-permute-start(bf16[12,256,256]{2,1,0:T(8,128)(2,1)} %get-tuple-element.55), channel_id=1, source_target_pairs={{0,1},{1,2},{2,3},{3,4},{4,5},{5,6},{6,7},{8,9},{9,10},{10,11},{11... | collective-permute-start | bytes 4718600 | tf_op jit(solution)/shard_map/ppermute | solution.py:730
  60.3 69.9 %collective-permute-start.8 = (bf16[12,256,256]{2,1,0:T(8,128)(2,1)}, bf16[12,256,256]{2,1,0:T(8,128)(2,1)S(1)}, u32[]{:S(2)}, u32[]{:S(2)}) collective-permute-start(bf16[12,256,256]{2,1,0:T(8,128)(2,1)} %get-tuple-element.56), channel_id=1, source_target_pairs={{1,0},{2,1},{3,2},{4,3},{5,4},{6,5},{7,6},{9,8},{10,9},{11,10},{12... | collective-permute-start | bytes 4718600 | tf_op jit(solution)/shard_map/ppermute | solution.py:731
  63.6 76.8 %collective-permute-start.5 = (bf16[18,256,256]{2,1,0:T(8,128)(2,1)}, bf16[18,256,256]{2,1,0:T(8,128)(2,1)}, u32[]{:S(2)}, u32[]{:S(2)}) collective-permute-start(bf16[18,256,256]{2,1,0:T(8,128)(2,1)} %get-tuple-element.53.rest_0_), channel_id=1, source_target_pairs={{0,8},{8,0},{16,24},{24,16},{1,9},{9,1},{17,25},{25,17},{2,10},{10... | collective-permute-start | bytes 7077896 | tf_op jit(solution)/shard_map/ppermute | solution.py:753
  82.4 57.9 %copy-start.8 = (bf16[6,256,256]{2,1,0:T(8,128)(2,1)}, bf16[6,256,256]{2,1,0:T(8,128)(2,1)S(1)}, u32[]{:S(2)}) copy-start(bf16[6,256,256]{2,1,0:T(8,128)(2,1)S(1)} %collective-permute-done.9.rest_3_) | copy-start | bytes 2359300
  82.5 47.8 %collective-permute-start.10 = (bf16[6,256,256]{2,1,0:T(8,128)(2,1)S(1)}, bf16[6,256,256]{2,1,0:T(8,128)(2,1)}, u32[]{:S(2)}, u32[]{:S(2)}) collective-permute-start(bf16[6,256,256]{2,1,0:T(8,128)(2,1)S(1)} %collective-permute-done.9.rest_3_), channel_id=1, source_target_pairs={{0,8},{8,0},{16,24},{24,16},{1,9},{9,1},{17,25},{25,17},{2,10},{10... | collective-permute-start | bytes 2359304 | tf_op jit(solution)/shard_map/ppermute | solution.py:756
  82.6 57.7 %collective-permute-start.6 = (bf16[12,256,256]{2,1,0:T(8,128)(2,1)}, bf16[12,256,256]{2,1,0:T(8,128)(2,1)}, u32[]{:S(2)}, u32[]{:S(2)}) collective-permute-start(bf16[12,256,256]{2,1,0:T(8,128)(2,1)} %get-tuple-element.54), channel_id=1, source_target_pairs={{8,16},{16,8},{9,17},{17,9},{10,18},{18,10},{11,19},{19,11},{12,20... | collective-permute-start | bytes 4718600 | tf_op jit(solution)/shard_map/ppermute | solution.py:752
  126.8 3.4 %copy-start.2 = (bf16[12,256,256]{2,1,0:T(8,128)(2,1)}, bf16[12,256,256]{2,1,0:T(8,128)(2,1)S(1)}, u32[]{:S(2)}) copy-start(bf16[12,256,256]{2,1,0:T(8,128)(2,1)S(1)} %collective-permute-done.7.refs_0_.left) | copy-start | bytes 4718596
  130.2 1.2 copy-start.3
  134.7 18.6 %collective-permute-start.11 = (bf16[10,256,256]{2,1,0:T(8,128)(2,1)}, bf16[10,256,256]{2,1,0:T(8,128)(2,1)S(1)}, u32[]{:S(2)}, u32[]{:S(2)}) collective-permute-start(bf16[10,256,256]{2,1,0:T(8,128)(2,1)} %get-tuple-element.69), channel_id=1, source_target_pairs={{0,8},{8,16},{16,24},{1,9},{9,17},{17,25},{2,10},{10,18},{18,26},{... | collective-permute-start | bytes 3932168 | tf_op jit(solution)/shard_map/ppermute | solution.py:766
  138.4 19.1 %collective-permute-start.12 = (bf16[10,256,256]{2,1,0:T(8,128)(2,1)}, bf16[10,256,256]{2,1,0:T(8,128)(2,1)S(1)}, u32[]{:S(2)}, u32[]{:S(2)}) collective-permute-start(bf16[10,256,256]{2,1,0:T(8,128)(2,1)} %get-tuple-element.70), channel_id=1, source_target_pairs={{8,0},{16,8},{24,16},{9,1},{17,9},{25,17},{10,2},{18,10},{26,18},{... | collective-permute-start | bytes 3932168 | tf_op jit(solution)/shard_map/ppermute | solution.py:767
  153.3 4.3 %copy-start.5 = (bf16[10,256,256]{2,1,0:T(8,128)(2,1)}, bf16[10,256,256]{2,1,0:T(8,128)(2,1)S(1)}, u32[]{:S(2)}) copy-start(bf16[10,256,256]{2,1,0:T(8,128)(2,1)S(1)} %collective-permute-done.11.corner_above) | copy-start | bytes 3932164
  157.5 1.1 copy-start.6
